TPU v7x, 32 devices: a whole 2x2x4 slice. The times are simulated.
32 devices in a mesh: dp: 8 (over z, x), tr: 2 (over y), tc: 2 (over core).
Axes of the slice: x: 2, y: 2, z: 4, core: 2. Of those that a mesh axis runs over, the one named last changes fastest.
Arguments:
- tokens_in: bfloat16 [16928, 768], P(('dp', 'tr', 'tc')), may hold values from -6 to 6
- valid_len: int32 [32], P(('dp', 'tr', 'tc')), may hold values from 40 to 529, as said below
- mask_pos: int32 [32, 132], P(('dp', 'tr', 'tc')), may hold values from 0 to 528, as said below
- encoder_gains: bfloat16 [768, 2], P(('dp', 'tr', 'tc')), may hold values from 0.5 to 1.5
- encoder_biases: bfloat16 [768, 5], P(('dp', 'tr', 'tc')), may hold values from -1 to 1
- encoder_inproj: bfloat16 [768, 2304], P(('dp', 'tr', 'tc')), may hold values from -0.21875 to 0.21875
- encoder_outproj: bfloat16 [768, 768], P(('dp', 'tr', 'tc')), may hold values from -0.625 to 0.625
- encoder_up: bfloat16 [768, 3072], P('tc', 'tr'), may hold values from -0.21875 to 0.21875
- encoder_upbias: bfloat16 [3072], P('tr'), may hold values from -1 to 1
- encoder_down: bfloat16 [3072, 768], P('tr', 'tc'), may hold values from -0.109375 to 0.109375
- encoder_downbias: bfloat16 [768], P('tc'), may hold values from -1 to 1
- embed_weight: bfloat16 [768, 512], P(('dp', 'tr', 'tc')), may hold values from -0.21875 to 0.21875
- mask_token: bfloat16 [512], P(('dp', 'tr', 'tc')), may hold values from -4 to 4
- decoder_gains: bfloat16 [512, 2], P(('dp', 'tr', 'tc')), may hold values from 0.5 to 1.5
- decoder_biases: bfloat16 [512, 6], P(('dp', 'tr', 'tc')), may hold values from -1 to 1
- decoder_inproj: bfloat16 [512, 1536], P(('dp', 'tr', 'tc')), may hold values from -0.25 to 0.25
- decoder_outproj: bfloat16 [512, 512], P(('dp', 'tr', 'tc')), may hold values from -0.75 to 0.75
- decoder_up: bfloat16 [512, 2048], P('tc', 'tr'), may hold values from -0.25 to 0.25
- decoder_upbias: bfloat16 [2048], P('tr'), may hold values from -1 to 1
- decoder_down: bfloat16 [2048, 512], P('tr', 'tc'), may hold values from -0.125 to 0.125
- decoder_downbias: bfloat16 [512], P('tc'), may hold values from -1 to 1
- cotangent: bfloat16 [16928, 512], P(('dp', 'tr', 'tc')), may hold values from -6 to 6
Outputs:
- decoder_output: float32 [16928, 512], P(('dp', 'tr', 'tc'))
- input_grad: float32 [16928, 768], P(('dp', 'tr', 'tc'))
- encoder_gains_grad: float32 [768, 2], P(('dp', 'tr', 'tc'))
- encoder_biases_grad: float32 [768, 5], P(('dp', 'tr', 'tc'))
- encoder_inproj_grad: float32 [768, 2304], P(('dp', 'tr', 'tc'))
- encoder_outproj_grad: float32 [768, 768], P(('dp', 'tr', 'tc'))
- encoder_up_grad: float32 [768, 3072], P('tc', 'tr')
- encoder_upbias_grad: float32 [3072], P('tr')
- encoder_down_grad: float32 [3072, 768], P('tr', 'tc')
- encoder_downbias_grad: float32 [768], P('tc')
- embed_grad: float32 [768, 512], P(('dp', 'tr', 'tc'))
- mask_token_grad: float32 [512], P(('dp', 'tr', 'tc'))
- decoder_gains_grad: float32 [512, 2], P(('dp', 'tr', 'tc'))
- decoder_biases_grad: float32 [512, 6], P(('dp', 'tr', 'tc'))
- decoder_inproj_grad: float32 [512, 1536], P(('dp', 'tr', 'tc'))
- decoder_outproj_grad: float32 [512, 512], P(('dp', 'tr', 'tc'))
- decoder_up_grad: float32 [512, 2048], P('tc', 'tr')
- decoder_upbias_grad: float32 [2048], P('tr')
- decoder_down_grad: float32 [2048, 512], P('tr', 'tc')
- decoder_downbias_grad: float32 [512], P('tc')
Inputs may be any that keep to these rules, and one draw needn't show every extreme that they name: `valid_len`: some sentence has exactly 529 valid patches and some exactly 40. `mask_pos`: the 132 positions of a sentence are distinct; exactly valid_len // 4 of them lie below the sentence's valid_len, the others at or beyond it.
All inputs are finite; a program needn't handle non-finite values.
Results may differ from a plain program's by a relative error of at most 0.02.
Values may be sent and summed in bfloat16 or wider, within the bound.
No kernel may reach another device: no remote copies, remote signals or barrier semaphores. Data moves between devices by JAX's collectives and lax.ppermute only.
A program may use at most 320 MiB of HBM per device.

v0:
```python
from functools import partial

import jax
import jax.numpy as jnp
from jax import lax
from jax.sharding import PartitionSpec as P

HEADS = 12
HEADS2 = 16


epsilon = 1e-06
masked_score = -1e30


def normalize(values, gain, shift):
    center = values - jnp.mean(values, axis=-1, keepdims=True)
    spread = jnp.mean(center * center, axis=-1, keepdims=True)
    return center * lax.rsqrt(spread + epsilon) * gain + shift


def gelu_exact(values):
    return jax.nn.gelu(values, approximate=False)


def product(operand, matrix, flipped):
    contract = 1 if flipped else 0
    return lax.dot_general(
        operand, matrix, (((1,), (contract,)), ((), ())), preferred_element_type=jnp.float32
    )


def product_rows(operand, matrix, flipped):
    return product(operand, matrix, flipped)


def outer_sum(operand, matrix):
    return lax.dot_general(
        operand, matrix, (((0,), (0,)), ((), ())), preferred_element_type=jnp.float32
    )


def split_heads(packed, head_count):
    model_width = packed.shape[-1] // 3
    head_size = model_width // head_count
    query_rows = packed[:, :model_width].reshape(-1, head_count, head_size)
    key_rows = packed[:, model_width : 2 * model_width].reshape(-1, head_count, head_size)
    value_rows = packed[:, 2 * model_width :].reshape(-1, head_count, head_size)
    return (query_rows, key_rows, value_rows, head_size ** (-0.5))


def item_scores(query_rows, key_rows, score_scale, key_mask):
    scores = (
        jnp.einsum("qhd,khd->hqk", query_rows, key_rows, preferred_element_type=jnp.float32)
        * score_scale
    )
    return jnp.where(key_mask[None, None, :], scores, masked_score)


def attend_item(head_count, inputs):
    packed, key_mask = inputs
    query_rows, key_rows, value_rows, score_scale = split_heads(packed, head_count)
    scores = item_scores(query_rows, key_rows, score_scale, key_mask)
    row_peak = jnp.max(scores, axis=2, keepdims=True)
    exponent = jnp.exp(scores - row_peak)
    row_total = jnp.sum(exponent, axis=2, keepdims=True)
    weights = (exponent / row_total).astype(jnp.bfloat16)
    attended = jnp.einsum("hqk,khd->qhd", weights, value_rows, preferred_element_type=jnp.float32)
    logsum = (row_peak + jnp.log(row_total))[:, :, 0]
    return (attended.reshape(packed.shape[0], -1).astype(jnp.bfloat16), logsum)


def attend_back(head_count, inputs):
    packed, key_mask, logsum, grad_attended = inputs
    query_rows, key_rows, value_rows, score_scale = split_heads(packed, head_count)
    scores = item_scores(query_rows, key_rows, score_scale, key_mask)
    probs = jnp.exp(scores - logsum[:, :, None])
    grad_rows = grad_attended.reshape(query_rows.shape)
    grad_values = jnp.einsum(
        "hqk,qhd->khd", probs.astype(jnp.bfloat16), grad_rows, preferred_element_type=jnp.float32
    )
    grad_probs = jnp.einsum(
        "qhd,khd->hqk", grad_rows, value_rows, preferred_element_type=jnp.float32
    )
    row_delta = jnp.sum(grad_probs * probs, axis=2, keepdims=True)
    grad_scores = (probs * (grad_probs - row_delta)).astype(jnp.bfloat16)
    grad_queries = (
        jnp.einsum("hqk,khd->qhd", grad_scores, key_rows, preferred_element_type=jnp.float32)
        * score_scale
    )
    grad_keys = (
        jnp.einsum("hqk,qhd->khd", grad_scores, query_rows, preferred_element_type=jnp.float32)
        * score_scale
    )
    item_rows = packed.shape[0]
    return jnp.concatenate(
        [
            grad_queries.reshape(item_rows, -1),
            grad_keys.reshape(item_rows, -1),
            grad_values.reshape(item_rows, -1),
        ],
        axis=1,
    )


def spread_rows(values):
    part_width = values.shape[1] // lax.axis_size("tc")
    whole_rows = lax.all_gather(values, ("tr", "tc"), axis=0, tiled=True)
    return lax.dynamic_slice_in_dim(whole_rows, lax.axis_index("tc") * part_width, part_width, 1)


def sum_hidden(operand, matrix, flipped):
    return lax.psum_scatter(
        product_rows(operand, matrix, flipped).astype(jnp.bfloat16),
        "tc",
        scatter_dimension=0,
        tiled=True,
    ).astype(jnp.float32)


def share_hidden(values):
    return lax.all_gather(values, "tc", axis=0, tiled=True)


def sum_output(operand, matrix, flipped):
    return lax.psum_scatter(
        product_rows(operand, matrix, flipped).astype(jnp.bfloat16),
        "tr",
        scatter_dimension=0,
        tiled=True,
    ).astype(jnp.float32)


def return_rows(values):
    return lax.all_to_all(values, "tc", split_axis=0, concat_axis=1, tiled=True)


def grid_forward(normed_two, feed_params):
    up_weight, up_bias, down_weight, down_bias = feed_params
    gathered = spread_rows(normed_two)
    hidden = sum_hidden(gathered, up_weight, False) + up_bias.astype(jnp.float32)
    active = share_hidden(gelu_exact(hidden).astype(jnp.bfloat16))
    result = sum_output(active, down_weight, False) + down_bias.astype(jnp.float32)
    return (return_rows(result.astype(jnp.bfloat16)), (gathered, hidden, active))


def grid_backward(grad_result, feed_params, saved_state):
    up_weight, up_bias, down_weight, down_bias = feed_params
    gathered, hidden, active = saved_state
    grad_rows = spread_rows(grad_result)
    grad_active = sum_hidden(grad_rows, down_weight, True).astype(jnp.bfloat16)
    unused, pullback = jax.vjp(gelu_exact, hidden)
    grad_hidden = pullback(grad_active.astype(jnp.float32))[0].astype(jnp.bfloat16)
    grad_hidden = share_hidden(grad_hidden)
    grad_input = return_rows(sum_output(grad_hidden, up_weight, True).astype(jnp.bfloat16))
    gradients = (
        outer_sum(gathered, grad_hidden),
        jnp.sum(grad_hidden, axis=0, dtype=jnp.float32),
        outer_sum(active, grad_rows),
        jnp.sum(grad_rows, axis=0, dtype=jnp.float32),
    )
    return (grad_input, gradients)


def block_forward(stream, attention_params, feed_ready, key_mask, head_count, forward_feed):
    gains, biases, inproj, outproj = attention_params
    gain_table = gains.astype(jnp.float32)
    bias_table = biases.astype(jnp.float32)
    model_width = stream.shape[1]
    item_span = key_mask.shape[1]
    normed = normalize(stream, gain_table[:, 0], bias_table[:, 0]).astype(jnp.bfloat16)
    bias_row = jnp.concatenate(
        [bias_table[:, 1], jnp.zeros_like(bias_table[:, 1]), bias_table[:, 2]]
    )
    packed = (product(normed, inproj, False) + bias_row).astype(jnp.bfloat16)
    attended, logsum = lax.map(
        partial(attend_item, head_count), (packed.reshape(-1, item_span, 3 * model_width), key_mask)
    )
    attended = attended.reshape(-1, model_width)
    middle = stream + product(attended, outproj, False) + bias_table[:, 3]
    normed_two = normalize(middle, gain_table[:, 1], bias_table[:, 4]).astype(jnp.bfloat16)
    result, feed_saved = forward_feed(normed_two, feed_ready)
    return (
        middle + result.astype(jnp.float32),
        (normed, packed, logsum, attended, middle, feed_saved),
    )


def block_backward(
    grad_out, stream, attention_params, feed_ready, key_mask, head_count, saved_state, backward_feed
):
    gains, biases, inproj, outproj = attention_params
    normed, packed, logsum, attended, middle, feed_saved = saved_state
    gain_table = gains.astype(jnp.float32)
    bias_table = biases.astype(jnp.float32)
    model_width = stream.shape[1]
    item_span = key_mask.shape[1]
    grad_normed_two, feed_grads = backward_feed(
        grad_out.astype(jnp.bfloat16), feed_ready, feed_saved
    )
    unused, pull_second = jax.vjp(normalize, middle, gain_table[:, 1], bias_table[:, 4])
    grad_from_norm, grad_gain_second, grad_shift_second = pull_second(
        grad_normed_two.astype(jnp.float32)
    )
    grad_middle = grad_out + grad_from_norm
    grad_branch = grad_middle.astype(jnp.bfloat16)
    grad_outproj = outer_sum(attended, grad_branch)
    grad_outbias = jnp.sum(grad_branch, axis=0, dtype=jnp.float32)
    grad_attended = product(grad_branch, outproj, True).astype(jnp.bfloat16)
    grad_packed = lax.map(
        partial(attend_back, head_count),
        (
            packed.reshape(-1, item_span, 3 * model_width),
            key_mask,
            logsum,
            grad_attended.reshape(-1, item_span, model_width),
        ),
    )
    grad_packed = grad_packed.reshape(-1, 3 * model_width).astype(jnp.bfloat16)
    grad_inproj = outer_sum(normed, grad_packed)
    grad_querybias = jnp.sum(grad_packed[:, :model_width], axis=0, dtype=jnp.float32)
    grad_valuebias = jnp.sum(grad_packed[:, 2 * model_width :], axis=0, dtype=jnp.float32)
    grad_normed = product(grad_packed, inproj, True)
    unused_first, pull_first = jax.vjp(normalize, stream, gain_table[:, 0], bias_table[:, 0])
    grad_from_first, grad_gain_first, grad_shift_first = pull_first(grad_normed)
    grad_stream = grad_middle + grad_from_first
    grad_gains = jnp.stack([grad_gain_first, grad_gain_second], axis=1)
    grad_biases = jnp.stack(
        [grad_shift_first, grad_querybias, grad_valuebias, grad_outbias, grad_shift_second], axis=1
    )
    return (grad_stream, (grad_gains, grad_biases, grad_inproj, grad_outproj), feed_grads)


def local(
    tokens_in,
    valid_len,
    mask_pos,
    encoder_gains,
    encoder_biases,
    encoder_inproj,
    encoder_outproj,
    encoder_up,
    encoder_upbias,
    encoder_down,
    encoder_downbias,
    embed_weight,
    mask_token,
    decoder_gains,
    decoder_biases,
    decoder_inproj,
    decoder_outproj,
    decoder_up,
    decoder_upbias,
    decoder_down,
    decoder_downbias,
    cotangent,
):
    item_count = valid_len.shape[0]
    item_span = tokens_in.shape[0] // item_count
    places = lax.broadcasted_iota(jnp.int32, (item_count, item_span), 1)
    inside = places < valid_len[:, None]
    covered = jnp.any(mask_pos[:, None, :] == places[:, :, None], axis=2)
    encoder_keys = jnp.logical_and(inside, jnp.logical_not(covered))
    mask_rows = covered.reshape(-1, 1)
    gathered = (
        lax.all_gather(encoder_gains, ("dp", "tr", "tc"), axis=0, tiled=True),
        lax.all_gather(encoder_biases, ("dp", "tr", "tc"), axis=0, tiled=True),
        lax.all_gather(encoder_inproj, ("dp", "tr", "tc"), axis=0, tiled=True),
        lax.all_gather(encoder_outproj, ("dp", "tr", "tc"), axis=0, tiled=True),
        lax.all_gather(decoder_gains, ("dp", "tr", "tc"), axis=0, tiled=True),
        lax.all_gather(decoder_biases, ("dp", "tr", "tc"), axis=0, tiled=True),
        lax.all_gather(decoder_inproj, ("dp", "tr", "tc"), axis=0, tiled=True),
        lax.all_gather(decoder_outproj, ("dp", "tr", "tc"), axis=0, tiled=True),
        lax.all_gather(embed_weight, ("dp", "tr", "tc"), axis=0, tiled=True),
        lax.all_gather(mask_token, ("dp", "tr", "tc"), axis=0, tiled=True),
    )
    encoder_attention = (gathered[0], gathered[1], gathered[2], gathered[3])
    decoder_attention = (gathered[4], gathered[5], gathered[6], gathered[7])
    full_embed = gathered[8]
    full_mask = gathered[9].astype(jnp.float32)
    encoder_feed = (encoder_up, encoder_upbias, encoder_down, encoder_downbias)
    decoder_feed = (decoder_up, decoder_upbias, decoder_down, decoder_downbias)
    stream = tokens_in.astype(jnp.float32)
    encoded, unused_saved = block_forward(
        stream, encoder_attention, encoder_feed, encoder_keys, HEADS, grid_forward
    )
    encoded_low = encoded.astype(jnp.bfloat16)
    decoder_bias_table = gathered[5].astype(jnp.float32)
    embedded = product(encoded_low, full_embed, False) + decoder_bias_table[:, 5]
    decoded = jnp.where(mask_rows, full_mask[None, :], embedded)
    output, decoder_saved = block_forward(
        decoded, decoder_attention, decoder_feed, inside, HEADS2, grid_forward
    )
    grad_decoded, decoder_attn_grads, decoder_feed_grads = block_backward(
        cotangent.astype(jnp.float32),
        decoded,
        decoder_attention,
        decoder_feed,
        inside,
        HEADS2,
        decoder_saved,
        grid_backward,
    )
    grad_mask = jnp.sum(jnp.where(mask_rows, grad_decoded, 0.0), axis=0)
    grad_embedded = jnp.where(mask_rows, 0.0, grad_decoded).astype(jnp.bfloat16)
    grad_embed = outer_sum(encoded_low, grad_embedded)
    grad_embias = jnp.sum(grad_embedded, axis=0, dtype=jnp.float32)
    grad_encoded = product(grad_embedded, full_embed, True)
    regathered = (
        lax.all_gather(encoder_gains, ("dp", "tr", "tc"), axis=0, tiled=True),
        lax.all_gather(encoder_biases, ("dp", "tr", "tc"), axis=0, tiled=True),
        lax.all_gather(encoder_inproj, ("dp", "tr", "tc"), axis=0, tiled=True),
        lax.all_gather(encoder_outproj, ("dp", "tr", "tc"), axis=0, tiled=True),
    )
    again_attention = (regathered[0], regathered[1], regathered[2], regathered[3])
    recomputed, encoder_saved = block_forward(
        stream, again_attention, encoder_feed, encoder_keys, HEADS, grid_forward
    )
    grad_stream, encoder_attn_grads, encoder_feed_grads = block_backward(
        grad_encoded,
        stream,
        again_attention,
        encoder_feed,
        encoder_keys,
        HEADS,
        encoder_saved,
        grid_backward,
    )
    decoder_bias_grads = jnp.concatenate([decoder_attn_grads[1], grad_embias[:, None]], axis=1)
    attention_sums = (
        lax.psum_scatter(
            encoder_attn_grads[0], ("dp", "tr", "tc"), scatter_dimension=0, tiled=True
        ),
        lax.psum_scatter(
            encoder_attn_grads[1], ("dp", "tr", "tc"), scatter_dimension=0, tiled=True
        ),
        lax.psum_scatter(
            encoder_attn_grads[2], ("dp", "tr", "tc"), scatter_dimension=0, tiled=True
        ),
        lax.psum_scatter(
            encoder_attn_grads[3], ("dp", "tr", "tc"), scatter_dimension=0, tiled=True
        ),
        lax.psum_scatter(
            decoder_attn_grads[0], ("dp", "tr", "tc"), scatter_dimension=0, tiled=True
        ),
        lax.psum_scatter(decoder_bias_grads, ("dp", "tr", "tc"), scatter_dimension=0, tiled=True),
        lax.psum_scatter(
            decoder_attn_grads[2], ("dp", "tr", "tc"), scatter_dimension=0, tiled=True
        ),
        lax.psum_scatter(
            decoder_attn_grads[3], ("dp", "tr", "tc"), scatter_dimension=0, tiled=True
        ),
        lax.psum_scatter(grad_embed, ("dp", "tr", "tc"), scatter_dimension=0, tiled=True),
        lax.psum_scatter(grad_mask, ("dp", "tr", "tc"), scatter_dimension=0, tiled=True),
    )
    feed_sums = lax.psum(
        (
            encoder_feed_grads[0],
            encoder_feed_grads[1],
            encoder_feed_grads[2],
            encoder_feed_grads[3],
            decoder_feed_grads[0],
            decoder_feed_grads[1],
            decoder_feed_grads[2],
            decoder_feed_grads[3],
        ),
        "dp",
    )
    return (
        output,
        grad_stream,
        attention_sums[0],
        attention_sums[1],
        attention_sums[2],
        attention_sums[3],
        feed_sums[0],
        feed_sums[1],
        feed_sums[2],
        feed_sums[3],
        attention_sums[8],
        attention_sums[9],
        attention_sums[4],
        attention_sums[5],
        attention_sums[6],
        attention_sums[7],
        feed_sums[4],
        feed_sums[5],
        feed_sums[6],
        feed_sums[7],
    )


def solution(mesh):
    in_specs = (
        P(("dp", "tr", "tc"), None),
        P(("dp", "tr", "tc")),
        P(("dp", "tr", "tc"), None),
        P(("dp", "tr", "tc"), None),
        P(("dp", "tr", "tc"), None),
        P(("dp", "tr", "tc"), None),
        P(("dp", "tr", "tc"), None),
        P("tc", "tr"),
        P("tr"),
        P("tr", "tc"),
        P("tc"),
        P(("dp", "tr", "tc"), None),
        P(("dp", "tr", "tc")),
        P(("dp", "tr", "tc"), None),
        P(("dp", "tr", "tc"), None),
        P(("dp", "tr", "tc"), None),
        P(("dp", "tr", "tc"), None),
        P("tc", "tr"),
        P("tr"),
        P("tr", "tc"),
        P("tc"),
        P(("dp", "tr", "tc"), None),
    )
    out_specs = (
        P(("dp", "tr", "tc"), None),
        P(("dp", "tr", "tc"), None),
        P(("dp", "tr", "tc"), None),
        P(("dp", "tr", "tc"), None),
        P(("dp", "tr", "tc"), None),
        P(("dp", "tr", "tc"), None),
        P("tc", "tr"),
        P("tr"),
        P("tr", "tc"),
        P("tc"),
        P(("dp", "tr", "tc"), None),
        P(("dp", "tr", "tc")),
        P(("dp", "tr", "tc"), None),
        P(("dp", "tr", "tc"), None),
        P(("dp", "tr", "tc"), None),
        P(("dp", "tr", "tc"), None),
        P("tc", "tr"),
        P("tr"),
        P("tr", "tc"),
        P("tc"),
    )
    return jax.shard_map(local, mesh=mesh, in_specs=in_specs, out_specs=out_specs, check_vma=False)
```

profile of v0, /device:TPU:0, one launch (start us, length us, event | category | flops | bytes accessed | tf_op | source)
XLA Modules:
  0.0 1913.4 jit_solution(110767395482838884)
XLA Ops:
  13.1 43.3 %all-gather = bf16[32,24,2]{1,2,0:T(2,128)(2,1)S(1)} all-gather(bf16[1,24,2]{1,2,0:T(2,128)(2,1)} %bitcast.264), channel_id=1, replica_groups=mesh['dp'=8,'tr'=2,'tc'=2] {'dp','tr','tc'}, dimensions={0}, use_global_device_ids=true | all-gather | bytes 3168 | tf_op jit(solution)/shard_map/all_gather | solution.py:266
  56.8 37.1 %all-gather.1 = bf16[32,24,5]{1,2,0:T(8,128)(2,1)S(1)} all-gather(bf16[1,24,5]{1,2,0:T(8,128)(2,1)} %bitcast.257), channel_id=1, replica_groups=mesh['dp'=8,'tr'=2,'tc'=2] {'dp','tr','tc'}, dimensions={0}, use_global_device_ids=true | all-gather | bytes 7920 | tf_op jit(solution)/shard_map/all_gather | solution.py:267
  135.0 28.1 %all-gather.30.cloned.1.call-done = bf16[4,529,768]{2,1,0:T(8,128)(2,1)} async-done(((bf16[1,529,768]{2,1,0:T(8,128)(2,1)}), bf16[4,529,768]{2,1,0:T(8,128)(2,1)}) %all-gather.30.cloned.1.call-update) | async-done | bytes 3250192 | tf_op jit(solution)/shard_map/all_gather | solution.py:108
  175.5 12.3 fusion
  192.0 16.7 concatenate.25
  208.7 17.0 fusion.58
  227.0 40.3 %all-gather.5 = bf16[32,16,2]{1,2,0:T(2,128)(2,1)S(1)} all-gather(bf16[1,16,2]{1,2,0:T(2,128)(2,1)S(1)} %bitcast.265), channel_id=1, replica_groups=mesh['dp'=8,'tr'=2,'tc'=2] {'dp','tr','tc'}, dimensions={0}, use_global_device_ids=true | all-gather | bytes 2112 | tf_op jit(solution)/shard_map/all_gather | solution.py:270
  267.6 36.8 %all-gather.4 = bf16[32,16,6]{1,2,0:T(8,128)(2,1)S(1)} all-gather(bf16[1,16,6]{1,2,0:T(8,128)(2,1)S(1)} %bitcast.258), channel_id=1, replica_groups=mesh['dp'=8,'tr'=2,'tc'=2] {'dp','tr','tc'}, dimensions={0}, use_global_device_ids=true | all-gather | bytes 6336 | tf_op jit(solution)/shard_map/all_gather | solution.py:271
  304.7 42.5 %all_gather.71 = bf16[512,512]{1,0:T(8,128)(2,1)} all-gather(bf16[16,512]{1,0:T(8,128)(2,1)S(1)} %copy-done.81), channel_id=1, replica_groups=mesh['dp'=8,'tr'=2,'tc'=2] {'dp','tr','tc'}, dimensions={0}, use_global_device_ids=true | all-gather | bytes 540672 | tf_op jit(solution)/shard_map/all_gather | solution.py:273
  347.3 41.4 %all_gather.67 = bf16[768,512]{1,0:T(8,128)(2,1)} all-gather(bf16[24,512]{1,0:T(8,128)(2,1)S(1)} %copy-done.80), channel_id=1, replica_groups=mesh['dp'=8,'tr'=2,'tc'=2] {'dp','tr','tc'}, dimensions={0}, use_global_device_ids=true | all-gather | bytes 811008 | tf_op jit(solution)/shard_map/all_gather | solution.py:274
  403.2 25.6 %fusion.1 = bf16[1072,384]{1,0:T(8,128)(2,1)} fusion(bf16[2116,384]{1,0:T(8,128)(2,1)} %convolution_convert_fusion.5), kind=kCustom, calls=%all-reduce-scatter.1 | all-reduce-scatter fusion | flops 823297 | bytes 2448896
  433.3 36.9 %all-reduce = bf16[512]{0:T(512)(128)(2,1)S(1)} all-reduce(bf16[512]{0:T(512)(128)(2,1)S(1)} %dynamic-update-slice), channel_id=1, replica_groups=mesh['dp'=8,'tr'=2,'tc'=2] {'dp','tr','tc'}, use_global_device_ids=true, to_apply=%add | all-reduce | flops 512 | bytes 2048
  532.6 15.5 all-gather.34.cloned.1.call-done
  556.2 14.6 fusion.128
  599.0 13.7 fusion.66
  613.4 13.4 all-gather.40.cloned.1.call-done
  636.6 18.7 fusion.5
  683.9 13.9 multiply_reduce_fusion
  697.7 15.1 multiply_convert_fusion
  730.2 26.1 %all-gather.42.cloned.1.call-done = bf16[4,529,768]{2,1,0:T(8,128)(2,1)} async-done(((bf16[1,529,768]{2,1,0:T(8,128)(2,1)}), bf16[4,529,768]{2,1,0:T(8,128)(2,1)}) %all-gather.42.cloned.1.call-update) | async-done | bytes 3250192 | tf_op jit(solution)/shard_map/all_gather | solution.py:108
  783.7 16.9 concatenate.31
  850.4 37.0 %fusion.129 = (bf16[1064,256]{1,0:T(8,128)(2,1)S(1)}, bf16[1072,384]{1,0:T(8,128)(2,1)}) fusion(bf16[2116,256]{1,0:T(8,128)(2,1)} %convolution_convert_fusion.7, bf16[2116,384]{1,0:T(8,128)(2,1)} %convolution_convert_fusion.4), kind=kCustom, calls=%all-reduce-scatter.9 | all-reduce-scatter fusion | flops 1368066 | bytes 4077056
  946.9 15.1 multiply_reduce_fusion.1
  1001.1 94.1 %reduce-scatter.42.cloned.1.call-done = f32[16,6]{1,0:T(8,128)} async-done(((f32[512,6]{1,0:T(8,128)}), f32[16,6]{1,0:T(8,128)}) %reduce-scatter.42.cloned.1.call-update) | async-done | bytes 400
  1103.4 34.3 %all-reduce.21 = (f32[1536]{0:T(1024)}, f32[384]{0:T(512)}, f32[1024]{0:T(1024)}, f32[256]{0:T(256)}) all-reduce(f32[1536]{0:T(1024)S(1)} %convert_reduce_fusion, f32[384]{0:T(512)S(1)} %convert_reduce_fusion.2, f32[1024]{0:T(1024)S(1)} %convert_reduce_fusion.1, ...), channel_id=1, replica_groups=mesh['dp'=8,'tr'=2,'tc'=2] {'dp'}, use_global_device_ids=true, to_apply=%region_44.45 | all-reduce | flops 3200 | bytes 25600 | tf_op jit(solution)/shard_map/psum | solution.py:356
  1157.4 37.6 %all-reduce.20 = (f32[768,2]{0,1:T(2,128)S(1)}, f32[768,5]{0,1:T(8,128)S(1)}, f32[512]{0:T(512)S(1)}) all-reduce(f32[768,2]{0,1:T(2,128)S(1)} %pad_maximum_fusion.8, f32[768,5]{0,1:T(8,128)S(1)} %stack.59, f32[512]{0:T(512)S(1)} %get-tuple-element.151), channel_id=10, replica_groups=mesh['dp'=8,'tr'=2,'tc'=2] {'dp','tr','tc'}, use_global_device_ids=true, to_apply=%region_33.34.clone | all-reduce | flops 5888 | bytes 47104
  1200.9 27.9 %reduce-scatter.38.cloned.1.call-done = f32[16,512]{1,0:T(8,128)} async-done(((f32[512,512]{1,0:T(8,128)}), f32[16,512]{1,0:T(8,128)}) %reduce-scatter.38.cloned.1.call-update) | async-done | bytes 32784 | tf_op jit(solution)/shard_map/reduce_scatter | solution.py:350
  1228.8 99.5 %reduce-scatter.34.cloned.1.call-done = f32[24,512]{1,0:T(8,128)} async-done(((f32[768,512]{1,0:T(8,128)}), f32[24,512]{1,0:T(8,128)}) %reduce-scatter.34.cloned.1.call-update) | async-done | bytes 49168 | tf_op jit(solution)/shard_map/reduce_scatter | solution.py:353
  1328.3 107.3 %reduce-scatter.36.cloned.1.call-done = f32[16,1536]{1,0:T(8,128)} async-done(((f32[512,1536]{1,0:T(8,128)}), f32[16,1536]{1,0:T(8,128)}) %reduce-scatter.36.cloned.1.call-update) | async-done | bytes 98320 | tf_op jit(solution)/shard_map/reduce_scatter | solution.py:347
  1435.5 105.2 %reduce-scatter.32.cloned.1.call-done = f32[24,768]{1,0:T(8,128)} async-done(((f32[768,768]{1,0:T(8,128)}), f32[24,768]{1,0:T(8,128)}) %reduce-scatter.32.cloned.1.call-update) | async-done | bytes 73744 | tf_op jit(solution)/shard_map/reduce_scatter | solution.py:340
  1540.8 234.2 %all-reduce.27.cloned.1.call-done = (f32[384,1536]{1,0:T(8,128)}, f32[1536,384]{1,0:T(8,128)}, f32[256,1024]{1,0:T(8,128)}, f32[1024,256]{1,0:T(8,128)}) async-done(((f32[384,1536]{1,0:T(8,128)}, f32[1536,384]{1,0:T(8,128)}, f32[256,1024]{1,0:T(8,128)}, f32[1024,256]{1,0:T(8,128)}), (f32[384,1536]{1,0:T(8,128)}, f32[1536,384]{1,0:T(8,128)}, f32[256,1024]{1,0:T(8,128)}, ...) | async-done | bytes 6815760 | tf_op jit(solution)/shard_map/psum | solution.py:356
  1775.0 124.3 %reduce-scatter.30.cloned.1.call-done = f32[24,2304]{1,0:T(8,128)} async-done(((f32[768,2304]{1,0:T(8,128)}), f32[24,2304]{1,0:T(8,128)}) %reduce-scatter.30.cloned.1.call-update) | async-done | bytes 221200 | tf_op jit(solution)/shard_map/reduce_scatter | solution.py:337
  (462 shorter events, 452.4 us)
Async XLA Ops:
  7.2 388.3 %copy-start = (bf16[1536,384]{1,0:T(8,128)(2,1)S(1)}, bf16[1536,384]{1,0:T(8,128)(2,1)}, u32[]{:S(2)}) copy-start(bf16[1536,384]{1,0:T(8,128)(2,1)} %param.31) | copy-start | bytes 3538948
  7.2 87.0 %all-gather.24.cloned.1.call-start = ((), (), s32[]{:S(2)}) async-start(), calls=%async_computation.11 | async-start | bytes 3649536 | tf_op jit(solution)/shard_map/all_gather | solution.py:268
  7.9 121.9 %all-gather.26.cloned.1.call-start = ((), (), s32[]{:S(2)}) async-start(), calls=%async_computation.12 | async-start | bytes 1216512 | tf_op jit(solution)/shard_map/all_gather | solution.py:269
  8.7 154.4 %all-gather.30.cloned.1.call-start = ((), (), s32[]{:S(2)}) async-start(), calls=%async_computation.19 | async-start | bytes 4116480 | tf_op jit(solution)/shard_map/all_gather | solution.py:108
  132.6 354.9 %copy-start.2 = (f32[529,768]{1,0:T(8,128)}, f32[529,768]{1,0:T(8,128)S(1)}, u32[]{:S(2)}) copy-start(f32[529,768]{1,0:T(8,128)S(1)} %get-tuple-element.169) | copy-start | bytes 4875268
  134.6 254.1 %all-gather.32.cloned.1.call-start = ((), (), s32[]{:S(2)}) async-start(), calls=%async_computation.20 | async-start | bytes 9805824 | tf_op jit(solution)/shard_map/all_gather | solution.py:122
  188.5 3.5 collective-permute-start
  225.7 121.5 %copy-start.80 = (bf16[24,512]{1,0:T(8,128)(2,1)S(1)}, bf16[24,512]{1,0:T(8,128)(2,1)}, u32[]{:S(2)}) copy-start(bf16[24,512]{1,0:T(8,128)(2,1)} %param.33) | copy-start | bytes 73732
  225.8 263.8 %all-gather.28.cloned.1.call-start = ((), (), s32[]{:S(2)}) async-start(), calls=%async_computation.13 | async-start | bytes 1622016 | tf_op jit(solution)/shard_map/all_gather | solution.py:272
  226.4 298.0 %all-gather.38.cloned.1.call-start = ((), (), s32[]{:S(2)}) async-start(), calls=%async_computation.23 | async-start | bytes 2744320 | tf_op jit(solution)/shard_map/all_gather | solution.py:108
  226.9 321.1 %all-gather.34.cloned.1.call-start = ((), (), s32[]{:S(2)}) async-start(), calls=%async_computation.21 | async-start | bytes 2744320 | tf_op jit(solution)/shard_map/all_gather | solution.py:108
  429.5 40.7 %collective-permute-start.1 = (bf16[14,384]{1,0:T(8,128)(2,1)S(1)}, bf16[14,384]{1,0:T(8,128)(2,1)S(1)}, u32[]{:S(2)}, u32[]{:S(2)}) collective-permute-start(bf16[14,384]{1,0:T(8,128)(2,1)S(1)} %slice.145), channel_id=1, source_target_pairs={{0,2},{1,3},{4,6},{5,7},{8,10},{9,11},{12,14},{13,15},{16,18},{17,... | collective-permute-start | bytes 32264
  522.9 146.0 %copy-start.4 = (f32[529,512]{1,0:T(8,128)}, f32[529,512]{1,0:T(8,128)S(1)}, u32[]{:S(2)}) copy-start(f32[529,512]{1,0:T(8,128)S(1)} %get-tuple-element.175) | copy-start | bytes 3250180
  524.3 102.5 %all-gather.40.cloned.1.call-start = ((), (), s32[]{:S(2)}) async-start(), calls=%async_computation.24 | async-start | bytes 6537216 | tf_op jit(solution)/shard_map/all_gather | solution.py:122
  571.6 4.2 collective-permute-start.4
  574.5 12.9 collective-permute-start.2
  612.7 143.6 %all-gather.42.cloned.1.call-start = ((), (), s32[]{:S(2)}) async-start(), calls=%async_computation.25 | async-start | bytes 4116480 | tf_op jit(solution)/shard_map/all_gather | solution.py:108
  655.3 3.5 collective-permute-start.5
  724.8 95.0 %all-gather.36.cloned.1.call-start = ((), (), s32[]{:S(2)}) async-start(), calls=%async_computation.22 | async-start | bytes 6537216 | tf_op jit(solution)/shard_map/all_gather | solution.py:122
  730.1 105.6 %all-gather.44.cloned.1.call-start = ((), (), s32[]{:S(2)}) async-start(), calls=%async_computation.26 | async-start | bytes 9805824 | tf_op jit(solution)/shard_map/all_gather | solution.py:122
  780.7 3.0 collective-permute-start.6
  808.9 190.8 %reduce-scatter.40.cloned.1.call-start = ((), (), s32[]{:S(2)}) async-start(), calls=%async_computation.27 | async-start | bytes 270336
  812.3 282.9 %reduce-scatter.42.cloned.1.call-start = ((), (), s32[]{:S(2)}) async-start(), calls=%async_computation.28 | async-start | bytes 270336
  813.4 415.3 %reduce-scatter.38.cloned.1.call-start = ((), (), s32[]{:S(2)}) async-start(), calls=%async_computation.18 | async-start | bytes 1081344 | tf_op jit(solution)/shard_map/reduce_scatter | solution.py:350
  816.4 511.9 %reduce-scatter.34.cloned.1.call-start = ((), (), s32[]{:S(2)}) async-start(), calls=%async_computation.16 | async-start | bytes 1622016 | tf_op jit(solution)/shard_map/reduce_scatter | solution.py:353
  819.7 615.8 %reduce-scatter.36.cloned.1.call-start = ((), (), s32[]{:S(2)}) async-start(), calls=%async_computation.17 | async-start | bytes 3244032 | tf_op jit(solution)/shard_map/reduce_scatter | solution.py:347
  830.6 710.2 %reduce-scatter.32.cloned.1.call-start = ((), (), s32[]{:S(2)}) async-start(), calls=%async_computation.15 | async-start | bytes 2433024 | tf_op jit(solution)/shard_map/reduce_scatter | solution.py:340
  888.1 4.4 collective-permute-start.7
  917.6 857.4 %all-reduce.27.cloned.1.call-start = ((), (), s32[]{:S(2)}) async-start(), calls=%async_computation.29 | async-start | bytes 13631488 | tf_op jit(solution)/shard_map/psum | solution.py:356
  940.5 958.8 %reduce-scatter.30.cloned.1.call-start = ((), (), s32[]{:S(2)}) async-start(), calls=%async_computation.14 | async-start | bytes 7299072 | tf_op jit(solution)/shard_map/reduce_scatter | solution.py:337
  1098.3 39.4 %collective-permute-start.3 = (bf16[6,256]{1,0:T(8,128)(2,1)S(1)}, bf16[6,256]{1,0:T(8,128)(2,1)S(1)}, u32[]{:S(2)}, u32[]{:S(2)}) collective-permute-start(bf16[6,256]{1,0:T(8,128)(2,1)S(1)} %slice.147), channel_id=1, source_target_pairs={{0,2},{1,3},{4,6},{5,7},{8,10},{9,11},{12,14},{13,15},{16,18},{17,... | collective-permute-start | bytes 9224
  1775.0 127.6 %copy-start.46 = (f32[1536,384]{1,0:T(8,128)S(1)}, f32[1536,384]{1,0:T(8,128)}, u32[]{:S(2)}) copy-start(f32[1536,384]{1,0:T(8,128)} %get-tuple-element.192) | copy-start | bytes 7077892
  (92 other events, 1178.2 us)
Sparse Core Ops, SparseCore 0:
  10.9 62.9 all-gather.23
  76.9 52.8 all-gather.25
  134.7 28.2 all-gather.29
  225.9 17.1 all-gather.31
  245.8 56.2 all-gather.27
  303.5 24.3 all-gather.37
  524.4 23.5 all-gather.33
  612.8 13.9 all-gather.39
  724.9 31.3 all-gather.41
  758.2 13.9 all-gather.35
  809.0 17.7 all-gather.43
  828.9 134.5 reduce-scatter.39
  965.8 129.3 reduce-scatter.41
  1097.9 130.8 reduce-scatter.37
  1235.3 92.9 reduce-scatter.33
  1335.0 100.5 reduce-scatter.35
  1442.7 98.0 reduce-scatter.31
  1546.4 228.5 all-reduce.26
  1781.3 118.0 reduce-scatter.29
where the time goes:
time: 1930 us; the launch traced here: 1910 us
  waiting for transfers between devices  882 us (46%)
  blocking collectives  491 us (25%)
  matrix products  205 us (11%)
  local copies, waits for them, and re-layouts  179 us (9%)
  other arithmetic  119 us (6%)
    psum x1, waiting for transfers between devices, local(): lax.psum((encoder_feed_grads[0], encoder_feed_grads[1], encoder_feed_grad...  234 us
    unnamed x8, blocking collectives  195 us
    unnamed x245, local copies, waits for them, and re-layouts  153 us
    reduce_scatter x1, waiting for transfers between devices, local(): lax.psum_scatter(encoder_attn_grads[2], ('dp', 'tr', 'tc'), scatter_dimen...  124 us
    reduce_scatter x1, waiting for transfers between devices, local(): lax.psum_scatter(decoder_attn_grads[2], ('dp', 'tr', 'tc'), scatter_dimen...  107 us
    reduce_scatter x1, waiting for transfers between devices, local(): lax.psum_scatter(encoder_attn_grads[3], ('dp', 'tr', 'tc'), scatter_dimen...  105 us
    unnamed x29, waiting for transfers between devices  100 us
    reduce_scatter x1, waiting for transfers between devices, local(): lax.psum_scatter(grad_embed, ('dp', 'tr', 'tc'), scatter_dimension=0, til...  99.5 us
  transfers between devices with their start and end apart: 27, of which 15 were waited for; matrix products, arithmetic and copies ran while one was open for 21% of the time, Pallas kernels for 0%

commit v1 on v0

v1 whole, which is shorter than its diff:
```python
import math
from functools import partial

import jax
import jax.numpy as jnp
from jax import lax
from jax.experimental import pallas as pl
from jax.experimental.pallas import tpu as pltpu
from jax.sharding import PartitionSpec as P

HEADS = 12
HEADS2 = 16
ALL = ("dp", "tr", "tc")
EPS = 1e-06
MASKED = -1e30
LOG2E = math.log2(math.e)
F32 = jnp.float32
BF = jnp.bfloat16
VMEM_BYTES = 58 * 1024 * 1024


def dot_nn(a, b):
    return lax.dot_general(a, b, (((1,), (0,)), ((), ())), preferred_element_type=F32)


def dot_nt(a, b):
    return lax.dot_general(a, b, (((1,), (1,)), ((), ())), preferred_element_type=F32)


def cost(us):
    return pl.CostEstimate(flops=int(us * 1e9), bytes_accessed=int(us * 3e6), transcendentals=0)


def call(body, outs, args, scratch=(), smem=0, us=2):
    specs = [pl.BlockSpec(memory_space=pltpu.SMEM)] * smem
    specs += [pl.BlockSpec(memory_space=pltpu.VMEM)] * (len(args) - smem)
    return pl.pallas_call(
        body,
        out_shape=[jax.ShapeDtypeStruct(s, d) for s, d in outs],
        in_specs=specs,
        out_specs=[pl.BlockSpec(memory_space=pltpu.VMEM)] * len(outs),
        scratch_shapes=[pltpu.VMEM(s, d) for s, d in scratch],
        compiler_params=pltpu.CompilerParams(vmem_limit_bytes=VMEM_BYTES),
        cost_estimate=cost(us),
    )(*args)


def norm_parts(v):
    center = v - jnp.mean(v, axis=-1, keepdims=True)
    r = lax.rsqrt(jnp.mean(center * center, axis=-1, keepdims=True) + EPS)
    return center * r, r


def norm_back(u, r, gain, y):
    e = y * gain
    back = r * (e - jnp.mean(e, axis=-1, keepdims=True) - u * jnp.mean(e * u, axis=-1, keepdims=True))
    return back, jnp.sum(y * u, axis=0, keepdims=True), jnp.sum(y, axis=0, keepdims=True)


def split3(v):
    hi = v.astype(BF)
    rest = v - hi.astype(F32)
    mid = rest.astype(BF)
    return hi, mid, (rest - mid.astype(F32)).astype(BF)


def head_masks(head_size):
    lane = lax.broadcasted_iota(jnp.int32, (1, 128), 1) // head_size
    return [(lane == h).astype(F32).astype(BF) for h in range(128 // head_size)]


def stack_heads(rows, masks):
    return jnp.concatenate([rows * m for m in masks], axis=0)


def prep_body(kept, mp_col, mp_row, tokens, cot, x_out, cot_out, place_out):
    rows, span = x_out.shape[0], tokens.shape[0]
    wide = lax.broadcasted_iota(jnp.int32, (mp_col.shape[0], span), 1)
    below = jnp.sum((mp_col[...] < wide).astype(F32), axis=0, keepdims=True)
    here = jnp.sum((mp_col[...] == wide).astype(F32), axis=0, keepdims=True)
    place = jnp.where(here > 0, kept, wide[:1] - below.astype(jnp.int32))
    pick = lax.broadcasted_iota(jnp.int32, (rows, span), 0) == place
    pick_f = pick.astype(F32)
    cot_out[...] = dot_nn(pick_f.astype(BF), cot[...])
    keep = lax.broadcasted_iota(jnp.int32, (rows, span), 0) < kept
    x_out[...] = dot_nn(jnp.where(keep, pick_f, 0.0).astype(BF), tokens[...]).astype(BF)
    tall = lax.broadcasted_iota(jnp.int32, (span, mp_row.shape[1]), 0)
    below_t = jnp.sum((mp_row[...] < tall).astype(F32), axis=1, keepdims=True)
    here_t = jnp.sum((mp_row[...] == tall).astype(F32), axis=1, keepdims=True)
    place_out[...] = jnp.where(here_t > 0, kept, tall[:, :1] - below_t.astype(jnp.int32))


def spread_back(place, rows, limit):
    at = lax.broadcasted_iota(jnp.int32, (place.shape[0], rows), 1)
    return jnp.where(at < limit, (at == place).astype(F32), 0.0).astype(BF)


def key_bias(lens, kept, rows, with_mask_row):
    at = lax.broadcasted_iota(jnp.int32, (rows, 1), 0)
    bias = jnp.where(at < lens[0], 0.0, MASKED)
    if with_mask_row:
        count = jnp.full((rows, 1), lens[1], jnp.int32).astype(F32)
        bias = jnp.where(at == kept, jnp.log(count) * LOG2E, bias)
    return bias


def attention_forward(packed, att_t, lse, bias, head_size):
    width = packed.shape[1] // 3
    rows = packed.shape[0]
    masks = head_masks(head_size)
    scale = head_size**-0.5 * LOG2E

    def group(g, carry):
        at = pl.multiple_of(g * 128, 128)
        q = packed[:, pl.ds(at, 128)]
        k = packed[:, pl.ds(width + at, 128)]
        v_t = packed[:, pl.ds(2 * width + at, 128)].T
        scores = dot_nt(k, stack_heads(q, masks)) * scale + bias
        peak = jnp.max(scores, axis=0, keepdims=True)
        weights = jnp.exp2(scores - peak)
        total = jnp.sum(weights, axis=0, keepdims=True)
        out = dot_nn(v_t, weights.astype(BF)) * (1.0 / total)
        for h in range(len(masks)):
            block = out[h * head_size : (h + 1) * head_size, h * rows : (h + 1) * rows]
            att_t[pl.ds(at + h * head_size, head_size), :] = block.astype(BF)
        lse[pl.ds(g, 1), :] = peak + jnp.log(total) * LOG2E
        return carry

    lax.fori_loop(0, width // 128, group, 0)


def attention_backward(packed, g_att, lse, g_packed, gq_t, bias, head_size):
    width = packed.shape[1] // 3
    rows = packed.shape[0]
    masks = head_masks(head_size)
    scale = head_size**-0.5

    def group(g, carry):
        at = pl.multiple_of(g * 128, 128)
        q = packed[:, pl.ds(at, 128)]
        k = packed[:, pl.ds(width + at, 128)]
        v = packed[:, pl.ds(2 * width + at, 128)]
        q_s = stack_heads(q, masks)
        g_s = stack_heads(g_att[:, pl.ds(at, 128)], masks)
        scores = dot_nt(k, q_s) * (scale * LOG2E) + bias
        probs = jnp.exp2(scores - lse[pl.ds(g, 1), :])
        g_v = dot_nn(probs.astype(BF), g_s)
        g_probs = dot_nt(v, g_s)
        delta = jnp.sum(g_probs * probs, axis=0, keepdims=True)
        g_scores = (probs * (g_probs - delta)).astype(BF)
        g_k = dot_nn(g_scores, q_s) * scale
        out = dot_nn(k.T, g_scores) * scale
        for h in range(len(masks)):
            block = out[h * head_size : (h + 1) * head_size, h * rows : (h + 1) * rows]
            gq_t[pl.ds(at + h * head_size, head_size), :] = block.astype(BF)
        g_packed[:, pl.ds(width + at, 128)] = g_k.astype(BF)
        g_packed[:, pl.ds(2 * width + at, 128)] = g_v.astype(BF)
        return carry

    lax.fori_loop(0, width // 128, group, 0)
    g_packed[:, :width] = gq_t[...].T


def project_in(stream, params, inproj, normed_out, packed_out):
    u, r = norm_parts(stream)
    normed = (u * params[0:1, :] + params[2:3, :]).astype(BF)
    normed_out[...] = normed
    width = stream.shape[1]
    step = 256
    for part in range(3):
        for at in range(0, width, step):
            lo = part * width + at
            value = dot_nn(normed, inproj[:, lo : lo + step])
            if part == 0:
                value = value + params[3:4, at : at + step]
            if part == 2:
                value = value + params[4:5, at : at + step]
            packed_out[:, lo : lo + step] = value.astype(BF)


GATHER_A = (("dp", 4), ("tr", 1), ("dp", 2), ("dp", 1))
GATHER_B = (("dp", 4), ("tr", 1), ("dp", 1), ("dp", 2))
GATHER_C = (("tr", 1), ("dp", 4), ("dp", 2), ("dp", 1))
GATHER_D = (("tr", 1), ("dp", 4), ("dp", 1), ("dp", 2))
SCATTER_A = (("tr", 1), ("dp", 1), ("dp", 2), ("dp", 4))
SCATTER_B = (("dp", 1), ("tr", 1), ("dp", 2), ("dp", 4))
SCATTER_C = (("dp", 2), ("dp", 1), ("tr", 1), ("dp", 4))


def differences(order, bits):
    dp = tr = 0
    for (axis, distance), bit in zip(order, bits):
        if axis == "dp":
            dp = dp + distance * bit
        else:
            tr = tr + bit
    return dp, tr


def gathered_block(order, j, last):
    return differences(order, (j & 1, (j >> 1) & 1, (j >> 2) & 1, last))


def scattered_block(order, m):
    return differences(order, (m >> 3, (m >> 2) & 1, (m >> 1) & 1, m & 1))


def feed_block(m):
    return (m & 1) * 4 + ((m >> 1) & 1) * 2 + (m >> 2)


def place_rows(place, order, sources, block, put):
    first = place[2] == 0
    for x in range(2):
        own_ref, oth_ref = sources[x], sources[2 + x]
        count = own_ref.shape[0] // block

        def one(j, carry, own_ref=own_ref, oth_ref=oth_ref, x=x):
            dp, tr = gathered_block(order, j, x)
            chip = (place[0] ^ dp) * 2 + (place[1] ^ tr)
            at = pl.multiple_of(j * block, block)
            own = own_ref[pl.ds(at, block), :].astype(F32)
            oth = oth_ref[pl.ds(at, block), :].astype(F32)
            put(chip, jnp.where(first, own, oth), jnp.where(first, oth, own))
            return carry

        lax.fori_loop(0, count, one, 0)


def place_halves(place, order, sources, cuts):
    block = sources[0].shape[0] // 8
    half = block // 2

    def put(chip, low, high):
        at = pl.multiple_of(chip * block, block)
        top = jnp.concatenate([low[:half], high[:half]], axis=0).astype(BF)
        bottom = jnp.concatenate([low[half:], high[half:]], axis=0).astype(BF)
        lo = 0
        for target, first, width, shift in cuts:
            target[pl.ds(at, block), first : first + width] = top[:, lo : lo + width]
            if shift is not None:
                right = first + shift
                target[pl.ds(at, block), right : right + width] = bottom[:, lo : lo + width]
            lo += width

    place_rows(place, order, sources, block, put)


def place_whole(place, order, sources, cuts):
    block = sources[0].shape[0] // 8

    def put(chip, low, high):
        at = pl.multiple_of(chip * 2 * block, 2 * block)
        both = jnp.concatenate([low, high], axis=0).astype(BF)
        lo = 0
        for target, width in cuts:
            target[pl.ds(at, 2 * block), :] = both[:, lo : lo + width]
            lo += width

    place_rows(place, order, sources, block, put)


def param_rows(columns):
    return columns[...].astype(F32).T[:16]


def reorder_rows(place, order, source, target):
    block = source.shape[0] // 32
    for core in range(2):
        for m in range(16):
            dp, tr = scattered_block(order, m)
            device = ((place[0] ^ dp) * 2 + (place[1] ^ tr)) * 2 + (place[2] ^ core)
            at = pl.multiple_of(device * block, 8)
            to = (core * 16 + m) * block
            target[to : to + block, :] = source[pl.ds(at, block), :]


def write_halves(ordered, columns, outs, first=0, count=None):
    half_rows = ordered.shape[0] // 2
    block = half_rows // 16
    width = columns.shape[1] // 2
    count = width if count is None else count
    step = max(n for n in (384, 320, 256) if count % n == 0) if count != 640 else 640
    for core in range(2):
        rows = ordered[core * half_rows : (core + 1) * half_rows, :].astype(BF)
        for at in range(first, first + count, step):
            left = dot_nn(rows, columns[:, at : at + step])
            right = dot_nn(rows, columns[:, width + at : width + at + step])
            for m in range(16):
                both = [left[m * block : (m + 1) * block], right[m * block : (m + 1) * block]]
                outs[core][m * 2 * block : (m + 1) * 2 * block, at - first : at - first + step] = (
                    jnp.concatenate(both, axis=0).astype(BF)
                )


def write_whole(ordered, columns, outs, lo):
    half_rows = ordered.shape[0] // 2
    width = columns.shape[1]
    for core in range(2):
        rows = ordered[core * half_rows : (core + 1) * half_rows, :].astype(BF)
        for at in range(0, width, 256):
            outs[core][:, lo + at : lo + at + 256] = dot_nn(rows, columns[:, at : at + 256]).astype(BF)


def small_columns(small):
    table = jnp.concatenate([small[...], jnp.zeros((112, small.shape[1]), F32)], axis=0)
    return table.T


def pack_body(
    e_gains, e_biases, e_in, e_out, embed, d_gains, d_biases, token, d_in, d_out, one_a, one_b, two, three
):
    def columns(parts):
        total, lo = 0.0, 0
        for part in parts:
            count, rows = part.shape
            spot = lax.broadcasted_iota(jnp.int32, (count, 128), 1)
            want = lax.broadcasted_iota(jnp.int32, (count, 128), 0) + lo
            table = (spot == want).astype(F32).astype(BF)
            total = total + lax.dot_general(
                part[...], table, (((0,), (0,)), ((), ())), preferred_element_type=F32
            )
            lo += count
        return total

    e_par = columns([e_gains, e_biases])

    def halves(v):
        v = v[...].astype(F32)
        width = v.shape[1] // 2
        return jnp.concatenate([v[:, :width], v[:, width:]], axis=0).astype(BF)

    n = one_a.shape[1]
    m = one_b.shape[1] - 128
    both = halves(e_in)
    one_a[...] = both[:, :n]
    one_b[:, :m] = both[:, n:]
    one_b[:, m:] = jnp.concatenate([e_par, jnp.zeros_like(e_par)], axis=0).astype(BF)
    n = e_out.shape[1] // 2
    two[:, :n] = halves(e_out)
    two[:, n:] = halves(embed)
    n = d_in.shape[1]
    m = n + d_out.shape[1]
    three[:, :n] = d_in[...]
    three[:, n:m] = d_out[...]
    three[:, m:] = columns([d_gains, d_biases, token]).astype(BF)


def enc_attn_body(
    kept, place, x, s0, s1, s2, s3, r0, r1, r2, r3,
    normed, packed, att_t, lse, inproj, par_t, par_c,
):
    width = x.shape[1]
    n, shift = s0.shape[1], 3 * width // 2
    place_halves(place, GATHER_A, (s0, s1, s2, s3), ((inproj, 0, n, shift),))
    place_halves(
        place, GATHER_B, (r0, r1, r2, r3), ((inproj, n, shift - n, shift), (par_c, 0, 128, None))
    )
    par_t[...] = param_rows(par_c)
    project_in(x[...].astype(F32), par_t, inproj, normed, packed)
    bias = key_bias((place[5], place[6]), kept, x.shape[0], False)
    attention_forward(packed, att_t, lse, bias, width // HEADS)


def dec_attn_body(
    kept, place, e_low, embed, s0, s1, s2, s3,
    stream, normed, packed, att_t, lse, inproj, outproj, params, par_c,
):
    rows = e_low.shape[0]
    width = stream.shape[1]
    place_whole(
        place, GATHER_D, (s0, s1, s2, s3), ((inproj, 3 * width), (outproj, width), (par_c, 128))
    )
    params[...] = param_rows(par_c)
    embedded = dot_nn(e_low[...], embed[...]) + params[7:8, :]
    at = lax.broadcasted_iota(jnp.int32, (rows, 1), 0)
    decoded = jnp.where(at < kept, embedded, params[8:9, :])
    stream[...] = decoded
    project_in(decoded, params, inproj, normed, packed)
    bias = key_bias((place[5], place[6]), kept, rows, True)
    attention_forward(packed, att_t, lse, bias, width // HEADS2)


def load_feed(place, ups, downs, up, down, sems, part=0):
    copies = []
    half = up.shape[0] // 2
    units = up.shape[1] // 2
    for tr in range(2):
        for core in range(2):
            at = pl.multiple_of((place[4] ^ core) * half, 128)
            n = 2 * (2 * tr + core)
            here = pl.ds(part * units, units)
            to_up = up.at[pl.ds(at, half), pl.ds(tr * units, units)]
            to_down = down.at[pl.ds(tr * units, units), pl.ds(at, half)]
            copies.append(pltpu.make_async_copy(ups[2 * tr + core].at[:, here], to_up, sems.at[n]))
            copies.append(
                pltpu.make_async_copy(downs[2 * tr + core].at[here, :], to_down, sems.at[n + 1])
            )
    for copy in copies:
        copy.start()
    return copies


def middle_of(stream, att_t, outproj, params):
    return stream + dot_nn(att_t[...].T, outproj[...]) + params[5:6, :]


def feed_forward(normed_two, up, up_bias, down, active_out, slope_out, total, step):
    hidden_units = up.shape[1]
    total[...] = jnp.zeros_like(total)

    def chunk(c, carry):
        at = pl.multiple_of(c * step, step)
        hidden = dot_nn(normed_two, up[:, pl.ds(at, step)]) + up_bias[:, pl.ds(at, step)]
        phi = 0.5 * (1.0 + lax.erf(hidden * math.sqrt(0.5)))
        bell = jnp.exp2(hidden * hidden * (-0.5 * LOG2E)) * (1.0 / math.sqrt(2 * math.pi))
        active = (hidden * phi).astype(BF)
        active_out[:, pl.ds(at, step)] = active
        slope_out[:, pl.ds(at, step)] = (phi + hidden * bell).astype(BF)
        total[...] += dot_nn(active, down[pl.ds(at, step), :])
        return carry

    lax.fori_loop(0, hidden_units // step, chunk, 0)


def feed_backward(
    place, part, parts, g_result, normed_two, active, slope, up, down,
    g_ups, g_downs, g_upbias, g_normed, step, normed_t, ordered_t, act_t, act_o, g_cols,
):
    width = normed_two.shape[1]
    half = width // 2
    count = up.shape[1] // 2
    units = count * parts
    block, hidden_block = half // 8, count // 8
    g_cols[:, :half] = g_result[:, pl.ds(pl.multiple_of(place[4] * half, 128), half)]
    g_cols[:, half:] = g_result[:, pl.ds(pl.multiple_of((1 - place[4]) * half, 128), half)]
    normed_t[...] = normed_two[...].T
    for core in range(2):
        for m in range(8):
            at = ((place[4] ^ core) * 8 + (place[3] ^ feed_block(m))) * block
            to = (core * 8 + m) * block
            ordered_t[to : to + block, :] = normed_t[pl.ds(pl.multiple_of(at, block), block), :]
    for tr in range(2):
        base = tr * units + part * count
        out_base = pl.multiple_of((place[7] ^ tr) * units + part * count, 128)
        act_t[...] = active[:, base : base + count].T
        for m in range(8):
            at = pl.multiple_of((place[3] ^ feed_block(m)) * hidden_block, hidden_block)
            to = m * hidden_block
            act_o[to : to + hidden_block, :] = act_t[pl.ds(at, hidden_block), :]

        def chunk(c, carry, tr=tr, base=base, out_base=out_base):
            at = pl.multiple_of(c * step, step)
            here = pl.ds(pl.multiple_of(tr * count + at, 128), step)
            g_active = dot_nt(g_result[...], down[here, :]).astype(BF).astype(F32)
            there = pl.ds(pl.multiple_of(base + at, 128), step)
            g_hidden = (slope[:, there].astype(F32) * g_active).astype(BF)
            g_upbias[:, pl.ds(pl.multiple_of(out_base + at, 128), step)] = jnp.sum(
                g_hidden.astype(F32), axis=0, keepdims=True
            )
            g_up = dot_nn(ordered_t[...], g_hidden).astype(BF)
            g_ups[2 * tr][:, pl.ds(at, step)] = g_up[:half]
            g_ups[2 * tr + 1][:, pl.ds(at, step)] = g_up[half:]
            g_down = dot_nn(act_o[pl.ds(at, step), :], g_cols[...]).astype(BF)
            g_downs[2 * tr][pl.ds(at, step), :] = g_down[:, :half]
            g_downs[2 * tr + 1][pl.ds(at, step), :] = g_down[:, half:]
            g_normed[...] += dot_nt(g_hidden, up[:, here])
            return carry

        lax.fori_loop(0, count // step, chunk, 0)


def after_feed_backward(
    place, order, g_out, g_normed, middle, params, att_t, outproj, g_middle, g_att, small, att_f, att_o
):
    u, r = norm_parts(middle)
    y = g_normed.astype(BF).astype(F32)
    back, g_gain, g_shift = norm_back(u, r, params[1:2, :], y)
    grad = g_out + back
    g_middle[...] = grad
    branch = grad.astype(BF)
    att_f[...] = att_t[...].astype(F32)
    reorder_rows(place, order, att_f, att_o)
    g_att[...] = dot_nt(branch, outproj[...]).astype(BF)
    small[1:2, :] = g_gain
    small[5:6, :] = jnp.sum(branch.astype(F32), axis=0, keepdims=True)
    small[6:7, :] = g_shift
    return branch


def enc_feed_body(
    place, x, att_t, s0, s1, s2, s3, params, up_bias, down_bias, u0, u1, u2, u3, d0, d1, d2, d3,
    middle, normed_two, active, slope, e_low, outproj, embed, up, down, total, sems,
):
    copies = load_feed(place, (u0, u1, u2, u3), (d0, d1, d2, d3), up, down, sems)
    width = x.shape[1]
    n, m = width // 2, embed.shape[1] // 2
    place_halves(
        place, GATHER_C, (s0, s1, s2, s3), ((outproj, 0, n, n), (embed, 0, m, m))
    )
    mid = middle_of(x[...].astype(F32), att_t, outproj, params)
    middle[...] = mid
    u, r = norm_parts(mid)
    n2 = (u * params[1:2, :] + params[6:7, :]).astype(BF)
    normed_two[...] = n2
    for copy in copies:
        copy.wait()
    feed_forward(n2, up, up_bias, down, active, slope, total, 512)
    result = (total[...] + down_bias[...]).astype(BF)
    e_low[...] = (middle[...] + result.astype(F32)).astype(BF)


def dec_feed_body(
    kept, place, stream, att_t, outproj, params, up_bias, down_bias, cot, spots,
    u0, u1, u2, u3, d0, d1, d2, d3,
    output, gu0, gu1, gu2, gu3, gd0, gd1, gd2, gd3, g_middle, g_att, go0, go1, small, biases,
    up, down, active, slope, total, n2_s, g_res, normed_t, ordered_t, act_t, act_o, g_cols,
    att_f, att_o, branch_s, sems,
):
    copies = load_feed(place, (u0, u1, u2, u3), (d0, d1, d2, d3), up, down, sems)
    mid = middle_of(stream[...], att_t, outproj, params)
    u, r = norm_parts(mid)
    n2 = (u * params[1:2, :] + params[6:7, :]).astype(BF)
    n2_s[...] = n2
    for copy in copies:
        copy.wait()
    feed_forward(n2, up, up_bias, down, active, slope, total, 512)
    result = (total[...] + down_bias[...]).astype(BF)
    out = mid + result.astype(F32)
    pick = spread_back(spots[...], out.shape[0], kept + 1)
    hi, mid_part, low = split3(out)
    output[...] = dot_nn(pick, hi) + dot_nn(pick, mid_part) + dot_nn(pick, low)
    g_out = cot[...]
    g_res[...] = g_out.astype(BF)
    small[...] = jnp.zeros_like(small)
    units = up.shape[1]
    biases[:, units:] = jnp.sum(g_res[...].astype(F32), axis=0, keepdims=True)
    total[...] = jnp.zeros_like(total)
    feed_backward(
        place, 0, 1, g_res, n2_s, active, slope, up, down, (gu0, gu1, gu2, gu3),
        (gd0, gd1, gd2, gd3), biases, total, 512, normed_t, ordered_t, act_t, act_o, g_cols,
    )
    branch = after_feed_backward(
        place, SCATTER_A, g_out, total[...], mid, params, att_t, outproj, g_middle, g_att, small, att_f, att_o
    )
    branch_s[...] = branch
    write_whole(att_o, branch_s, (go0, go1), 0)


def enc_feed_back_one_body(
    place, g_enc, normed_two, active, slope, u0, u1, u2, u3, d0, d1, d2, d3,
    gu0, gu1, gu2, gu3, gd0, gd1, gd2, gd3, total, biases,
    up, down, g_res, normed_t, ordered_t, act_t, act_o, g_cols, sems,
):
    copies = load_feed(place, (u0, u1, u2, u3), (d0, d1, d2, d3), up, down, sems)
    g_res[...] = g_enc[...].astype(BF)
    total[...] = jnp.zeros_like(total)
    biases[:, 2 * up.shape[1] :] = jnp.sum(g_res[...].astype(F32), axis=0, keepdims=True)
    for copy in copies:
        copy.wait()
    feed_backward(
        place, 0, 2, g_res, normed_two, active, slope, up, down, (gu0, gu1, gu2, gu3),
        (gd0, gd1, gd2, gd3), biases, total, 384, normed_t, ordered_t, act_t, act_o, g_cols,
    )


def enc_feed_back_two_body(
    place, g_enc, normed_two, active, slope, total_in, biases_in, biases_dec, middle, params, att_t,
    outproj, u0, u1, u2, u3, d0, d1, d2, d3,
    gu0, gu1, gu2, gu3, gd0, gd1, gd2, gd3, g_middle, g_att, go0, go1, small, biases,
    total, up, down, g_res, normed_t, ordered_t, act_t, act_o, g_cols, att_f, att_o, branch_s, sems,
):
    copies = load_feed(place, (u0, u1, u2, u3), (d0, d1, d2, d3), up, down, sems, 1)
    g_res[...] = g_enc[...].astype(BF)
    total[...] = total_in[...]
    count = biases_in.shape[1]
    biases[:, :count] = biases_in[...]
    biases[:, count:] = biases_dec[...]
    small[...] = jnp.zeros_like(small)
    for copy in copies:
        copy.wait()
    feed_backward(
        place, 1, 2, g_res, normed_two, active, slope, up, down, (gu0, gu1, gu2, gu3),
        (gd0, gd1, gd2, gd3), biases, total, 384, normed_t, ordered_t, act_t, act_o, g_cols,
    )
    branch = after_feed_backward(
        place, SCATTER_C, g_enc[...], total[...], middle[...], params, att_t, outproj, g_middle, g_att, small,
        att_f, att_o,
    )
    branch_s[...] = branch
    write_halves(att_o, branch_s, (go0, go1))


def project_back(place, order, stream, normed, g_packed, g_middle, params, inproj, small, first, rows_f, rows_o):
    width = stream.shape[1]
    rows_f[...] = normed[...].astype(F32).T
    reorder_rows(place, order, rows_f, rows_o)
    g_normed = dot_nt(g_packed[...], inproj[...])
    u, r = norm_parts(stream)
    back, g_gain, g_shift = norm_back(u, r, params[0:1, :], g_normed)
    small[...] = first[...]
    small[0:1, :] = g_gain
    small[2:3, :] = g_shift
    small[3:4, :] = jnp.sum(g_packed[:, :width].astype(F32), axis=0, keepdims=True)
    small[4:5, :] = jnp.sum(g_packed[:, 2 * width :].astype(F32), axis=0, keepdims=True)
    return g_middle[...] + back


def dec_attn_back_body(
    kept, place, packed, g_att, lse, stream, normed, g_middle, params, inproj, embed, e_low, first,
    go0, go1, gi0, gi1, ge0, ge1, g_enc, small, g_packed, gq_t, rows_f, rows_o, cols, cols_o,
    emb_f, emb_o, g_emb,
):
    rows = stream.shape[0]
    width = stream.shape[1]
    bias = key_bias((place[5], place[6]), kept, rows, True)
    attention_backward(packed, g_att, lse, g_packed, gq_t, bias, width // HEADS2)
    g_stream = project_back(
        place, SCATTER_A, stream[...], normed, g_packed, g_middle, params, inproj, small, first, rows_f, rows_o,
    )
    write_whole(rows_o, g_packed, (gi0, gi1), 0)
    at = lax.broadcasted_iota(jnp.int32, (rows, 1), 0)
    small[8:9, :] = jnp.sum(jnp.where(at == kept, g_stream, 0.0), axis=0, keepdims=True)
    g_embedded = jnp.where(at < kept, g_stream, 0.0).astype(BF)
    small[7:8, :] = jnp.sum(g_embedded.astype(F32), axis=0, keepdims=True)
    g_emb[...] = g_embedded
    g_enc[...] = dot_nt(g_embedded, embed[...])
    emb_f[...] = e_low[...].astype(F32).T
    reorder_rows(place, SCATTER_B, emb_f, emb_o)
    write_halves(emb_o, g_emb, (ge0, ge1))
    cols[...] = small_columns(small)
    reorder_rows(place, SCATTER_A, cols, cols_o)
    n = cols_o.shape[0] // 2
    for core, (gi, go) in enumerate(((gi0, go0), (gi1, go1))):
        gi[:, 3 * width : 4 * width] = go[...]
        gi[:, 4 * width :] = cols_o[core * n : (core + 1) * n, :].astype(BF)


def enc_attn_back_body(
    kept, place, packed, g_att, lse, x, normed, g_middle, params, inproj, first, spots,
    ga0, ga1, gb0, gb1, g_tokens, small, g_packed, gq_t, rows_f, rows_o, cols, cols_o,
):
    rows = x.shape[0]
    width = x.shape[1]
    bias = key_bias((place[5], place[6]), kept, rows, False)
    attention_backward(packed, g_att, lse, g_packed, gq_t, bias, width // HEADS)
    g_stream = project_back(
        place, SCATTER_A, x[...].astype(F32), normed, g_packed, g_middle, params, inproj, small, first,
        rows_f, rows_o,
    )
    n = ga0.shape[1]
    write_halves(rows_o, g_packed, (ga0, ga1), 0, n)
    reorder_rows(place, SCATTER_B, rows_f, rows_o)
    m = 3 * width // 2 - n
    write_halves(rows_o, g_packed, (gb0, gb1), n, m)
    cols[...] = small_columns(small)
    reorder_rows(place, SCATTER_B, cols, cols_o)
    count = cols_o.shape[0] // 2
    block = count // 16
    for core, out in enumerate((gb0, gb1)):
        for k in range(16):
            part = cols_o[core * count + k * block : core * count + (k + 1) * block, :]
            both = jnp.concatenate([part, jnp.zeros_like(part)], axis=0).astype(BF)
            out[k * 2 * block : (k + 1) * 2 * block, m:] = both
    pick = spread_back(spots[...], rows, kept)
    hi, mid, low = split3(g_stream)
    g_tokens[...] = dot_nn(pick, hi) + dot_nn(pick, mid) + dot_nn(pick, low)


def out_feed_body(parts, place, *refs):
    n = 4 * parts
    g_up, g_down = refs[n:]
    units = g_up.shape[1] // parts
    for part in range(parts):
        for x in range(2):
            u_ref, d_ref = refs[4 * part + x], refs[4 * part + 2 + x]
            block, hidden_block = u_ref.shape[0] // 4, d_ref.shape[0] // 4
            for m in range(4):
                dp = place[3] ^ feed_block(4 * x + m)
                at = pl.multiple_of(dp * block, block)
                g_up[pl.ds(at, block), part * units : (part + 1) * units] = u_ref[
                    m * block : (m + 1) * block, :
                ].astype(F32)
                at = pl.multiple_of(part * units + dp * hidden_block, hidden_block)
                g_down[pl.ds(at, hidden_block), :] = d_ref[
                    m * hidden_block : (m + 1) * hidden_block, :
                ].astype(F32)


def out_dec_body(mine, theirs, g_in, g_out, g_gains, g_biases, g_token):
    total = mine[...].astype(F32) + theirs[...].astype(F32)
    n, m = g_in.shape[1], g_in.shape[1] + g_out.shape[1]
    g_in[...] = total[:, :n]
    g_out[...] = total[:, n:m]
    rows = total[:, m:].T
    g_gains[...] = rows[0:2]
    g_biases[...] = rows[2:8]
    g_token[...] = rows[8:9]


def out_halves_body(mine, theirs, out):
    total = mine[...].astype(F32) + theirs[...].astype(F32)
    n, width = out.shape[0], out.shape[1] // 2
    out[:, :width] = total[:n]
    out[:, width:] = total[n:]


def out_enc_body(mine_a, theirs_a, mine_b, theirs_b, g_in, g_gains, g_biases):
    a = mine_a[...].astype(F32) + theirs_a[...].astype(F32)
    b = mine_b[...].astype(F32) + theirs_b[...].astype(F32)
    n, width, cut = g_in.shape[0], g_in.shape[1] // 2, a.shape[1]
    rest = width - cut
    g_in[:, :cut] = a[:n]
    g_in[:, cut:width] = b[:n, :rest]
    g_in[:, width : width + cut] = a[n:]
    g_in[:, width + cut :] = b[n:, :rest]
    rows = b[:n, rest:].T
    g_gains[...] = rows[0:2]
    g_biases[...] = rows[2:7]


def out_bias_body(place, biases, up1, down1, up2, down2):
    lo = 0
    for k, (out, at) in enumerate(((up1, place[7]), (down1, place[4]), (up2, place[7]), (down2, place[4]))):
        n = out.shape[1]
        out[...] = biases[:, pl.ds(pl.multiple_of(lo + at * n, 128), n)]
        lo += 2 * n


def swap(v, axis, distance=1):
    return lax.ppermute(v, axis, [(i, i ^ distance) for i in range(lax.axis_size(axis))])


def add(a, b):
    return (a.astype(F32) + b.astype(F32)).astype(BF)


class Flight:
    def __init__(self, steps):
        self.steps, self.result = steps, None
        self.waits = next(steps)

    def land(self, arrays):
        try:
            self.waits = self.steps.send(arrays)
        except StopIteration as end:
            self.waits, self.result = None, end.value


def land(flights, outs=()):
    flights = [f for f in flights if f.waits is not None]
    outs, arrays = lax.optimization_barrier((outs, [f.waits for f in flights]))
    for flight, landed in zip(flights, arrays):
        flight.land(landed)
    return outs


def finish(flight):
    while flight.waits is not None:
        flight.land(flight.waits)
    return flight.result


def gather_all(v, order):
    for axis, distance in order[:-1]:
        (got,) = yield (swap(v, axis, distance),)
        v = jnp.concatenate([v, got], axis=0)
    (last,) = yield (swap(v, *order[-1]),)
    a, b = yield (swap(v, "tc"), swap(last, "tc"))
    return v, last, a, b


def scatter_all(pair, order):
    own, oth = pair
    (got,) = yield (swap(oth, "tc"),)
    v = add(own, got)
    for axis, distance in order[:-1]:
        half = v.shape[0] // 2
        (got,) = yield (swap(v[half:], axis, distance),)
        v = add(v[:half], got)
    half = v.shape[0] // 2
    (got,) = yield (swap(v[half:], *order[-1]),)
    return v[:half], got


def reduce_feed(parts, x_first):
    one, two = yield (swap(parts[1], "tc"), swap(parts[3], "tc"))
    near, far = add(parts[0], one), add(parts[2], two)
    half = near.shape[0] // 2
    if x_first:
        one, two = yield (swap(near[half:], "dp", 1), swap(far[half:], "dp", 1))
        near, far = add(near[:half], one), add(far[:half], two)
    (got,) = yield (swap(far, "tr"),)
    v = add(near, got)
    for distance in (2, 4) if x_first else (1, 2, 4):
        half = v.shape[0] // 2
        (got,) = yield (swap(v[half:], "dp", distance),)
        v = add(v[:half], got)
    for distance in (4, 2):
        (got,) = yield (swap(v, "dp", distance),)
        v = jnp.concatenate([v, got], axis=0)
    (got,) = yield (swap(v, "dp", 1),)
    return v, got


def reduce_small(v):
    for axis, distance in (("tc", 1),) + SCATTER_A:
        (got,) = yield (swap(v, axis, distance),)
        v = v + got
    return v


def from_far(v):
    (far,) = yield (swap(v, "tr"),)
    (other,) = yield (swap(far, "tc"),)
    return far, other


def near_far(v):
    (far,) = yield (swap(v, "tr"),)
    return far


def near_swap(*arrays):
    got = yield tuple(swap(v, "tc") for v in arrays)
    return got


def chip_axes(order):
    return [{("dp", 4): 0, ("dp", 2): 1, ("dp", 1): 2, ("tr", 1): 3}[step] for step in order]


def cut_gathered(whole, order, halves):
    rows, width = whole.shape
    if halves:
        v = whole.reshape(32, rows // 32, 2, width // 2).transpose(0, 2, 1, 3)
        v = v.reshape(32, rows // 16, width // 2)
    else:
        v = whole.reshape(32, rows // 32, width)
    v = v.reshape((2, 2, 2, 2, 2) + v.shape[1:])
    first = chip_axes(order)
    v = v.transpose(first[3], 4, first[2], first[1], first[0], 5, 6)
    v = v.reshape(2, 2, -1, v.shape[-1])
    return v[0, 0], v[1, 0], v[0, 1], v[1, 1]


def join_scattered(pair, order, halves):
    v = jnp.stack(pair)
    v = v.reshape(2, 2, 2, 2, 2, v.shape[1] // 16, v.shape[2])
    first = chip_axes(order)
    v = v.transpose(*(1 + first.index(k) for k in range(4)), 0, 5, 6)
    v = v.reshape(32, v.shape[5], v.shape[6])
    if halves:
        v = v.reshape(32, 2, v.shape[1] // 2, v.shape[2]).transpose(0, 2, 1, 3)
        v = v.reshape(32, v.shape[1], -1)
    return v.reshape(-1, v.shape[-1])


def call2(body, outs, args, scratch=(), any_args=0, sems=0, us=2):
    count = len(args) - 1 - any_args
    specs = [pl.BlockSpec(memory_space=pltpu.SMEM)]
    specs += [pl.BlockSpec(memory_space=pltpu.VMEM)] * count
    specs += [pl.BlockSpec(memory_space=pl.ANY)] * any_args
    shapes = [pltpu.VMEM(s, d) for s, d in scratch]
    if sems:
        shapes.append(pltpu.SemaphoreType.DMA((sems,)))
    return pl.pallas_call(
        body,
        out_shape=[jax.ShapeDtypeStruct(s, d) for s, d in outs],
        in_specs=specs,
        out_specs=[pl.BlockSpec(memory_space=pltpu.VMEM)] * len(outs),
        scratch_shapes=shapes,
        compiler_params=pltpu.CompilerParams(vmem_limit_bytes=VMEM_BYTES),
        cost_estimate=cost(us),
    )(*args)


class Sentence:
    def __init__(self, place, tokens, mask_pos, cot):
        self.place = place
        span, self.width = tokens.shape
        masks = mask_pos.shape[1]
        self.span, self.kept = span, span - masks
        self.rows = -(-(self.kept + 1) // 16) * 16
        self.width2 = cot.shape[1]
        self.x, self.cot, self.spots = call(
            partial(prep_body, self.kept),
            [((self.rows, self.width), BF), ((self.rows, self.width2), F32), ((span, 1), jnp.int32)],
            [mask_pos.reshape(masks, 1), mask_pos, tokens, cot],
            us=3,
        )

    def enc_attn(self, one_a, one_b):
        rows, width = self.rows, self.width
        self.normed, self.packed, self.att_t, self.lse, self.e_in, self.e_par = call2(
            partial(enc_attn_body, self.kept),
            [((rows, width), BF), ((rows, 3 * width), BF), ((width, rows), BF),
             ((width // 128, rows * (128 * HEADS // width)), F32), ((width, 3 * width), BF),
             ((16, width), F32)],
            [self.place, self.x, *one_a, *one_b],
            scratch=[((width, 128), BF)],
            us=12,
        )

    def enc_feed(self, two, ups, downs, up_bias, down_bias):
        rows, width, hidden = self.rows, self.width, up_bias.shape[1]
        self.e_ups, self.e_downs = ups, downs
        self.middle, self.normed_two, self.active, self.slope, self.e_low, self.e_out, self.embed = call2(
            enc_feed_body,
            [((rows, width), F32), ((rows, width), BF), ((rows, hidden), BF), ((rows, hidden), BF),
             ((rows, width), BF), ((width, width), BF), ((width, self.width2), BF)],
            [self.place, self.x, self.att_t, *two, self.e_par, up_bias, down_bias, *ups, *downs],
            scratch=[((width, hidden), BF), ((hidden, width), BF), ((rows, width), F32)],
            any_args=8,
            sems=8,
            us=15,
        )

    def dec_attn(self, three):
        rows, width = self.rows, self.width2
        (self.stream2, self.normed2, self.packed2, self.att2_t, self.lse2, self.d_in, self.d_out,
         self.d_par) = call2(
            partial(dec_attn_body, self.kept),
            [((rows, width), F32), ((rows, width), BF), ((rows, 3 * width), BF), ((width, rows), BF),
             ((width // 128, rows * (128 * HEADS2 // width)), F32), ((width, 3 * width), BF),
             ((width, width), BF), ((16, width), F32)],
            [self.place, self.e_low, self.embed, *three],
            scratch=[((width, 128), BF)],
            us=11,
        )

    def dec_feed(self, ups, downs, up_bias, down_bias):
        rows, width, hidden = self.rows, self.width2, up_bias.shape[1]
        ff = [((width // 2, hidden // 2), BF)] * 4 + [((hidden // 2, width // 2), BF)] * 4
        (self.output, *g_ff, self.g_middle2, self.g_att2, self.go20, self.go21, self.small2,
         self.biases2) = call2(
            partial(dec_feed_body, self.kept),
            [((self.span, width), F32), *ff, ((rows, width), F32), ((rows, width), BF),
             ((width // 2, width), BF), ((width // 2, width), BF), ((16, width), F32),
             ((1, hidden + width), F32)],
            [self.place, self.stream2, self.att2_t, self.d_out, self.d_par, up_bias, down_bias,
             self.cot, self.spots, *ups, *downs],
            scratch=[((width, hidden), BF), ((hidden, width), BF), ((rows, hidden), BF),
                     ((rows, hidden), BF), ((rows, width), F32), ((rows, width), BF),
                     ((rows, width), BF), ((width, rows), BF), ((width, rows), BF),
                     ((hidden // 2, rows), BF), ((hidden // 2, rows), BF), ((rows, width), BF),
                     ((width, rows), F32), ((width, rows), F32), ((rows, width), BF)],
            any_args=8,
            sems=8,
            us=18,
        )
        return g_ff[:4], g_ff[4:]

    def dec_attn_back(self):
        rows, width = self.rows, self.width2
        gi0, gi1, ge0, ge1, self.g_enc, _ = call2(
            partial(dec_attn_back_body, self.kept),
            [((width // 2, 4 * width + 128), BF)] * 2 + [((self.width, width // 2), BF)] * 2
            + [((rows, self.width), F32), ((16, width), F32)],
            [self.place, self.packed2, self.g_att2, self.lse2, self.stream2, self.normed2,
             self.g_middle2, self.d_par, self.d_in, self.embed, self.e_low, self.small2, self.go20,
             self.go21],
            scratch=[((rows, 3 * width), BF), ((width, rows), BF), ((width, rows), F32),
                     ((width, rows), F32), ((width, 128), F32), ((width, 128), F32),
                     ((self.width, rows), F32), ((self.width, rows), F32), ((rows, width), BF)],
            us=16,
        )
        return (gi0, gi1), (ge0, ge1)

    def _feed_back(self, hidden):
        rows, width = self.rows, self.width
        ff = [((width // 2, hidden // 4), BF)] * 4 + [((hidden // 4, width // 2), BF)] * 4
        scratch = [((width, hidden // 2), BF), ((hidden // 2, width), BF), ((rows, width), BF),
                   ((width, rows), BF), ((width, rows), BF), ((hidden // 4, rows), BF),
                   ((hidden // 4, rows), BF), ((rows, width), BF)]
        return ff, scratch

    def enc_feed_back_one(self):
        rows, width, hidden = self.rows, self.width, self.active.shape[1]
        ff, scratch = self._feed_back(hidden)
        (*g_ff, self.total, self.biases1) = call2(
            enc_feed_back_one_body,
            [*ff, ((rows, width), F32), ((1, hidden + width), F32)],
            [self.place, self.g_enc, self.normed_two, self.active, self.slope, *self.e_ups, *self.e_downs],
            scratch=scratch,
            any_args=8,
            sems=8,
            us=15,
        )
        return g_ff[:4], g_ff[4:]

    def enc_feed_back_two(self):
        rows, width, hidden = self.rows, self.width, self.active.shape[1]
        ff, scratch = self._feed_back(hidden)
        (*g_ff, self.g_middle, self.g_att, go0, go1, self.small, biases) = call2(
            enc_feed_back_two_body,
            [*ff, ((rows, width), F32), ((rows, width), BF), ((width, width // 2), BF),
             ((width, width // 2), BF), ((16, width), F32),
             ((1, self.biases1.shape[1] + self.biases2.shape[1]), F32)],
            [self.place, self.g_enc, self.normed_two, self.active, self.slope, self.total, self.biases1,
             self.biases2, self.middle, self.e_par, self.att_t, self.e_out, *self.e_ups, *self.e_downs],
            scratch=[((rows, width), F32), *scratch, ((width, rows), F32), ((width, rows), F32),
                     ((rows, width), BF)],
            any_args=8,
            sems=8,
            us=19,
        )
        return g_ff[:4], g_ff[4:], (go0, go1), biases

    def enc_attn_back(self, cut):
        rows, width = self.rows, self.width
        n = 3 * width // 2 + 128
        ga0, ga1, gb0, gb1, g_tokens, _ = call2(
            partial(enc_attn_back_body, self.kept),
            [((width, cut), BF)] * 2 + [((width, n - cut), BF)] * 2
            + [((self.span, width), F32), ((16, width), F32)],
            [self.place, self.packed, self.g_att, self.lse, self.x, self.normed, self.g_middle,
             self.e_par, self.e_in, self.small, self.spots],
            scratch=[((rows, 3 * width), BF), ((width, rows), BF), ((width, rows), F32),
                     ((width, rows), F32), ((width, 128), F32), ((width, 128), F32)],
            us=20,
        )
        return (ga0, ga1), (gb0, gb1), g_tokens

    def land(self, flights, names):
        for name, value in zip(names, land(flights, [getattr(self, n) for n in names])):
            setattr(self, name, value)


CUT = 640


def whole_weights(params, inproj, outproj, embed=None):
    columns = jnp.pad(params, ((0, 0), (0, 128 - params.shape[1])))
    if embed is None:
        return (jnp.concatenate([inproj, outproj, columns], axis=1),)
    n, m, k = inproj.shape[1] // 2, outproj.shape[1] // 2, embed.shape[1] // 2
    one_a = [inproj[:, :CUT], inproj[:, n : n + CUT]]
    one_b = [inproj[:, CUT:n], columns, inproj[:, n + CUT :], jnp.zeros_like(columns)]
    two = [outproj[:, :m], embed[:, :k], outproj[:, m:], embed[:, k:]]
    return tuple(jnp.concatenate(v, axis=1) for v in (one_a, one_b, two))


def local(
    tokens_in, valid_len, mask_pos,
    encoder_gains, encoder_biases, encoder_inproj, encoder_outproj,
    encoder_up, encoder_upbias, encoder_down, encoder_downbias,
    embed_weight, mask_token,
    decoder_gains, decoder_biases, decoder_inproj, decoder_outproj,
    decoder_up, decoder_upbias, decoder_down, decoder_downbias,
    cotangent,
):
    dp, tr, tc = (lax.axis_index(a) for a in ALL)
    blocks = tuple(lax.axis_size(a) for a in ALL) == (8, 2, 2)
    width, width2 = tokens_in.shape[1], cotangent.shape[1]
    hidden, hidden2 = 2 * encoder_up.shape[1], 2 * decoder_up.shape[1]
    masked = jnp.sum((mask_pos[0] < valid_len[0]).astype(jnp.int32))
    at = (dp, tr, tc, dp) if blocks else (0, 0, 0, 0)
    place = jnp.stack([jnp.int32(v) for v in (*at, tc, valid_len[0] - masked, masked, tr)])

    biases = [encoder_upbias, decoder_upbias, encoder_downbias, decoder_downbias]
    biases = [v.reshape(1, -1).astype(F32) for v in biases]
    up_biases, down_biases = jnp.concatenate(biases[:2], axis=1), jnp.concatenate(biases[2:], axis=1)
    near = Flight(near_swap(encoder_up, encoder_down, decoder_up, decoder_down, down_biases))
    if blocks:
        weights = call(
            pack_body,
            [((48, CUT), BF), ((48, 3 * width // 2 + 128 - CUT), BF), ((48, width // 2 + width2 // 2), BF),
             ((16, 4 * width2 + 128), BF)],
            [encoder_gains.T, encoder_biases.T, encoder_inproj, encoder_outproj, embed_weight,
             decoder_gains.T, decoder_biases.T, mask_token[None], decoder_inproj, decoder_outproj],
        )
        orders = (GATHER_A, GATHER_B, GATHER_C, GATHER_D)
        one_a, one_b, two, three = (Flight(gather_all(v, o)) for v, o in zip(weights, orders))
        land([one_a, one_b, two, three])
        far_bias, up_far, down_far = land([one_a, one_b, near], (up_biases, encoder_up, encoder_down))
        far_bias, up_far = Flight(near_far(far_bias)), Flight(from_far(up_far))
        land([one_a, one_b, two, far_bias])
        land([one_a, one_b, two, three, up_far])
        down_far = Flight(from_far(down_far))
        land([one_a, one_b, up_far])
        sentence = Sentence(place, tokens_in, mask_pos, cotangent)
        one_a, one_b = one_a.result, one_b.result
    else:
        def whole(v):
            return lax.all_gather(v, ALL, axis=0, tiled=True)

        e_par = whole(jnp.concatenate([encoder_gains, encoder_biases], axis=1))
        d_par = whole(jnp.concatenate([decoder_gains, decoder_biases, mask_token[:, None]], axis=1))
        one_a, one_b, two = whole_weights(
            e_par, whole(encoder_inproj), whole(encoder_outproj), whole(embed_weight)
        )
        (three,) = whole_weights(d_par, whole(decoder_inproj), whole(decoder_outproj))
        one_a, one_b = cut_gathered(one_a, GATHER_A, True), cut_gathered(one_b, GATHER_B, True)
        two = cut_gathered(two, GATHER_C, True)
        three = cut_gathered(three, GATHER_D, False)
        far_bias, up_far, down_far = (
            Flight(near_far(up_biases)), Flight(from_far(encoder_up)), Flight(from_far(encoder_down))
        )
        finish(near), finish(far_bias), finish(up_far)
        sentence = Sentence(place, tokens_in, mask_pos, cotangent)

    e_up, e_down, d_up, d_down, far_down_biases = near.result
    far_biases = far_bias.result
    first = tc == 0

    def row_of(own, far, lo, n, switch):
        own, far = own[:, lo : lo + n], far[:, lo : lo + n]
        pair = jnp.concatenate([own, far], axis=1)
        return jnp.where(first, pair, jnp.concatenate([far, own], axis=1)) if switch else pair

    e_upb = row_of(up_biases, far_biases, 0, hidden // 2, False)
    d_upb = row_of(up_biases, far_biases, hidden // 2, hidden2 // 2, False)
    e_downb = row_of(down_biases, far_down_biases, 0, width // 2, True)
    d_downb = row_of(down_biases, far_down_biases, width // 2, width2 // 2, True)

    gathers = [two, three] if blocks else []
    sentence.enc_attn(one_a, one_b)
    sentence.land([*gathers, down_far], ["att_t", "e_par"])
    dec_up, dec_down = lax.optimization_barrier((decoder_up, decoder_down, sentence.e_par))[:2]
    up_far2 = Flight(from_far(dec_up))
    sentence.land([*gathers[:1], down_far], ["att_t", "e_par"])
    two = two.result if blocks else two
    ups, downs = (encoder_up, e_up, *up_far.result), (encoder_down, e_down, *down_far.result)
    sentence.enc_feed(two, ups, downs, e_upb, e_downb)
    sentence.land([*gathers[1:], up_far2], ["e_low", "embed"])
    dec_down, _ = lax.optimization_barrier((dec_down, sentence.e_low))
    down_far2 = Flight(from_far(dec_down))
    sentence.land([*gathers[1:]], ["e_low", "embed"])
    three = three.result if blocks else three
    sentence.dec_attn(three)
    sentence.land([up_far2, down_far2], ["stream2", "att2_t"])
    sentence.land([down_far2], ["stream2", "att2_t"])
    ups = (decoder_up, d_up, *up_far2.result)
    downs = (decoder_down, d_down, *down_far2.result)
    g_ups2, g_downs2 = sentence.dec_feed(ups, downs, d_upb, d_downb)

    if blocks:
        ff2 = [Flight(reduce_feed(g_ups2, False)), Flight(reduce_feed(g_downs2, True))]
        sentence.land(ff2, ["g_middle2", "g_att2"])
        gi2, ge = sentence.dec_attn_back()
        sentence.land(ff2, ["g_enc"])
        att2 = [Flight(scatter_all(gi2, SCATTER_A)), Flight(scatter_all(ge, SCATTER_B))]
        sentence.land(att2, ["g_enc"])
        g_ups, g_downs = sentence.enc_feed_back_one()
        sentence.land(ff2 + att2, ["total", "biases1"])
        ff_a = [Flight(reduce_feed(g_ups, False)), Flight(reduce_feed(g_downs, True))]
        sentence.land(ff_a, ["total", "biases1"])
        g_ups, g_downs, go, biases = sentence.enc_feed_back_two()
        sentence.land(ff2 + att2 + ff_a, ["g_middle", "g_att", "small"])
        ff_b = [Flight(reduce_feed(g_ups, False)), Flight(reduce_feed(g_downs, True))]
        out, biases = Flight(scatter_all(go, SCATTER_C)), Flight(reduce_small(biases))
        sentence.land([*ff_b, out, biases], ["g_middle", "g_att", "small"])
        ga, gb, g_tokens = sentence.enc_attn_back(CUT)
        (g_tokens,) = land([*ff2, *att2, *ff_a, *ff_b, out, biases], (g_tokens,))
        gi = [Flight(scatter_all(ga, SCATTER_A)), Flight(scatter_all(gb, SCATTER_B))]
        halves2 = [*finish(ff2[0]), *finish(ff2[1])]
        halves = [v for f in (*ff_a, *ff_b) for v in finish(f)]
        biases = finish(biases)
    else:
        gi2, ge = sentence.dec_attn_back()
        g_ups, g_downs = sentence.enc_feed_back_one()
        g_ups_b, g_downs_b, go, biases = sentence.enc_feed_back_two()
        ga, gb, g_tokens = sentence.enc_attn_back(CUT)

        def halves_of(v):
            near, far = add(v[0], swap(v[1], "tc")), add(v[2], swap(v[3], "tc"))
            v = lax.psum(add(near, swap(far, "tr")), "dp")
            return [v[: v.shape[0] // 2], v[v.shape[0] // 2 :]]

        halves2 = halves_of(g_ups2) + halves_of(g_downs2)
        halves = [h for v in (g_ups, g_downs, g_ups_b, g_downs_b) for h in halves_of(v)]
        biases = lax.psum(biases, ALL)

    def feed_out(rows, units, parts, arrays):
        outs = [((rows, units), F32), ((units, rows), F32)]
        return call2(partial(out_feed_body, parts), outs, [place, *arrays])

    g_up2, g_down2 = feed_out(width2 // 2, hidden2 // 2, 1, halves2)
    g_up, g_down = feed_out(width // 2, hidden // 2, 2, halves)
    b_up, b_down, b_up2, b_down2 = call2(
        out_bias_body,
        [((1, hidden // 2), F32), ((1, width // 2), F32), ((1, hidden2 // 2), F32), ((1, width2 // 2), F32)],
        [place, biases],
    )
    if blocks:
        n = width // 32
        n2 = width2 // 32
        g_in2, g_out2, g_gains2, g_biases2, g_token = call(
            out_dec_body,
            [((n2, 3 * width2), F32), ((n2, width2), F32), ((2, n2), F32), ((6, n2), F32), ((1, n2), F32)],
            finish(att2[0]),
        )
        (g_embed,) = call(out_halves_body, [((n, width2), F32)], finish(att2[1]))
        (g_out,) = call(out_halves_body, [((n, width), F32)], finish(out))
        g_in, g_gains, g_biases = call(
            out_enc_body,
            [((n, 3 * width), F32), ((2, n), F32), ((5, n), F32)],
            [*finish(gi[0]), *finish(gi[1])],
        )
        g_gains, g_biases, g_gains2, g_biases2 = g_gains.T, g_biases.T, g_gains2.T, g_biases2.T
        g_token = g_token[0]
    else:
        def scatter(v):
            return lax.psum_scatter(v, ALL, scatter_dimension=0, tiled=True).astype(F32)

        a, b = join_scattered(ga, SCATTER_A, True), join_scattered(gb, SCATTER_B, True)
        m = 3 * width // 2 - CUT
        k = m + 128
        g_in = [a[:, :CUT], b[:, :m], a[:, CUT:], b[:, k : k + m]]
        g_in = scatter(jnp.concatenate(g_in, axis=1))
        small = scatter(b[:, m:k])
        g_gains, g_biases = small[:, :2], small[:, 2:7]
        g_out = scatter(join_scattered(go, SCATTER_C, True))
        g_embed = scatter(join_scattered(ge, SCATTER_B, True))
        v = join_scattered(gi2, SCATTER_A, False)
        g_in2, g_out2 = scatter(v[:, : 3 * width2]), scatter(v[:, 3 * width2 : 4 * width2])
        small = scatter(v[:, 4 * width2 :])
        g_gains2, g_biases2, g_token = small[:, :2], small[:, 2:8], small[:, 8]
    return (
        sentence.output, g_tokens, g_gains, g_biases, g_in, g_out, g_up, b_up[0], g_down, b_down[0],
        g_embed, g_token, g_gains2, g_biases2, g_in2, g_out2, g_up2, b_up2[0], g_down2, b_down2[0],
    )


def solution(mesh):
    rows = P(ALL, None)
    attention = (rows, rows, rows, rows)
    feed = (P("tc", "tr"), P("tr"), P("tr", "tc"), P("tc"))
    in_specs = (
        (rows, P(ALL), rows) + attention + feed + (rows, P(ALL)) + attention + feed + (rows,)
    )
    out_specs = (rows, rows) + attention + feed + (rows, P(ALL)) + attention + feed
    return jax.shard_map(local, mesh=mesh, in_specs=in_specs, out_specs=out_specs, check_vma=False)
```

time: 1930 us -> 461 us (0.24)
  waiting for transfers between devices: 882 us -> 140 us
  blocking collectives: 491 us -> 0 us
  matrix products: 205 us -> 0 us
  local copies, waits for them, and re-layouts: 179 us -> 22.3 us
  Pallas kernels: 0 us -> 146 us
  starting transfers between devices: 18.2 us -> 116 us
  other arithmetic: 119 us -> 27.9 us
    reduce_scatter x5 -> x0, waiting for transfers between devices: 464 us -> none  [the longest x1 124 us: local(): lax.psum_scatter(encoder_attn_grads[2], ('dp', 'tr', 'tc'), scatter_dimen...]
    all_gather x6 -> x0, blocking collectives: 241 us -> none  [the longest x1 43.3 us: local(): lax.all_gather(encoder_gains, ('dp', 'tr', 'tc'), axis=0, tiled=True)]
    psum x1 -> x0, waiting for transfers between devices: 234 us -> none  [local(): lax.psum((encoder_feed_grads[0], encoder_feed_grads[1], encoder_feed_grad...]
    dot_general x39 -> x0, matrix products: 205 us -> none  [the longest x18 71.3 us: product(): lax.dot_general(operand, matrix, (((1,), (contract,)), ((), ())), preferr...]
    unnamed x8 -> x0, blocking collectives: 195 us -> none
    pallas_call x0 -> x17, Pallas kernels: none -> 146 us  [the longest x11 135 us: call2(): pl.pallas_call(body, out_shape=[jax.ShapeDtypeStruct(s, d) for s, d in ou...]
    unnamed x245 -> x187, local copies, waits for them, and re-layouts: 153 us -> 11.5 us
    ppermute x0 -> x125, waiting for transfers between devices: none -> 140 us  [swap(): lax.ppermute(v, axis, [(i, i ^ distance) for i in range(lax.axis_size(axi...]
  transfers between devices with their start and end apart: 27 -> 125, of which waited for: 15 -> 48; matrix products, arithmetic and copies ran while one was open for 21% -> 9% of each run, Pallas kernels for 0% -> 24%
where the time goes in v1:
time: 461 us; the launch traced here: 456 us
  Pallas kernels  146 us (32%)
  waiting for transfers between devices  140 us (30%)
  starting transfers between devices  116 us (25%)
  other arithmetic  27.9 us (6%)
  local copies, waits for them, and re-layouts  22.3 us (5%)
    ppermute x125, waiting for transfers between devices, swap(): lax.ppermute(v, axis, [(i, i ^ distance) for i in range(lax.axis_size(axi...  140 us
    pallas_call x11, Pallas kernels, call2(): pl.pallas_call(body, out_shape=[jax.ShapeDtypeStruct(s, d) for s, d in ou...  135 us
    ppermute x125, starting transfers between devices, swap(): lax.ppermute(v, axis, [(i, i ^ distance) for i in range(lax.axis_size(axi...  116 us
    convert_element_type x53, other arithmetic, add(): return (a.astype(F32) + b.astype(F32)).astype(BF)  15.1 us
    unnamed x187, local copies, waits for them, and re-layouts  11.5 us
    pallas_call x6, Pallas kernels, call(): pl.pallas_call(body, out_shape=[jax.ShapeDtypeStruct(s, d) for s, d in ou...  11.2 us
  transfers between devices with their start and end apart: 125, of which 48 were waited for; matrix products, arithmetic and copies ran while one was open for 9% of the time, Pallas kernels for 24%

profile of v1, /device:TPU:0, one launch (start us, length us, event | category | flops | bytes accessed | tf_op | source)
XLA Modules:
  0.0 456.0 jit_solution(837838955880407427)
XLA Ops:
  3.2 4.1 collective-permute-start
  31.0 3.4 collective-permute-start.11
  36.6 23.9 %collective-permute-done.14 = f32[1,2560]{1,0:T(1,128)S(1)} collective-permute-done((f32[1,2560]{1,0:T(1,128)S(1)}, f32[1,2560]{1,0:T(1,128)S(1)}, u32[]{:S(2)}, u32[]{:S(2)}) %collective-permute-start.14) | collective-permute-done | bytes 10272 | tf_op jit(solution)/shard_map/ppermute | solution.py:731
  63.8 3.3 shard_map.365
  67.8 6.9 %collective-permute-done.18 = bf16[32,2176]{1,0:T(8,128)(2,1)S(1)} collective-permute-done((bf16[32,2176]{1,0:T(8,128)(2,1)S(1)}, bf16[32,2176]{1,0:T(8,128)(2,1)S(1)}, u32[]{:S(2)}, u32[]{:S(2)}) %collective-permute-start.18) | collective-permute-done | bytes 139296 | tf_op jit(solution)/shard_map/ppermute | solution.py:731
  74.7 4.6 collective-permute-done.17
  88.6 12.9 %shard_map.367 = (bf16[400,768]{1,0:T(8,128)(2,1)}, bf16[400,2304]{1,0:T(8,128)(2,1)}, bf16[768,400]{1,0:T(8,128)(2,1)}, f32[6,800]{1,0:T(8,128)}, bf16[768,2304]{1,0:T(8,128)(2,1)}, /*index=5*/f32[16,768]{1,0:T(8,128)}) custom-call(s32[8]{0:T(128)} %stack.26.place, bf16[400,768]{1,0:T(8,128)(2,1)} %get-tuple-element.225.x, bf16[384,640]{1,0:T(8,128)(2,1)} %copy-done.52, ...), custom_call_target="tpu_custom_call" | custom-call | flops 12000000000 | bytes 36000000 | tf_op jit(solution)/shard_map/pallas_call | solution.py:867
  101.6 11.0 %collective-permute-done.27.d2 = bf16[1536,384]{1,0:T(8,128)(2,1)} collective-permute-done((bf16[1536,384]{1,0:T(8,128)(2,1)}, bf16[1536,384]{1,0:T(8,128)(2,1)}, u32[]{:S(2)}, u32[]{:S(2)}) %collective-permute-start.27) | collective-permute-done | bytes 1179680 | tf_op jit(solution)/shard_map/ppermute | solution.py:731
  119.0 15.0 %shard_map.368 = (f32[400,768]{1,0:T(8,128)}, bf16[400,768]{1,0:T(8,128)(2,1)}, bf16[400,3072]{1,0:T(8,128)(2,1)}, bf16[400,3072]{1,0:T(8,128)(2,1)}, bf16[400,7...) custom-call(s32[8]{0:T(128)} %stack.26.place, bf16[400,768]{1,0:T(8,128)(2,1)} %get-tuple-element.225.x, ...), custom_call_target="tpu_custom_call" | custom-call | flops 15000000512 | bytes 45000000 | tf_op jit(solution)/shard_map/pallas_call | solution.py:867
  137.5 10.9 %shard_map.369 = (f32[400,512]{1,0:T(8,128)}, bf16[400,512]{1,0:T(8,128)(2,1)}, bf16[400,1536]{1,0:T(8,128)(2,1)}, bf16[512,400]{1,0:T(8,128)(2,1)}, f32[4,1600]...) custom-call(s32[8]{0:T(128)} %stack.26.place, ...), custom_call_target="tpu_custom_call" | custom-call | flops 11000000512 | bytes 33000000 | tf_op jit(solution)/shard_map/pallas_call | solution.py:867
  151.4 18.4 %shard_map.370 = (f32[529,512]{1,0:T(8,128)}, bf16[256,1024]{1,0:T(8,128)(2,1)}, bf16[256,1024]{1,0:T(8,128)(2,1)}, bf16[256,1024]{1,0:T(8,128)(2,1)}, bf16[256,...) custom-call(s32[8]{0:T(128)} %stack.26.place, ...), custom_call_target="tpu_custom_call" | custom-call | flops 17999998976 | bytes 54000000 | tf_op jit(solution)/shard_map/pallas_call | solution.py:867
  174.3 16.5 %shard_map.371 = (bf16[256,2176]{1,0:T(8,128)(2,1)}, bf16[256,2176]{1,0:T(8,128)(2,1)}, bf16[768,256]{1,0:T(8,128)(2,1)}, bf16[768,256]{1,0:T(8,128)(2,1)}, f32[400,768]{1,0:T(8,128)}, /*index=5*/f32[16,512]{1,0:T(8,128)}) custom-call(s32[8]{0:T(128)} %stack.26.place, bf16[400,1536]{1,0:T(8,128)(2,1)} %get-tuple-element.298.packed, ...), custom_call_target="tpu_custom_call" | custom-call | flops 16000000000 | bytes 48000000 | tf_op jit(solution)/shard_map/pallas_call | solution.py:867
  195.9 7.2 %collective-permute-done.44 = bf16[512,256]{1,0:T(8,128)(2,1)S(1)} collective-permute-done((bf16[512,256]{1,0:T(8,128)(2,1)S(1)}, bf16[512,256]{1,0:T(8,128)(2,1)S(1)}, u32[]{:S(2)}, u32[]{:S(2)}) %collective-permute-start.44) | collective-permute-done | bytes 262176 | tf_op jit(solution)/shard_map/ppermute | solution.py:731
  203.1 4.5 collective-permute-done.43
  212.7 14.9 %shard_map.372 = (bf16[384,768]{1,0:T(8,128)(2,1)}, bf16[384,768]{1,0:T(8,128)(2,1)}, bf16[384,768]{1,0:T(8,128)(2,1)}, bf16[384,768]{1,0:T(8,128)(2,1)}, bf16[7...) custom-call(s32[8]{0:T(128)} %stack.26.place, ...), custom_call_target="tpu_custom_call" | custom-call | flops 15000000512 | bytes 45000000 | tf_op jit(solution)/shard_map/pallas_call | solution.py:867
  239.0 19.1 %shard_map.373 = (bf16[384,768]{1,0:T(8,128)(2,1)}, bf16[384,768]{1,0:T(8,128)(2,1)}, bf16[384,768]{1,0:T(8,128)(2,1)}, bf16[384,768]{1,0:T(8,128)(2,1)}, bf16[7...) custom-call(s32[8]{0:T(128)} %stack.26.place, ...), custom_call_target="tpu_custom_call" | custom-call | flops 19000000512 | bytes 57000000 | tf_op jit(solution)/shard_map/pallas_call | solution.py:867
  280.0 19.4 %shard_map.374 = (bf16[768,640]{1,0:T(8,128)(2,1)}, bf16[768,640]{1,0:T(8,128)(2,1)}, bf16[768,640]{1,0:T(8,128)(2,1)}, bf16[768,640]{1,0:T(8,128)(2,1)}, f32[529,768]{1,0:T(8,128)}, /*index=5*/f32[16,768]{1,0:T(8,128)}) custom-call(s32[8]{0:T(128)} %stack.26.place, bf16[400,2304]{1,0:T(8,128)(2,1)} %get-tuple-element.297.packed, ...), custom_call_target="tpu_custom_call" | custom-call | flops 20000000000 | bytes 60000000 | tf_op jit(solution)/shard_map/pallas_call | solution.py:867
  309.0 3.0 collective-permute-start.119
  349.0 2.9 collective-permute-done.98
  353.4 2.9 collective-permute-done.90
  358.6 3.3 collective-permute-done.93
  363.4 3.9 collective-permute-done.91.theirs
  373.0 4.7 %collective-permute-done.99 = bf16[96,384]{1,0:T(8,128)(2,1)S(1)} collective-permute-done((bf16[96,384]{1,0:T(8,128)(2,1)S(1)}, bf16[96,384]{1,0:T(8,128)(2,1)S(1)}, u32[]{:S(2)}, u32[]{:S(2)}) %collective-permute-start.99) | collective-permute-done | bytes 73760 | tf_op jit(solution)/shard_map/ppermute | solution.py:731
  379.1 4.4 collective-permute-done.94
  396.3 5.8 %collective-permute-done.104 = bf16[48,768]{1,0:T(8,128)(2,1)S(1)} collective-permute-done((bf16[48,768]{1,0:T(8,128)(2,1)S(1)}, bf16[48,768]{1,0:T(8,128)(2,1)S(1)}, u32[]{:S(2)}, u32[]{:S(2)}) %collective-permute-start.104) | collective-permute-done | bytes 73760 | tf_op jit(solution)/shard_map/ppermute | solution.py:731
  402.2 5.6 %collective-permute-done.110 = bf16[96,384]{1,0:T(8,128)(2,1)S(1)} collective-permute-done((bf16[96,384]{1,0:T(8,128)(2,1)S(1)}, bf16[96,384]{1,0:T(8,128)(2,1)S(1)}, u32[]{:S(2)}, u32[]{:S(2)}) %collective-permute-start.110) | collective-permute-done | bytes 73760 | tf_op jit(solution)/shard_map/ppermute | solution.py:731
  408.1 5.3 %collective-permute-done.105 = bf16[48,768]{1,0:T(8,128)(2,1)S(1)} collective-permute-done((bf16[48,768]{1,0:T(8,128)(2,1)S(1)}, bf16[48,768]{1,0:T(8,128)(2,1)S(1)}, u32[]{:S(2)}, u32[]{:S(2)}) %collective-permute-start.105) | collective-permute-done | bytes 73760 | tf_op jit(solution)/shard_map/ppermute | solution.py:731
  424.0 3.1 collective-permute-done.112
  427.2 4.6 %collective-permute-done.81 = bf16[192,640]{1,0:T(8,128)(2,1)S(1)} collective-permute-done((bf16[192,640]{1,0:T(8,128)(2,1)S(1)}, bf16[192,640]{1,0:T(8,128)(2,1)S(1)}, u32[]{:S(2)}, u32[]{:S(2)}) %collective-permute-start.81) | collective-permute-done | bytes 245792 | tf_op jit(solution)/shard_map/ppermute | solution.py:731
  434.1 4.7 %collective-permute-done.82 = bf16[96,640]{1,0:T(8,128)(2,1)S(1)} collective-permute-done((bf16[96,640]{1,0:T(8,128)(2,1)S(1)}, bf16[96,640]{1,0:T(8,128)(2,1)S(1)}, u32[]{:S(2)}, u32[]{:S(2)}) %collective-permute-start.82) | collective-permute-done | bytes 122912 | tf_op jit(solution)/shard_map/ppermute | solution.py:731
  439.6 4.1 collective-permute-done.87
  449.5 4.1 shard_map.377
  (564 shorter events, 193.9 us)
Async XLA Ops:
  0.7 28.6 %collective-permute-start.6 = (bf16[384,1536]{1,0:T(8,128)(2,1)}, bf16[384,1536]{1,0:T(8,128)(2,1)}, u32[]{:S(2)}, u32[]{:S(2)}) collective-permute-start(bf16[384,1536]{1,0:T(8,128)(2,1)} %u0.7), channel_id=1, source_target_pairs={{0,1},{1,0},{2,3},{3,2},{4,5},{5,4},{6,7},{7,6},{8,9},{9,8},{10,11... | collective-permute-start | bytes 3538952 | tf_op jit(solution)/shard_map/ppermute | solution.py:731
  1.2 28.1 %collective-permute-start.7 = (bf16[1536,384]{1,0:T(8,128)(2,1)}, bf16[1536,384]{1,0:T(8,128)(2,1)}, u32[]{:S(2)}, u32[]{:S(2)}) collective-permute-start(bf16[1536,384]{1,0:T(8,128)(2,1)} %d0.7), channel_id=1, source_target_pairs={{0,1},{1,0},{2,3},{3,2},{4,5},{5,4},{6,7},{7,6},{8,9},{9,8},{10,11... | collective-permute-start | bytes 3538952 | tf_op jit(solution)/shard_map/ppermute | solution.py:731
  29.4 31.2 %collective-permute-start.12 = (bf16[192,640]{1,0:T(8,128)(2,1)S(1)}, bf16[192,640]{1,0:T(8,128)(2,1)S(1)}, u32[]{:S(2)}, u32[]{:S(2)}) collective-permute-start(bf16[192,640]{1,0:T(8,128)(2,1)S(1)} %pad_maximum_fusion.8), channel_id=1, source_target_pairs={{0,4},{4,0},{8,12},{12,8},{16,20},{20,16},{24,28},{28,24},{1,5},{5... | collective-permute-start | bytes 737288 | tf_op jit(solution)/shard_map/ppermute | solution.py:731
  31.0 29.6 %collective-permute-start.11 = (bf16[192,640]{1,0:T(8,128)(2,1)S(1)}, bf16[192,640]{1,0:T(8,128)(2,1)S(1)}, u32[]{:S(2)}, u32[]{:S(2)}) collective-permute-start(bf16[192,640]{1,0:T(8,128)(2,1)S(1)} %pad_maximum_fusion.7), channel_id=1, source_target_pairs={{0,8},{4,12},{8,0},{12,4},{16,24},{20,28},{24,16},{28,20},{1,9},{5... | collective-permute-start | bytes 737288 | tf_op jit(solution)/shard_map/ppermute | solution.py:731
  34.4 44.9 %collective-permute-start.19 = (bf16[384,1536]{1,0:T(8,128)(2,1)S(1)}, bf16[384,1536]{1,0:T(8,128)(2,1)}, u32[]{:S(2)}, u32[]{:S(2)}) collective-permute-start(bf16[384,1536]{1,0:T(8,128)(2,1)S(1)} %copy-done.58), channel_id=1, source_target_pairs={{0,2},{2,0},{1,3},{3,1},{4,6},{6,4},{5,7},{7,5},{8,10},{10,8},{9,1... | collective-permute-start | bytes 3538952 | tf_op jit(solution)/shard_map/ppermute | solution.py:731
  36.0 24.6 %collective-permute-start.14 = (f32[1,2560]{1,0:T(1,128)S(1)}, f32[1,2560]{1,0:T(1,128)S(1)}, u32[]{:S(2)}, u32[]{:S(2)}) collective-permute-start(f32[1,2560]{1,0:T(1,128)S(1)} %pad_maximum_fusion.21), channel_id=1, source_target_pairs={{0,2},{2,0},{1,3},{3,1},{4,6},{6,4},{5,7},{7,5},{8,10},{10,8},{9,1... | collective-permute-start | bytes 30728 | tf_op jit(solution)/shard_map/ppermute | solution.py:731
  84.1 28.5 %collective-permute-start.27 = (bf16[1536,384]{1,0:T(8,128)(2,1)}, bf16[1536,384]{1,0:T(8,128)(2,1)}, u32[]{:S(2)}, u32[]{:S(2)}) collective-permute-start(bf16[1536,384]{1,0:T(8,128)(2,1)} %d0.7), channel_id=1, source_target_pairs={{0,2},{2,0},{1,3},{3,1},{4,6},{6,4},{5,7},{7,5},{8,10},{10,8},{9,1... | collective-permute-start | bytes 3538952 | tf_op jit(solution)/shard_map/ppermute | solution.py:731
  85.7 26.9 %collective-permute-start.26 = (bf16[64,2176]{1,0:T(8,128)(2,1)S(1)}, bf16[64,2176]{1,0:T(8,128)(2,1)S(1)}, u32[]{:S(2)}, u32[]{:S(2)}) collective-permute-start(bf16[64,2176]{1,0:T(8,128)(2,1)S(1)} %pad_maximum_fusion.4), channel_id=1, source_target_pairs={{0,4},{4,0},{8,12},{12,8},{16,20},{20,16},{24,28},{28,24},{1,5},{5... | collective-permute-start | bytes 835592 | tf_op jit(solution)/shard_map/ppermute | solution.py:731
  86.3 26.3 %collective-permute-start.25 = (bf16[384,640]{1,0:T(8,128)(2,1)S(1)}, bf16[384,640]{1,0:T(8,128)(2,1)}, u32[]{:S(2)}, u32[]{:S(2)}) collective-permute-start(bf16[384,640]{1,0:T(8,128)(2,1)S(1)} %constant_dynamic-update-slice_fusion.8.s0), channel_id=1, source_target_pairs={{0,4},{4,0},{8,12},{12,8},{16,20},{20,16},{24,28},{28,24},{1,5},{5... | collective-permute-start | bytes 1474568 | tf_op jit(solution)/shard_map/ppermute | solution.py:731
  114.4 21.4 %collective-permute-start.33 = (bf16[128,2176]{1,0:T(8,128)(2,1)S(1)}, bf16[128,2176]{1,0:T(8,128)(2,1)S(1)}, u32[]{:S(2)}, u32[]{:S(2)}) collective-permute-start(bf16[128,2176]{1,0:T(8,128)(2,1)S(1)} %constant_dynamic-update-slice_fusion.12.s0), channel_id=1, source_target_pairs={{0,1},{1,0},{2,3},{3,2},{4,5},{5,4},{6,7},{7,6},{8,9},{9,8},{10,11... | collective-permute-start | bytes 1671176 | tf_op jit(solution)/shard_map/ppermute | solution.py:731
  207.9 19.8 %collective-permute-start.47 = (bf16[128,1024]{1,0:T(8,128)(2,1)S(1)}, bf16[128,1024]{1,0:T(8,128)(2,1)S(1)}, u32[]{:S(2)}, u32[]{:S(2)}) collective-permute-start(bf16[128,1024]{1,0:T(8,128)(2,1)S(1)} %slice.346), channel_id=1, source_target_pairs={{0,4},{4,0},{8,12},{12,8},{16,20},{20,16},{24,28},{28,24},{1,5},{5... | collective-permute-start | bytes 786440 | tf_op jit(solution)/shard_map/ppermute | solution.py:731
  231.8 26.3 %collective-permute-start.55 = (bf16[64,1024]{1,0:T(8,128)(2,1)}, bf16[64,1024]{1,0:T(8,128)(2,1)S(1)}, u32[]{:S(2)}, u32[]{:S(2)}) collective-permute-start(bf16[64,1024]{1,0:T(8,128)(2,1)} %slice.351), channel_id=1, source_target_pairs={{0,8},{4,12},{8,0},{12,4},{16,24},{20,28},{24,16},{28,20},{1,9},{5... | collective-permute-start | bytes 393224 | tf_op jit(solution)/shard_map/ppermute | solution.py:731
  233.3 24.9 %collective-permute-start.57 = (bf16[64,2176]{1,0:T(8,128)(2,1)}, bf16[64,2176]{1,0:T(8,128)(2,1)S(1)}, u32[]{:S(2)}, u32[]{:S(2)}) collective-permute-start(bf16[64,2176]{1,0:T(8,128)(2,1)} %slice.355), channel_id=1, source_target_pairs={{0,4},{4,0},{8,12},{12,8},{16,20},{20,16},{24,28},{28,24},{1,5},{5... | collective-permute-start | bytes 835592 | tf_op jit(solution)/shard_map/ppermute | solution.py:731
  234.0 24.7 %collective-permute-start.61 = (bf16[384,384]{1,0:T(8,128)(2,1)S(1)}, bf16[384,384]{1,0:T(8,128)(2,1)S(1)}, u32[]{:S(2)}, u32[]{:S(2)}) collective-permute-start(bf16[384,384]{1,0:T(8,128)(2,1)S(1)} %slice.359), channel_id=1, source_target_pairs={{0,4},{4,0},{8,12},{12,8},{16,20},{20,16},{24,28},{28,24},{1,5},{5... | collective-permute-start | bytes 884744 | tf_op jit(solution)/shard_map/ppermute | solution.py:731
  236.0 22.8 %collective-permute-start.60 = (bf16[384,384]{1,0:T(8,128)(2,1)S(1)}, bf16[384,384]{1,0:T(8,128)(2,1)S(1)}, u32[]{:S(2)}, u32[]{:S(2)}) collective-permute-start(bf16[384,384]{1,0:T(8,128)(2,1)S(1)} %slice.358), channel_id=1, source_target_pairs={{0,4},{4,0},{8,12},{12,8},{16,20},{20,16},{24,28},{28,24},{1,5},{5... | collective-permute-start | bytes 884744 | tf_op jit(solution)/shard_map/ppermute | solution.py:731
  237.7 21.6 %collective-permute-start.59 = (bf16[384,768]{1,0:T(8,128)(2,1)S(1)}, bf16[384,768]{1,0:T(8,128)(2,1)S(1)}, u32[]{:S(2)}, u32[]{:S(2)}) collective-permute-start(bf16[384,768]{1,0:T(8,128)(2,1)S(1)} %add_convert_fusion.13), channel_id=1, source_target_pairs={{0,2},{2,0},{1,3},{3,1},{4,6},{6,4},{5,7},{7,5},{8,10},{10,8},{9,1... | collective-permute-start | bytes 1769480 | tf_op jit(solution)/shard_map/ppermute | solution.py:731
  274.3 25.2 %collective-permute-start.77 = (bf16[384,384]{1,0:T(8,128)(2,1)S(1)}, bf16[384,384]{1,0:T(8,128)(2,1)S(1)}, u32[]{:S(2)}, u32[]{:S(2)}) collective-permute-start(bf16[384,384]{1,0:T(8,128)(2,1)S(1)} %slice.372), channel_id=1, source_target_pairs={{0,8},{4,12},{8,0},{12,4},{16,24},{20,28},{24,16},{28,20},{1,9},{5... | collective-permute-start | bytes 884744 | tf_op jit(solution)/shard_map/ppermute | solution.py:731
  274.9 24.7 %collective-permute-start.76 = (bf16[384,384]{1,0:T(8,128)(2,1)S(1)}, bf16[384,384]{1,0:T(8,128)(2,1)}, u32[]{:S(2)}, u32[]{:S(2)}) collective-permute-start(bf16[384,384]{1,0:T(8,128)(2,1)S(1)} %slice.371), channel_id=1, source_target_pairs={{0,4},{4,0},{8,12},{12,8},{16,20},{20,16},{24,28},{28,24},{1,5},{5... | collective-permute-start | bytes 884744 | tf_op jit(solution)/shard_map/ppermute | solution.py:731
  276.1 24.0 %collective-permute-start.75 = (bf16[384,384]{1,0:T(8,128)(2,1)}, bf16[384,384]{1,0:T(8,128)(2,1)}, u32[]{:S(2)}, u32[]{:S(2)}) collective-permute-start(bf16[384,384]{1,0:T(8,128)(2,1)} %slice.370), channel_id=1, source_target_pairs={{0,4},{4,0},{8,12},{12,8},{16,20},{20,16},{24,28},{28,24},{1,5},{5... | collective-permute-start | bytes 884744 | tf_op jit(solution)/shard_map/ppermute | solution.py:731
  277.8 22.2 %collective-permute-start.73 = (bf16[384,384]{1,0:T(8,128)(2,1)}, bf16[384,384]{1,0:T(8,128)(2,1)}, u32[]{:S(2)}, u32[]{:S(2)}) collective-permute-start(bf16[384,384]{1,0:T(8,128)(2,1)} %add_convert_fusion.31), channel_id=1, source_target_pairs={{0,2},{2,0},{1,3},{3,1},{4,6},{6,4},{5,7},{7,5},{8,10},{10,8},{9,1... | collective-permute-start | bytes 884744 | tf_op jit(solution)/shard_map/ppermute | solution.py:731
  279.2 20.8 %collective-permute-start.74 = (bf16[384,768]{1,0:T(8,128)(2,1)S(1)}, bf16[384,768]{1,0:T(8,128)(2,1)S(1)}, u32[]{:S(2)}, u32[]{:S(2)}) collective-permute-start(bf16[384,768]{1,0:T(8,128)(2,1)S(1)} %add_convert_fusion.8), channel_id=1, source_target_pairs={{0,2},{2,0},{1,3},{3,1},{4,6},{6,4},{5,7},{7,5},{8,10},{10,8},{9,1... | collective-permute-start | bytes 1769480 | tf_op jit(solution)/shard_map/ppermute | solution.py:731
  299.5 83.9 %collective-permute-start.79 = (bf16[768,640]{1,0:T(8,128)(2,1)}, bf16[768,640]{1,0:T(8,128)(2,1)}, u32[]{:S(2)}, u32[]{:S(2)}) collective-permute-start(bf16[768,640]{1,0:T(8,128)(2,1)} %get-tuple-element.397), channel_id=1, source_target_pairs={{0,1},{1,0},{2,3},{3,2},{4,5},{5,4},{6,7},{7,6},{8,9},{9,8},{10,11... | collective-permute-start | bytes 2949128 | tf_op jit(solution)/shard_map/ppermute | solution.py:731
  299.6 87.5 %collective-permute-start.84 = (bf16[768,640]{1,0:T(8,128)(2,1)}, bf16[768,640]{1,0:T(8,128)(2,1)S(1)}, u32[]{:S(2)}, u32[]{:S(2)}) collective-permute-start(bf16[768,640]{1,0:T(8,128)(2,1)} %get-tuple-element.399), channel_id=1, source_target_pairs={{0,1},{1,0},{2,3},{3,2},{4,5},{5,4},{6,7},{7,6},{8,9},{9,8},{10,11... | collective-permute-start | bytes 2949128 | tf_op jit(solution)/shard_map/ppermute | solution.py:731
  335.6 36.2 %collective-permute-start.102 = (bf16[192,768]{1,0:T(8,128)(2,1)}, bf16[192,768]{1,0:T(8,128)(2,1)S(1)}, u32[]{:S(2)}, u32[]{:S(2)}) collective-permute-start(bf16[192,768]{1,0:T(8,128)(2,1)} %slice.407), channel_id=1, source_target_pairs={{0,4},{4,0},{8,12},{12,8},{16,20},{20,16},{24,28},{28,24},{1,5},{5... | collective-permute-start | bytes 884744 | tf_op jit(solution)/shard_map/ppermute | solution.py:731
  342.9 26.6 %collective-permute-start.108 = (bf16[384,384]{1,0:T(8,128)(2,1)S(1)}, bf16[384,384]{1,0:T(8,128)(2,1)S(1)}, u32[]{:S(2)}, u32[]{:S(2)}) collective-permute-start(bf16[384,384]{1,0:T(8,128)(2,1)S(1)} %copy-done.23), channel_id=1, source_target_pairs={{0,2},{2,0},{1,3},{3,1},{4,6},{6,4},{5,7},{7,5},{8,10},{10,8},{9,1... | collective-permute-start | bytes 884744 | tf_op jit(solution)/shard_map/ppermute | solution.py:731
  367.2 46.2 %collective-permute-start.124 = (bf16[512,256]{1,0:T(8,128)(2,1)}, bf16[512,256]{1,0:T(8,128)(2,1)}, u32[]{:S(2)}, u32[]{:S(2)}) collective-permute-start(bf16[512,256]{1,0:T(8,128)(2,1)} %pad_maximum_fusion.6.refs_2_), channel_id=1, source_target_pairs={{0,4},{4,0},{8,12},{12,8},{16,20},{20,16},{24,28},{28,24},{1,5},{5... | collective-permute-start | bytes 786440 | tf_op jit(solution)/shard_map/ppermute | solution.py:731
  369.6 43.9 %collective-permute-start.121 = (bf16[128,1024]{1,0:T(8,128)(2,1)}, bf16[128,1024]{1,0:T(8,128)(2,1)S(1)}, u32[]{:S(2)}, u32[]{:S(2)}) collective-permute-start(bf16[128,1024]{1,0:T(8,128)(2,1)} %pad_maximum_fusion.5.refs_0_), channel_id=1, source_target_pairs={{0,4},{4,0},{8,12},{12,8},{16,20},{20,16},{24,28},{28,24},{1,5},{5... | collective-permute-start | bytes 786440 | tf_op jit(solution)/shard_map/ppermute | solution.py:731
  390.9 30.6 %collective-permute-start.80 = (bf16[384,640]{1,0:T(8,128)(2,1)S(1)}, bf16[384,640]{1,0:T(8,128)(2,1)S(1)}, u32[]{:S(2)}, u32[]{:S(2)}) collective-permute-start(bf16[384,640]{1,0:T(8,128)(2,1)S(1)} %slice.374), channel_id=1, source_target_pairs={{0,2},{2,0},{1,3},{3,1},{4,6},{6,4},{5,7},{7,5},{8,10},{10,8},{9,1... | collective-permute-start | bytes 1474568 | tf_op jit(solution)/shard_map/ppermute | solution.py:731
  392.5 30.6 %collective-permute-start.85 = (bf16[384,640]{1,0:T(8,128)(2,1)S(1)}, bf16[384,640]{1,0:T(8,128)(2,1)S(1)}, u32[]{:S(2)}, u32[]{:S(2)}) collective-permute-start(bf16[384,640]{1,0:T(8,128)(2,1)S(1)} %slice.382), channel_id=1, source_target_pairs={{0,4},{4,0},{8,12},{12,8},{16,20},{20,16},{24,28},{28,24},{1,5},{5... | collective-permute-start | bytes 1474568 | tf_op jit(solution)/shard_map/ppermute | solution.py:731
  413.4 31.6 %collective-permute-start.96 = (bf16[192,768]{1,0:T(8,128)(2,1)S(1)}, bf16[192,768]{1,0:T(8,128)(2,1)S(1)}, u32[]{:S(2)}, u32[]{:S(2)}) collective-permute-start(bf16[192,768]{1,0:T(8,128)(2,1)S(1)} %pad_maximum_fusion.refs_0_), channel_id=1, source_target_pairs={{0,4},{4,0},{8,12},{12,8},{16,20},{20,16},{24,28},{28,24},{1,5},{5... | collective-permute-start | bytes 884744 | tf_op jit(solution)/shard_map/ppermute | solution.py:731
  419.3 28.0 %collective-permute-start.101 = (bf16[384,384]{1,0:T(8,128)(2,1)S(1)}, bf16[384,384]{1,0:T(8,128)(2,1)S(1)}, u32[]{:S(2)}, u32[]{:S(2)}) collective-permute-start(bf16[384,384]{1,0:T(8,128)(2,1)S(1)} %pad_maximum_fusion.1.refs_2_), channel_id=1, source_target_pairs={{0,4},{4,0},{8,12},{12,8},{16,20},{20,16},{24,28},{28,24},{1,5},{5... | collective-permute-start | bytes 884744 | tf_op jit(solution)/shard_map/ppermute | solution.py:731
  421.5 25.8 %collective-permute-start.107 = (bf16[192,768]{1,0:T(8,128)(2,1)S(1)}, bf16[192,768]{1,0:T(8,128)(2,1)S(1)}, u32[]{:S(2)}, u32[]{:S(2)}) collective-permute-start(bf16[192,768]{1,0:T(8,128)(2,1)S(1)} %pad_maximum_fusion.2.refs_4_), channel_id=1, source_target_pairs={{0,4},{4,0},{8,12},{12,8},{16,20},{20,16},{24,28},{28,24},{1,5},{5... | collective-permute-start | bytes 884744 | tf_op jit(solution)/shard_map/ppermute | solution.py:731
  (181 other events, 1425.0 us)

commit v2 on v1

v2 whole, which is shorter than its diff:
```python
import math
from functools import partial

import jax
import jax.numpy as jnp
from jax import lax
from jax.experimental import pallas as pl
from jax.experimental.pallas import tpu as pltpu
from jax.sharding import PartitionSpec as P

HEADS = 12
HEADS2 = 16
ALL = ("dp", "tr", "tc")
EPS = 1e-06
MASKED = -1e30
LOG2E = math.log2(math.e)
F32 = jnp.float32
BF = jnp.bfloat16
SPARE_BYTES = 12 * 1024 * 1024
LAST = 0.01
WHOLE_BYTES = 58 * 1024 * 1024


def dot_nn(a, b):
    return lax.dot_general(a, b, (((1,), (0,)), ((), ())), preferred_element_type=F32)


def dot_nt(a, b):
    return lax.dot_general(a, b, (((1,), (1,)), ((), ())), preferred_element_type=F32)


def cost(us):
    return pl.CostEstimate(flops=int(us * 1e9), bytes_accessed=int(us * 3e6), transcendentals=0)


def vmem(arrays):
    total = sum(math.prod(s) * jnp.dtype(d).itemsize for s, d in arrays)
    return pltpu.CompilerParams(vmem_limit_bytes=SPARE_BYTES + total)


SAVES = []


def save(ref, columns=None):
    for entry in SAVES[-1]:
        if entry["buffer"] is ref:
            source, target = ref, entry["out"]
            if columns is not None:
                source, target = source.at[:, columns], target.at[:, columns]
            pltpu.make_async_copy(source, target, entry["sem"]).start()
            entry["started"] = True


def call(body, outs, args, scratch=(), smem=0, hbm_args=0, sems=0, keep=(), us=2, alone=False):
    count = len(args) - smem - hbm_args
    specs = [pl.BlockSpec(memory_space=pltpu.SMEM)] * smem
    specs += [pl.BlockSpec(memory_space=pltpu.VMEM)] * count
    specs += [pl.BlockSpec(memory_space=pltpu.HBM)] * hbm_args
    buffers = [outs[k] for k in keep]
    shapes = [pltpu.VMEM(s, d) for s, d in [*buffers, *scratch]]
    shapes += [pltpu.SemaphoreType.DMA((max(n, 1),)) for n in (len(keep), sems)]

    def kernel(*refs):
        ins, rest = refs[: len(args)], refs[len(args) :]
        results, rest = list(rest[: len(outs)]), rest[len(outs) :]
        own, keep_sems, own_sems = rest[:-2], rest[-2], rest[-1]
        entries = []
        for n, k in enumerate(keep):
            entries.append({"buffer": own[n], "out": results[k], "sem": keep_sems.at[n], "started": False})
            results[k] = own[n]
        SAVES.append(entries)
        body(*ins, *results, *own[len(keep) :], *((own_sems,) if sems else ()))
        SAVES.pop()
        for entry in entries:
            copy = pltpu.make_async_copy(entry["buffer"], entry["out"], entry["sem"])
            if not entry["started"]:
                copy.start()
        for entry in entries:
            pltpu.make_async_copy(entry["buffer"], entry["out"], entry["sem"]).wait()

    spaces = [pltpu.HBM if k in keep else pltpu.VMEM for k in range(len(outs))]
    return pl.pallas_call(
        kernel,
        out_shape=[jax.ShapeDtypeStruct(s, d) for s, d in outs],
        in_specs=specs,
        out_specs=[pl.BlockSpec(memory_space=space) for space in spaces],
        scratch_shapes=shapes,
        compiler_params=pltpu.CompilerParams(vmem_limit_bytes=WHOLE_BYTES) if alone else vmem([*buffers, *scratch]),
        cost_estimate=cost(us),
    )(*args)


def norm_parts(v):
    center = v - jnp.mean(v, axis=-1, keepdims=True)
    r = lax.rsqrt(jnp.mean(center * center, axis=-1, keepdims=True) + EPS)
    return center * r, r


def norm_back(u, r, gain, y):
    e = y * gain
    back = r * (e - jnp.mean(e, axis=-1, keepdims=True) - u * jnp.mean(e * u, axis=-1, keepdims=True))
    return back, jnp.sum(y * u, axis=0, keepdims=True), jnp.sum(y, axis=0, keepdims=True)


def split3(v):
    hi = v.astype(BF)
    rest = v - hi.astype(F32)
    mid = rest.astype(BF)
    return hi, mid, (rest - mid.astype(F32)).astype(BF)


def head_masks(head_size):
    lane = lax.broadcasted_iota(jnp.int32, (1, 128), 1) // head_size
    return [(lane == h).astype(F32).astype(BF) for h in range(128 // head_size)]


def stack_heads(rows, masks):
    return jnp.concatenate([rows * m for m in masks], axis=0)


def prep_body(kept, mp_col, mp_row, tokens, cot, x_out, cot_out, place_out):
    rows, span = x_out.shape[0], tokens.shape[0]
    wide = lax.broadcasted_iota(jnp.int32, (mp_col.shape[0], span), 1)
    below = jnp.sum((mp_col[...] < wide).astype(F32), axis=0, keepdims=True)
    here = jnp.sum((mp_col[...] == wide).astype(F32), axis=0, keepdims=True)
    place = jnp.where(here > 0, kept, wide[:1] - below.astype(jnp.int32))
    pick = lax.broadcasted_iota(jnp.int32, (rows, span), 0) == place
    pick_f = pick.astype(F32)
    cot_out[...] = dot_nn(pick_f.astype(BF), cot[...])
    keep = lax.broadcasted_iota(jnp.int32, (rows, span), 0) < kept
    x_out[...] = dot_nn(jnp.where(keep, pick_f, 0.0).astype(BF), tokens[...]).astype(BF)
    tall = lax.broadcasted_iota(jnp.int32, (span, mp_row.shape[1]), 0)
    below_t = jnp.sum((mp_row[...] < tall).astype(F32), axis=1, keepdims=True)
    here_t = jnp.sum((mp_row[...] == tall).astype(F32), axis=1, keepdims=True)
    place_out[...] = jnp.where(here_t > 0, kept, tall[:, :1] - below_t.astype(jnp.int32))


def spread_back(place, rows, limit):
    at = lax.broadcasted_iota(jnp.int32, (place.shape[0], rows), 1)
    return jnp.where(at < limit, (at == place).astype(F32), 0.0).astype(BF)


def key_bias(lens, kept, rows, with_mask_row):
    at = lax.broadcasted_iota(jnp.int32, (rows, 1), 0)
    bias = jnp.where(at < lens[0], 0.0, MASKED)
    if with_mask_row:
        count = jnp.full((rows, 1), lens[1], jnp.int32).astype(F32)
        bias = jnp.where(at == kept, jnp.log(count) * LOG2E, bias)
    return bias


def attention_forward(packed, att_t, lse, bias, head_size):
    width = packed.shape[1] // 3
    rows = packed.shape[0]
    masks = head_masks(head_size)
    scale = head_size**-0.5 * LOG2E

    def group(g, carry):
        at = pl.multiple_of(g * 128, 128)
        q = packed[:, pl.ds(at, 128)]
        k = packed[:, pl.ds(width + at, 128)]
        v_t = packed[:, pl.ds(2 * width + at, 128)].T
        scores = dot_nt(k, stack_heads(q, masks)) * scale + bias
        peak = jnp.max(scores, axis=0, keepdims=True)
        weights = jnp.exp2(scores - peak)
        total = jnp.sum(weights, axis=0, keepdims=True)
        out = dot_nn(v_t, weights.astype(BF)) * (1.0 / total)
        for h in range(len(masks)):
            block = out[h * head_size : (h + 1) * head_size, h * rows : (h + 1) * rows]
            att_t[pl.ds(at + h * head_size, head_size), :] = block.astype(BF)
        lse[pl.ds(g, 1), :] = peak + jnp.log(total) * LOG2E
        return carry

    lax.fori_loop(0, width // 128, group, 0)


def attention_backward(packed, g_att, lse, g_packed, gq_t, bias, head_size):
    width = packed.shape[1] // 3
    rows = packed.shape[0]
    masks = head_masks(head_size)
    scale = head_size**-0.5

    def group(g, carry):
        at = pl.multiple_of(g * 128, 128)
        q = packed[:, pl.ds(at, 128)]
        k = packed[:, pl.ds(width + at, 128)]
        v = packed[:, pl.ds(2 * width + at, 128)]
        q_s = stack_heads(q, masks)
        g_s = stack_heads(g_att[:, pl.ds(at, 128)], masks)
        scores = dot_nt(k, q_s) * (scale * LOG2E) + bias
        probs = jnp.exp2(scores - lse[pl.ds(g, 1), :])
        g_v = dot_nn(probs.astype(BF), g_s)
        g_probs = dot_nt(v, g_s)
        delta = jnp.sum(g_probs * probs, axis=0, keepdims=True)
        g_scores = (probs * (g_probs - delta)).astype(BF)
        g_k = dot_nn(g_scores, q_s) * scale
        out = dot_nn(k.T, g_scores) * scale
        for h in range(len(masks)):
            block = out[h * head_size : (h + 1) * head_size, h * rows : (h + 1) * rows]
            gq_t[pl.ds(at + h * head_size, head_size), :] = block.astype(BF)
        g_packed[:, pl.ds(width + at, 128)] = g_k.astype(BF)
        g_packed[:, pl.ds(2 * width + at, 128)] = g_v.astype(BF)
        return carry

    lax.fori_loop(0, width // 128, group, 0)
    g_packed[:, :width] = gq_t[...].T


def project_in(stream, params, inproj, normed_out, packed_out):
    u, r = norm_parts(stream)
    normed = (u * params[0:1, :] + params[2:3, :]).astype(BF)
    normed_out[...] = normed
    save(normed_out)
    width = stream.shape[1]
    step = 256
    for part in range(3):
        for at in range(0, width, step):
            lo = part * width + at
            value = dot_nn(normed, inproj[:, lo : lo + step])
            if part == 0:
                value = value + params[3:4, at : at + step]
            if part == 2:
                value = value + params[4:5, at : at + step]
            packed_out[:, lo : lo + step] = value.astype(BF)
    save(packed_out)


GATHER_A = (("tr", 1), ("dp", 4), ("dp", 2), ("dp", 1))
GATHER_B = (("tr", 1), ("dp", 4), ("dp", 1), ("dp", 2))
GATHER_C = (("tr", 1), ("dp", 4), ("dp", 2), ("dp", 1))
GATHER_D = (("tr", 1), ("dp", 4), ("dp", 1), ("dp", 2))
SCATTER_A = (("dp", 1), ("tr", 1), ("dp", 2), ("dp", 4))
SCATTER_B = (("tr", 1), ("dp", 1), ("dp", 2), ("dp", 4))
FEED = (("dp", 1), ("dp", 2), ("dp", 4))


def differences(order, bits):
    dp = tr = 0
    for (axis, distance), bit in zip(order, bits):
        if axis == "dp":
            dp = dp + distance * bit
        else:
            tr = tr + bit
    return dp, tr


def gathered_block(order, j, last):
    return differences(order, (j & 1, (j >> 1) & 1, (j >> 2) & 1, last))


def scattered_block(order, m):
    return differences(order, (m >> 3, (m >> 2) & 1, (m >> 1) & 1, m & 1))


def feed_block(m):
    return differences(FEED, (m >> 2, (m >> 1) & 1, m & 1))[0]


def place_rows(place, order, sources, block, put):
    first = place[2] == 0
    for x in range(2):
        own_ref, oth_ref = sources[x], sources[2 + x]
        count = own_ref.shape[0] // block

        def one(j, carry, own_ref=own_ref, oth_ref=oth_ref, x=x):
            dp, tr = gathered_block(order, j, x)
            chip = (place[0] ^ dp) * 2 + (place[1] ^ tr)
            at = pl.multiple_of(j * block, block)
            own = own_ref[pl.ds(at, block), :].astype(F32)
            oth = oth_ref[pl.ds(at, block), :].astype(F32)
            put(chip, jnp.where(first, own, oth), jnp.where(first, oth, own))
            return carry

        lax.fori_loop(0, count, one, 0)


def place_halves(place, order, sources, cuts):
    block = sources[0].shape[0] // 8
    half = block // 2

    def put(chip, low, high):
        at = pl.multiple_of(chip * block, block)
        top = jnp.concatenate([low[:half], high[:half]], axis=0).astype(BF)
        bottom = jnp.concatenate([low[half:], high[half:]], axis=0).astype(BF)
        lo = 0
        for target, first, width, shift in cuts:
            target[pl.ds(at, block), first : first + width] = top[:, lo : lo + width]
            if shift is not None:
                right = first + shift
                target[pl.ds(at, block), right : right + width] = bottom[:, lo : lo + width]
            lo += width

    place_rows(place, order, sources, block, put)


def place_whole(place, order, sources, cuts):
    block = sources[0].shape[0] // 8

    def put(chip, low, high):
        at = pl.multiple_of(chip * 2 * block, 2 * block)
        both = jnp.concatenate([low, high], axis=0).astype(BF)
        lo = 0
        for target, width in cuts:
            target[pl.ds(at, 2 * block), :] = both[:, lo : lo + width]
            lo += width

    place_rows(place, order, sources, block, put)


def param_rows(columns):
    return columns[...].astype(F32).T[:16]


def reorder_rows(place, order, source, target):
    block = source.shape[0] // 32
    for core in range(2):
        for m in range(16):
            dp, tr = scattered_block(order, m)
            device = ((place[0] ^ dp) * 2 + (place[1] ^ tr)) * 2 + (place[2] ^ core)
            at = pl.multiple_of(device * block, 8)
            to = (core * 16 + m) * block
            target[to : to + block, :] = source[pl.ds(at, block), :]


def write_halves(ordered, columns, outs, first=0, count=None):
    half_rows = ordered.shape[0] // 2
    block = half_rows // 16
    width = columns.shape[1] // 2
    count = width if count is None else count
    step = max(n for n in (384, 320, 256) if count % n == 0) if count != 640 else 640
    for core in range(2):
        rows = ordered[core * half_rows : (core + 1) * half_rows, :].astype(BF)
        for at in range(first, first + count, step):
            left = dot_nn(rows, columns[:, at : at + step])
            right = dot_nn(rows, columns[:, width + at : width + at + step])
            for m in range(16):
                both = [left[m * block : (m + 1) * block], right[m * block : (m + 1) * block]]
                outs[core][m * 2 * block : (m + 1) * 2 * block, at - first : at - first + step] = (
                    jnp.concatenate(both, axis=0).astype(BF)
                )


def write_whole(ordered, columns, outs, lo):
    half_rows = ordered.shape[0] // 2
    width = columns.shape[1]
    for core in range(2):
        rows = ordered[core * half_rows : (core + 1) * half_rows, :].astype(BF)
        for at in range(0, width, 256):
            outs[core][:, lo + at : lo + at + 256] = dot_nn(rows, columns[:, at : at + 256]).astype(BF)


def small_columns(small):
    table = jnp.concatenate([small[...], jnp.zeros((112, small.shape[1]), F32)], axis=0)
    return table.T


def pack_body(
    e_gains, e_biases, e_in, e_out, embed, d_gains, d_biases, token, d_in, d_out, one, two, three
):
    def columns(parts):
        total, lo = 0.0, 0
        for part in parts:
            count, rows = part.shape
            spot = lax.broadcasted_iota(jnp.int32, (count, 128), 1)
            want = lax.broadcasted_iota(jnp.int32, (count, 128), 0) + lo
            table = (spot == want).astype(F32).astype(BF)
            total = total + lax.dot_general(
                part[...], table, (((0,), (0,)), ((), ())), preferred_element_type=F32
            )
            lo += count
        return total

    e_par = columns([e_gains, e_biases])

    def halves(v):
        v = v[...].astype(F32)
        width = v.shape[1] // 2
        return jnp.concatenate([v[:, :width], v[:, width:]], axis=0).astype(BF)

    n = e_in.shape[1] // 2
    one[:, :n] = halves(e_in)
    one[:, n:] = jnp.concatenate([e_par, jnp.zeros_like(e_par)], axis=0).astype(BF)
    n = e_out.shape[1] // 2
    two[:, :n] = halves(e_out)
    two[:, n:] = halves(embed)
    n = d_in.shape[1]
    m = n + d_out.shape[1]
    three[:, :n] = d_in[...]
    three[:, n:m] = d_out[...]
    three[:, m:] = columns([d_gains, d_biases, token]).astype(BF)


def enc_attn_body(
    kept, place, x, s0, s1, s2, s3, r0, r1, r2, r3,
    normed, packed, att_t, lse, inproj, par_t, par_c,
):
    width = x.shape[1]
    n, shift = s0.shape[1], 3 * width // 2
    place_halves(place, GATHER_A, (s0, s1, s2, s3), ((inproj, 0, n, shift),))
    place_halves(
        place, GATHER_B, (r0, r1, r2, r3), ((inproj, n, shift - n, shift), (par_c, 0, 128, None))
    )
    save(inproj)
    par_t[...] = param_rows(par_c)
    project_in(x[...].astype(F32), par_t, inproj, normed, packed)
    bias = key_bias((place[5], place[6]), kept, x.shape[0], False)
    attention_forward(packed, att_t, lse, bias, width // HEADS)


def dec_attn_body(
    kept, place, e_low, embed, s0, s1, s2, s3,
    stream, normed, packed, att_t, lse, inproj, outproj, params, par_c,
):
    rows = e_low.shape[0]
    width = stream.shape[1]
    place_whole(
        place, GATHER_D, (s0, s1, s2, s3), ((inproj, 3 * width), (outproj, width), (par_c, 128))
    )
    save(inproj)
    save(outproj)
    params[...] = param_rows(par_c)
    embedded = dot_nn(e_low[...], embed[...]) + params[7:8, :]
    at = lax.broadcasted_iota(jnp.int32, (rows, 1), 0)
    decoded = jnp.where(at < kept, embedded, params[8:9, :])
    stream[...] = decoded
    save(stream)
    project_in(decoded, params, inproj, normed, packed)
    bias = key_bias((place[5], place[6]), kept, rows, True)
    attention_forward(packed, att_t, lse, bias, width // HEADS2)


def pack_feed_body(up, up_bias, down, down_bias, out):
    rows, width = up.shape[0], down.shape[1]
    out[:rows, :] = up[...]
    for at in range(0, up.shape[1], width):
        out[rows : 2 * rows, at : at + width] = down[at : at + width, :]
    row = lax.broadcasted_iota(jnp.int32, (16, up.shape[1]), 0)
    value = jnp.where(row == 0, up_bias[...].astype(F32), 0.0)
    out[2 * rows :, :] = value.astype(BF)
    row = lax.broadcasted_iota(jnp.int32, (16, width), 0)
    value = jnp.where(row == 1, down_bias[...].astype(F32), value[:, :width])
    out[2 * rows :, :width] = value.astype(BF)


def load_feed(place, gathered, up, down, sems, part=0, biases=None):
    copies = []
    half = up.shape[0] // 2
    units = up.shape[1] // 2
    block = gathered.shape[0] // 4

    def start(source, target):
        copies.append(pltpu.make_async_copy(source, target, sems.at[len(copies)]))
        copies[-1].start()

    for tr in range(2):
        for core in range(2):
            base = ((place[7] ^ tr) * 2 + core) * block

            def rows(at, count, base=base):
                return pl.ds(pl.multiple_of(base + at, 16), count)

            columns = pl.ds(tr * units, units)
            start(
                gathered.at[rows(0, half), pl.ds(part * units, units)],
                up.at[pl.ds(core * half, half), columns],
            )
            for at in range(0, units, half):
                start(
                    gathered.at[rows(half, half), pl.ds(part * units + at, half)],
                    down.at[pl.ds(tr * units + at, half), pl.ds(core * half, half)],
                )
            if biases is not None:
                start(gathered.at[rows(2 * half, 16), :], biases.at[2 * tr + core])
    return copies


def bias_rows(biases, half):
    up = jnp.concatenate([biases[0, 0:1, :], biases[2, 0:1, :]], axis=1)
    down = jnp.concatenate([biases[0, 1:2, :half], biases[1, 1:2, :half]], axis=1)
    return up.astype(F32), down.astype(F32)


def middle_of(stream, att_t, outproj, params):
    return stream + dot_nn(att_t[...].T, outproj[...]) + params[5:6, :]


def feed_forward(normed_two, up, up_bias, down, active_out, slope_out, total, step):
    hidden_units = up.shape[1]
    total[...] = jnp.zeros_like(total)

    def chunk(c, carry):
        at = pl.multiple_of(c * step, step)
        hidden = dot_nn(normed_two, up[:, pl.ds(at, step)]) + up_bias[:, pl.ds(at, step)]
        phi = 0.5 * (1.0 + lax.erf(hidden * math.sqrt(0.5)))
        bell = jnp.exp2(hidden * hidden * (-0.5 * LOG2E)) * (1.0 / math.sqrt(2 * math.pi))
        active = (hidden * phi).astype(BF)
        active_out[:, pl.ds(at, step)] = active
        slope_out[:, pl.ds(at, step)] = (phi + hidden * bell).astype(BF)
        save(active_out, pl.ds(at, step))
        save(slope_out, pl.ds(at, step))
        total[...] += dot_nn(active, down[pl.ds(at, step), :])
        return carry

    lax.fori_loop(0, hidden_units // step, chunk, 0)


def order_feed(place, source, target):
    block = source.shape[0] // 16
    for core in range(2):
        for m in range(8):
            at = ((place[4] ^ core) * 8 + (place[3] ^ feed_block(m))) * block
            to = (core * 8 + m) * block
            target[to : to + block, :] = source[pl.ds(pl.multiple_of(at, block), block), :]


def feed_backward(
    place, part, parts, g_result, normed_two, active, slope, up, down,
    g_ups, g_downs, g_upbias, g_normed, step, rows_t, ordered_n, ordered_g,
):
    width = normed_two.shape[1]
    count = up.shape[1] // 2
    units = count * parts
    half = width // 2
    rows_t[...] = normed_two[...].T
    order_feed(place, rows_t, ordered_n)
    rows_t[...] = g_result[...].T
    order_feed(place, rows_t, ordered_g)
    for tr in range(2):
        base = tr * units + part * count
        out_base = pl.multiple_of((place[7] ^ tr) * units + part * count, 128)

        def chunk(c, carry, tr=tr, base=base, out_base=out_base):
            at = pl.multiple_of(c * step, step)
            here = pl.ds(pl.multiple_of(tr * count + at, 128), step)
            g_active = dot_nt(g_result[...], down[here, :]).astype(BF).astype(F32)
            there = pl.ds(pl.multiple_of(base + at, 128), step)
            g_hidden = (slope[:, there].astype(F32) * g_active).astype(BF)
            g_upbias[:, pl.ds(pl.multiple_of(out_base + at, 128), step)] = jnp.sum(
                g_hidden.astype(F32), axis=0, keepdims=True
            )
            g_normed[...] += dot_nt(g_hidden, up[:, here])
            g_up = dot_nn(ordered_n[...], g_hidden).astype(BF)
            g_down = dot_nn(ordered_g[...], active[:, there]).astype(BF)
            for core in range(2):
                g_ups[2 * tr + core][:, pl.ds(at, step)] = g_up[core * half : (core + 1) * half]
                g_downs[2 * tr + core][:, pl.ds(at, step)] = g_down[core * half : (core + 1) * half]
            return carry

        lax.fori_loop(0, count // step, chunk, 0)


def after_feed_backward(
    place, order, g_out, g_normed, middle, params, att_t, outproj, g_middle, g_att, small, att_f, att_o
):
    u, r = norm_parts(middle)
    y = g_normed.astype(BF).astype(F32)
    back, g_gain, g_shift = norm_back(u, r, params[1:2, :], y)
    grad = g_out + back
    g_middle[...] = grad
    branch = grad.astype(BF)
    att_f[...] = att_t[...].astype(F32)
    reorder_rows(place, order, att_f, att_o)
    g_att[...] = dot_nt(branch, outproj[...]).astype(BF)
    small[1:2, :] = g_gain
    small[5:6, :] = jnp.sum(branch.astype(F32), axis=0, keepdims=True)
    small[6:7, :] = g_shift
    return branch


def enc_feed_body(
    place, x, att_t, s0, s1, s2, s3, params, weights,
    middle, normed_two, active, slope, e_low, outproj, embed,
    up, down, total, biases, up_bias, sems,
):
    copies = load_feed(place, weights, up, down, sems, 0, biases)
    width = x.shape[1]
    n, m = width // 2, embed.shape[1] // 2
    place_halves(place, GATHER_C, (s0, s1, s2, s3), ((outproj, 0, n, n), (embed, 0, m, m)))
    mid = middle_of(x[...].astype(F32), att_t, outproj, params)
    middle[...] = mid
    u, r = norm_parts(mid)
    n2 = (u * params[1:2, :] + params[6:7, :]).astype(BF)
    normed_two[...] = n2
    for ref in (middle, normed_two, outproj, embed):
        save(ref)
    for copy in copies:
        copy.wait()
    up_bias[...], down_bias = bias_rows(biases, width // 2)
    feed_forward(n2, up, up_bias, down, active, slope, total, 512)
    result = (total[...] + down_bias).astype(BF)
    e_low[...] = (middle[...] + result.astype(F32)).astype(BF)


def dec_feed_body(
    kept, place, stream, att_t, outproj, params, cot, weights,
    out, gu0, gu1, gu2, gu3, gd0, gd1, gd2, gd3, g_middle, g_att, go0, go1, small, g_biases,
    up, down, active, slope, total, n2_s, g_res, rows_t, ordered_n, ordered_g,
    att_f, att_o, branch_s, biases, up_bias, sems,
):
    copies = load_feed(place, weights, up, down, sems, 0, biases)
    mid = middle_of(stream[...], att_t, outproj, params)
    u, r = norm_parts(mid)
    n2 = (u * params[1:2, :] + params[6:7, :]).astype(BF)
    n2_s[...] = n2
    for copy in copies:
        copy.wait()
    up_bias[...], down_bias = bias_rows(biases, up.shape[0] // 2)
    feed_forward(n2, up, up_bias, down, active, slope, total, 512)
    result = (total[...] + down_bias).astype(BF)
    out[...] = mid + result.astype(F32)
    save(out)
    g_out = cot[...]
    g_res[...] = g_out.astype(BF)
    small[...] = jnp.zeros_like(small)
    units = up.shape[1]
    g_biases[:, units:] = jnp.sum(g_res[...].astype(F32), axis=0, keepdims=True)
    total[...] = jnp.zeros_like(total)
    feed_backward(
        place, 0, 1, g_res, n2_s, active, slope, up, down, (gu0, gu1, gu2, gu3), (gd0, gd1, gd2, gd3),
        g_biases, total, 512, rows_t, ordered_n, ordered_g,
    )
    branch = after_feed_backward(
        place, SCATTER_B, g_out, total[...], mid, params, att_t, outproj, g_middle, g_att, small,
        att_f, att_o,
    )
    branch_s[...] = branch
    write_whole(att_o, branch_s, (go0, go1), 0)


def enc_feed_back_one_body(
    place, g_enc, normed_two, active, slope, weights,
    gu0, gu1, gu2, gu3, gd0, gd1, gd2, gd3, total, biases, up, down, g_res, rows_t, ordered_n, ordered_g, sems,
):
    copies = load_feed(place, weights, up, down, sems)
    g_res[...] = g_enc[...].astype(BF)
    total[...] = jnp.zeros_like(total)
    biases[:, 2 * up.shape[1] :] = jnp.sum(g_res[...].astype(F32), axis=0, keepdims=True)
    for copy in copies:
        copy.wait()
    feed_backward(
        place, 0, 2, g_res, normed_two, active, slope, up, down, (gu0, gu1, gu2, gu3),
        (gd0, gd1, gd2, gd3), biases, total, 384, rows_t, ordered_n, ordered_g,
    )


def enc_feed_back_two_body(
    place, g_enc, normed_two, active, slope, total_in, biases_in, biases_dec, middle, params, att_t,
    outproj, weights,
    gu0, gu1, gu2, gu3, gd0, gd1, gd2, gd3, g_middle, g_att, go0, go1, small, biases,
    total, up, down, g_res, rows_t, ordered_n, ordered_g, att_f, att_o, branch_s, sems,
):
    copies = load_feed(place, weights, up, down, sems, 1)
    g_res[...] = g_enc[...].astype(BF)
    total[...] = total_in[...]
    count = biases_in.shape[1]
    biases[:, :count] = biases_in[...]
    biases[:, count:] = biases_dec[...]
    small[...] = jnp.zeros_like(small)
    for copy in copies:
        copy.wait()
    feed_backward(
        place, 1, 2, g_res, normed_two, active, slope, up, down, (gu0, gu1, gu2, gu3),
        (gd0, gd1, gd2, gd3), biases, total, 384, rows_t, ordered_n, ordered_g,
    )
    branch = after_feed_backward(
        place, SCATTER_A, g_enc[...], total[...], middle[...], params, att_t, outproj, g_middle,
        g_att, small, att_f, att_o,
    )
    branch_s[...] = branch
    write_halves(att_o, branch_s, (go0, go1))


def project_back(
    place, order, stream, normed, g_packed, g_middle, params, inproj, small, first, rows_f, rows_o
):
    width = stream.shape[1]
    rows_f[...] = normed[...].astype(F32).T
    reorder_rows(place, order, rows_f, rows_o)
    g_normed = dot_nt(g_packed[...], inproj[...])
    u, r = norm_parts(stream)
    back, g_gain, g_shift = norm_back(u, r, params[0:1, :], g_normed)
    small[...] = first[...]
    small[0:1, :] = g_gain
    small[2:3, :] = g_shift
    small[3:4, :] = jnp.sum(g_packed[:, :width].astype(F32), axis=0, keepdims=True)
    small[4:5, :] = jnp.sum(g_packed[:, 2 * width :].astype(F32), axis=0, keepdims=True)
    return g_middle[...] + back


def dec_attn_back_body(
    kept, place, packed, g_att, lse, stream, normed, g_middle, params, inproj, embed, e_low, first,
    go0, go1, ga0, ga1, gb0, gb1, g_enc, small, g_packed, gq_t, rows_f, rows_o, cols, cols_o,
    emb_f, emb_o, g_emb,
):
    rows = stream.shape[0]
    width = stream.shape[1]
    bias = key_bias((place[5], place[6]), kept, rows, True)
    attention_backward(packed, g_att, lse, g_packed, gq_t, bias, width // HEADS2)
    g_stream = project_back(
        place, SCATTER_A, stream[...], normed, g_packed, g_middle, params, inproj, small, first,
        rows_f, rows_o,
    )
    write_whole(rows_o, g_packed, (ga0, ga1), 0)
    at = lax.broadcasted_iota(jnp.int32, (rows, 1), 0)
    small[8:9, :] = jnp.sum(jnp.where(at == kept, g_stream, 0.0), axis=0, keepdims=True)
    g_embedded = jnp.where(at < kept, g_stream, 0.0).astype(BF)
    small[7:8, :] = jnp.sum(g_embedded.astype(F32), axis=0, keepdims=True)
    g_emb[...] = g_embedded
    g_enc[...] = dot_nt(g_embedded, embed[...])
    emb_f[...] = e_low[...].astype(F32).T
    reorder_rows(place, SCATTER_B, emb_f, emb_o)
    cols[...] = small_columns(small)
    reorder_rows(place, SCATTER_B, cols, cols_o)
    n = cols_o.shape[0] // 2
    half = emb_o.shape[0] // 2
    block, part = half // 16, g_emb.shape[1] // 2
    unit = n // 16
    for core, (gb, go) in enumerate(((gb0, go0), (gb1, go1))):
        gb[:, :width] = go[...]
        gb[:, width : width + 128] = cols_o[core * n : (core + 1) * n, :].astype(BF)
        rows_e = emb_o[core * half : (core + 1) * half, :].astype(BF)
        left, right = dot_nn(rows_e, g_emb[:, :part]), dot_nn(rows_e, g_emb[:, part:])
        for m in range(16):
            both = [left[m * block : (m + 1) * block], right[m * block : (m + 1) * block]]
            both = jnp.concatenate(both, axis=0).astype(BF)
            for k in range(2 * block // unit):
                lo = width + 128 + k * part
                gb[m * unit : (m + 1) * unit, lo : lo + part] = both[k * unit : (k + 1) * unit]


def enc_attn_back_one_body(kept, place, packed, g_att, lse, g_packed, gq_t):
    bias = key_bias((place[5], place[6]), kept, packed.shape[0], False)
    attention_backward(packed, g_att, lse, g_packed, gq_t, bias, g_att.shape[1] // HEADS)


def enc_attn_back_two_body(
    place, g_packed, x, normed, g_middle, params, inproj, first, go0, go1,
    ga0, ga1, gb0, gb1, g_stream, small, rows_f, rows_o, cols, cols_o,
):
    width = x.shape[1]
    g_stream[...] = project_back(
        place, SCATTER_A, x[...].astype(F32), normed, g_packed, g_middle, params, inproj, small, first,
        rows_f, rows_o,
    )
    m = gb0.shape[1] - 128
    n = 3 * width // 2 - m
    write_halves(rows_o, g_packed, (ga0, ga1), 0, n)
    reorder_rows(place, SCATTER_B, rows_f, rows_o)
    write_halves(rows_o, g_packed, (gb0, gb1), n, m)
    cols[...] = small_columns(small)
    reorder_rows(place, SCATTER_B, cols, cols_o)
    count = cols_o.shape[0] // 2
    block = count // 16
    for core, (a, b, go) in enumerate(((ga0, gb0, go0), (ga1, gb1, go1))):
        a[:, n:] = go[...]
        for k in range(16):
            part = cols_o[core * count + k * block : core * count + (k + 1) * block, :]
            both = jnp.concatenate([part, jnp.zeros_like(part)], axis=0).astype(BF)
            b[k * 2 * block : (k + 1) * 2 * block, m:] = both


def spread_body(kept, spots, out, g_stream, output, g_tokens):
    rows = out.shape[0]
    for limit, source, target in ((kept + 1, out, output), (kept, g_stream, g_tokens)):
        pick = spread_back(spots[...], rows, limit)
        hi, mid, low = split3(source[...])
        target[...] = dot_nn(pick, hi) + dot_nn(pick, mid) + dot_nn(pick, low)


def out_feed_body(part, *refs):
    place, halves = refs[0], refs[1:3]
    g_up, g_down, up, turned, down, sems = refs[-6:]
    units = up.shape[1]
    for x, ref in enumerate(halves):
        block = ref.shape[1] // 2
        for m in range(4):
            at = pl.multiple_of((place[3] ^ feed_block(4 * x + m)) * block, block)
            rows = ref[m].astype(F32)
            up[pl.ds(at, block), :] = rows[:block]
            turned[pl.ds(at, block), :] = rows[block:]
    here = pl.ds(part * units, units)
    first = pltpu.make_async_copy(up, g_up.at[:, here], sems.at[0])
    first.start()
    down[...] = turned[...].T
    second = pltpu.make_async_copy(down, g_down.at[here, :], sems.at[1])
    second.start()
    first.wait()
    second.wait()


def out_dec_body(mine, theirs, g_in, g_out, g_gains, g_biases, g_token, g_embed):
    total = mine[...].astype(F32) + theirs[...].astype(F32)
    n = g_in.shape[1]
    m = n + g_out.shape[1]
    g_in[...] = total[:, :n]
    g_out[...] = total[:, n:m]
    rows = total[:, m : m + 128].T
    g_gains[...] = rows[0:2]
    g_biases[...] = rows[2:8]
    g_token[...] = rows[8:9]
    half = g_embed.shape[1] // 2
    units = [total[:, m + 128 + k * half : m + 128 + (k + 1) * half] for k in range(3)]
    both = jnp.concatenate(units, axis=0)
    count = both.shape[0] // 2
    g_embed[:, :half] = both[:count]
    g_embed[:, half:] = both[count:]


def out_enc_body(mine, theirs, g_in, g_out, g_gains, g_biases):
    total = mine[...].astype(F32) + theirs[...].astype(F32)
    n, width, half = g_in.shape[0], g_in.shape[1] // 2, g_out.shape[1] // 2
    first = CUT_BACK
    a, b = total[:, : first + half], total[:, first + half :]
    rest = width - first
    g_in[:, :first] = a[:n, :first]
    g_in[:, first:width] = b[:n, :rest]
    g_in[:, width : width + first] = a[n:, :first]
    g_in[:, width + first :] = b[n:, :rest]
    g_out[:, :half] = a[:n, first:]
    g_out[:, half:] = a[n:, first:]
    rows = b[:n, rest:].T
    g_gains[...] = rows[0:2]
    g_biases[...] = rows[2:7]


def out_bias_body(place, biases, up1, down1, up2, down2):
    lo = 0
    for out, at in ((up1, place[7]), (down1, place[4]), (up2, place[7]), (down2, place[4])):
        n = out.shape[1]
        out[...] = biases[:, pl.ds(pl.multiple_of(lo + at * n, 128), n)]
        lo += 2 * n


def swap(v, axis, distance=1):
    return lax.ppermute(v, axis, [(i, i ^ distance) for i in range(lax.axis_size(axis))])


def add(a, b):
    return (a.astype(F32) + b.astype(F32)).astype(BF)


class Flight:
    def __init__(self, steps):
        self.steps, self.result = steps, None
        self.waits = next(steps)

    def land(self, arrays):
        try:
            self.waits = self.steps.send(arrays)
        except StopIteration as end:
            self.waits, self.result = None, end.value


def land(flights, outs=()):
    flights = [f for f in flights if f.waits is not None]
    outs, arrays = lax.optimization_barrier((outs, [f.waits for f in flights]))
    for flight, landed in zip(flights, arrays):
        flight.land(landed)
    return outs


def finish(flight):
    while flight.waits is not None:
        flight.land(flight.waits)
    return flight.result


def gather_all(v, order):
    for axis, distance in order[:-1]:
        (got,) = yield (swap(v, axis, distance),)
        v = jnp.concatenate([v, got], axis=0)
    (last,) = yield (swap(v, *order[-1]),)
    a, b = yield (swap(v, "tc"), swap(last, "tc"))
    return v, last, a, b


def gather_lanes(v, cut):
    for axis, distance in GATHER_A[:2]:
        (got,) = yield (swap(v, axis, distance),)
        v = jnp.concatenate([v, got], axis=0)
    a, b = v[:, :cut], v[:, cut:]
    one, two = yield (swap(a, *GATHER_A[2]), swap(b, *GATHER_B[2]))
    a, b = jnp.concatenate([a, one], axis=0), jnp.concatenate([b, two], axis=0)
    one, two = yield (swap(a, *GATHER_A[3]), swap(b, *GATHER_B[3]))
    got = yield (swap(a, "tc"), swap(one, "tc"), swap(b, "tc"), swap(two, "tc"))
    return (a, one, *got[:2]), (b, two, *got[2:])


def scatter_lanes(one, two, small=None):
    extra = [] if small is None else [small]
    a, b, *got = yield (swap(one[1], "tc"), swap(two[1], "tc"), *(swap(v, "tc") for v in extra))
    a, b = add(one[0], a), add(two[0], b)
    for k in range(2):
        extra = [v + w for v, w in zip(extra, got)]
        half = a.shape[0] // 2
        one, two, *got = yield (
            swap(a[half:], *SCATTER_A[k]), swap(b[half:], *SCATTER_B[k]), *(swap(v, *SCATTER_A[k]) for v in extra)
        )
        a, b = add(a[:half], one), add(b[:half], two)
    v = jnp.concatenate([a, b], axis=1)
    for k in (2, 3):
        extra = [v + w for v, w in zip(extra, got)]
        half = v.shape[0] // 2
        one, *got = yield (swap(v[half:], *SCATTER_A[k]), *(swap(w, *SCATTER_A[k]) for w in extra))
        v = (v[:half], one) if k == 3 else add(v[:half], one)
    return v, [v + w for v, w in zip(extra, got)]


def reduce_feed(ups, downs):
    got = yield tuple(swap(v, "tc") for v in (ups[1], ups[3], downs[1], downs[3]))
    up, up_far, down, down_far = (
        add(v, w) for v, w in zip((ups[0], ups[2], downs[0], downs[2]), got)
    )
    half = up.shape[0] // 2
    one, two, three = yield (
        swap(up_far, "tr"), swap(down[half:], "dp", 1), swap(down_far[half:], "dp", 1)
    )
    up, down, down_far = add(up, one), add(down[:half], two), add(down_far[:half], three)
    one, two = yield (swap(up[half:], "dp", 1), swap(down_far, "tr"))
    up, down = add(up[:half], one), add(down, two)
    shape = (4, half // 4, up.shape[1])
    v = jnp.concatenate([up.reshape(shape), down.reshape(shape)], axis=1)
    for distance in (2, 4):
        half = v.shape[0] // 2
        (got,) = yield (swap(v[half:], "dp", distance),)
        v = add(v[:half], got)
    for distance in (4, 2):
        (got,) = yield (swap(v, "dp", distance),)
        v = jnp.concatenate([v, got], axis=0)
    (got,) = yield (swap(v, "dp", 1),)
    return v, got


def chip_axes(order):
    return [{("dp", 4): 0, ("dp", 2): 1, ("dp", 1): 2, ("tr", 1): 3}[step] for step in order]


def cut_gathered(whole, order, halves):
    rows, width = whole.shape
    if halves:
        v = whole.reshape(32, rows // 32, 2, width // 2).transpose(0, 2, 1, 3)
        v = v.reshape(32, rows // 16, width // 2)
    else:
        v = whole.reshape(32, rows // 32, width)
    v = v.reshape((2, 2, 2, 2, 2) + v.shape[1:])
    first = chip_axes(order)
    v = v.transpose(first[3], 4, first[2], first[1], first[0], 5, 6)
    v = v.reshape(2, 2, -1, v.shape[-1])
    return v[0, 0], v[1, 0], v[0, 1], v[1, 1]


def join_scattered(pair, order, halves):
    v = jnp.stack(pair)
    v = v.reshape(2, 2, 2, 2, 2, v.shape[1] // 16, v.shape[2])
    first = chip_axes(order)
    v = v.transpose(*(1 + first.index(k) for k in range(4)), 0, 5, 6)
    v = v.reshape(32, v.shape[5], v.shape[6])
    if halves:
        v = v.reshape(32, 2, v.shape[1] // 2, v.shape[2]).transpose(0, 2, 1, 3)
        v = v.reshape(32, v.shape[1], -1)
    return v.reshape(-1, v.shape[-1])


def call2(body, outs, args, **more):
    return call(body, outs, args, smem=1, **more)


class Sentence:
    def __init__(self, place, tokens, mask_pos, cot):
        self.place = place
        span, self.width = tokens.shape
        masks = mask_pos.shape[1]
        self.span, self.kept = span, span - masks
        self.rows = -(-(self.kept + 1) // 16) * 16
        self.width2 = cot.shape[1]
        self.x, self.cot, self.spots = call(
            partial(prep_body, self.kept),
            [((self.rows, self.width), BF), ((self.rows, self.width2), F32), ((span, 1), jnp.int32)],
            [mask_pos.reshape(masks, 1), mask_pos, tokens, cot],
            us=3,
        )

    def enc_attn(self, one_a, one_b):
        rows, width = self.rows, self.width
        self.normed, self.packed, self.att_t, self.lse, self.e_in, self.e_par = call2(
            partial(enc_attn_body, self.kept),
            [((rows, width), BF), ((rows, 3 * width), BF), ((width, rows), BF),
             ((width // 128, rows * (128 * HEADS // width)), F32), ((width, 3 * width), BF),
             ((16, width), F32)],
            [self.place, self.x, *one_a, *one_b],
            scratch=[((width, 128), BF)],
            keep=(0, 1, 3, 4),
            alone=True,
            us=12,
        )

    def enc_feed(self, two, weights):
        rows, width, units = self.rows, self.width, weights.shape[1]
        hidden = 2 * units
        self.e_weights = weights
        self.middle, self.normed_two, self.active, self.slope, self.e_low, self.e_out, self.embed = call2(
            enc_feed_body,
            [((rows, width), F32), ((rows, width), BF), ((rows, hidden), BF), ((rows, hidden), BF),
             ((rows, width), BF), ((width, width), BF), ((width, self.width2), BF)],
            [self.place, self.x, self.att_t, *two, self.e_par, weights],
            scratch=[((width, hidden), BF), ((hidden, width), BF), ((rows, width), F32),
                     ((4, 16, units), BF), ((1, hidden), F32)],
            hbm_args=1,
            sems=8 + 8 * units // width,
            keep=(0, 1, 2, 3, 5),
            alone=True,
            us=15,
        )

    def dec_attn(self, three):
        rows, width = self.rows, self.width2
        (self.stream2, self.normed2, self.packed2, self.att2_t, self.lse2, self.d_in, self.d_out,
         self.d_par) = call2(
            partial(dec_attn_body, self.kept),
            [((rows, width), F32), ((rows, width), BF), ((rows, 3 * width), BF), ((width, rows), BF),
             ((width // 128, rows * (128 * HEADS2 // width)), F32), ((width, 3 * width), BF),
             ((width, width), BF), ((16, width), F32)],
            [self.place, self.e_low, self.embed, *three],
            scratch=[((width, 128), BF)],
            keep=(1, 2, 4, 5),
            alone=True,
            us=11,
        )

    def dec_feed(self, weights):
        rows, width, units = self.rows, self.width2, weights.shape[1]
        hidden = 2 * units
        (self.out, *g_ff, self.g_middle2, self.g_att2, self.go20, self.go21, self.small2,
         self.biases2) = call2(
            partial(dec_feed_body, self.kept),
            [((rows, width), F32), *[((width // 2, hidden // 2), BF)] * 8, ((rows, width), F32),
             ((rows, width), BF), ((width // 2, width), BF), ((width // 2, width), BF),
             ((16, width), F32), ((1, hidden + width), F32)],
            [self.place, self.stream2, self.att2_t, self.d_out, self.d_par, self.cot, weights],
            scratch=[((width, hidden), BF), ((hidden, width), BF), ((rows, hidden), BF),
                     ((rows, hidden), BF), ((rows, width), F32), ((rows, width), BF),
                     ((rows, width), BF), ((width, rows), BF), ((width, rows), BF),
                     ((width, rows), BF), ((width, rows), F32), ((width, rows), F32),
                     ((rows, width), BF), ((4, 16, units), BF), ((1, hidden), F32)],
            hbm_args=1,
            sems=8 + 8 * units // width,
            keep=(0,),
            us=16,
        )
        self.ff2 = (g_ff[:4], g_ff[4:])

    def dec_attn_back(self):
        rows, width = self.rows, self.width2
        ga0, ga1, gb0, gb1, self.g_enc, _ = call2(
            partial(dec_attn_back_body, self.kept),
            [((width // 2, 3 * width), BF)] * 2 + [((width // 2, width + 128 + 3 * width // 2), BF)] * 2
            + [((rows, self.width), F32), ((16, width), F32)],
            [self.place, self.packed2, self.g_att2, self.lse2, self.stream2, self.normed2,
             self.g_middle2, self.d_par, self.d_in, self.embed, self.e_low, self.small2, self.go20,
             self.go21],
            scratch=[((rows, 3 * width), BF), ((width, rows), BF), ((width, rows), F32),
                     ((width, rows), F32), ((width, 128), F32), ((width, 128), F32),
                     ((self.width, rows), F32), ((self.width, rows), F32), ((rows, width), BF)],
            us=16,
        )
        self.gi2 = ((ga0, ga1), (gb0, gb1))

    def _feed_back(self, hidden):
        rows, width = self.rows, self.width
        scratch = [((width, hidden // 2), BF), ((hidden // 2, width), BF), ((rows, width), BF),
                   ((width, rows), BF), ((width, rows), BF), ((width, rows), BF)]
        return [((width // 2, hidden // 4), BF)] * 8, scratch

    def enc_feed_back_one(self):
        rows, width, hidden = self.rows, self.width, self.active.shape[1]
        ff, scratch = self._feed_back(hidden)
        (*g_ff, self.total, self.biases1) = call2(
            enc_feed_back_one_body,
            [*ff, ((rows, width), F32), ((1, hidden + width), F32)],
            [self.place, self.g_enc, self.normed_two, self.active, self.slope, self.e_weights],
            scratch=scratch,
            hbm_args=1,
            sems=4 + 4 * hidden // width,
            us=14,
        )
        self.ffa = (g_ff[:4], g_ff[4:])

    def enc_feed_back_two(self):
        rows, width, hidden = self.rows, self.width, self.active.shape[1]
        ff, scratch = self._feed_back(hidden)
        (*g_ff, self.g_middle, self.g_att, go0, go1, self.small, self.biases) = call2(
            enc_feed_back_two_body,
            [*ff, ((rows, width), F32), ((rows, width), BF), ((width, width // 2), BF),
             ((width, width // 2), BF), ((16, width), F32),
             ((1, self.biases1.shape[1] + self.biases2.shape[1]), F32)],
            [self.place, self.g_enc, self.normed_two, self.active, self.slope, self.total, self.biases1,
             self.biases2, self.middle, self.e_par, self.att_t, self.e_out, self.e_weights],
            scratch=[((rows, width), F32), *scratch, ((width, rows), F32), ((width, rows), F32),
                     ((rows, width), BF)],
            hbm_args=1,
            sems=4 + 4 * hidden // width,
            us=19,
        )
        self.ffb = (g_ff[:4], g_ff[4:])
        self.go = (go0, go1)

    def enc_attn_back_one(self):
        rows, width = self.rows, self.width
        (self.g_packed,) = call2(
            partial(enc_attn_back_one_body, self.kept),
            [((rows, 3 * width), BF)],
            [self.place, self.packed, self.g_att, self.lse],
            scratch=[((width, rows), BF)],
            us=12,
        )

    def enc_attn_back_two(self):
        rows, width = self.rows, self.width
        n = 3 * width // 2 - CUT_BACK
        ga0, ga1, gb0, gb1, self.g_stream, _ = call2(
            enc_attn_back_two_body,
            [((width, CUT_BACK + width // 2), BF)] * 2 + [((width, n + 128), BF)] * 2
            + [((rows, width), F32), ((16, width), F32)],
            [self.place, self.g_packed, self.x, self.normed, self.g_middle, self.e_par, self.e_in,
             self.small, *self.go],
            scratch=[((width, rows), F32), ((width, rows), F32), ((width, 128), F32),
                     ((width, 128), F32)],
            us=9,
        )
        self.gi = ((ga0, ga1), (gb0, gb1))

    def spread(self):
        return call(
            partial(spread_body, self.kept),
            [((self.span, self.width2), F32), ((self.span, self.width), F32)],
            [self.spots, self.out, self.g_stream],
            us=LAST,
        )

    def land(self, flights, names=(), more=()):
        names = ["place", *names]
        values, more = land(flights, ([getattr(self, n) for n in names], more))
        for name, value in zip(names, values):
            setattr(self, name, value)
        return more


CUT = 640
CUT_BACK = 512


def whole_weights(params, inproj, outproj, embed=None):
    columns = jnp.pad(params, ((0, 0), (0, 128 - params.shape[1])))
    if embed is None:
        return (jnp.concatenate([inproj, outproj, columns], axis=1),)
    n, m, k = inproj.shape[1] // 2, outproj.shape[1] // 2, embed.shape[1] // 2
    one_a = [inproj[:, :CUT], inproj[:, n : n + CUT]]
    one_b = [inproj[:, CUT:n], columns, inproj[:, n + CUT :], jnp.zeros_like(columns)]
    two = [outproj[:, :m], embed[:, :k], outproj[:, m:], embed[:, k:]]
    return tuple(jnp.concatenate(v, axis=1) for v in (one_a, one_b, two))


def local(
    tokens_in, valid_len, mask_pos,
    encoder_gains, encoder_biases, encoder_inproj, encoder_outproj,
    encoder_up, encoder_upbias, encoder_down, encoder_downbias,
    embed_weight, mask_token,
    decoder_gains, decoder_biases, decoder_inproj, decoder_outproj,
    decoder_up, decoder_upbias, decoder_down, decoder_downbias,
    cotangent,
):
    dp, tr, tc = (lax.axis_index(a) for a in ALL)
    blocks = tuple(lax.axis_size(a) for a in ALL) == (8, 2, 2)
    width, width2 = tokens_in.shape[1], cotangent.shape[1]
    hidden, hidden2 = 2 * encoder_up.shape[1], 2 * decoder_up.shape[1]
    masked = jnp.sum((mask_pos[0] < valid_len[0]).astype(jnp.int32))
    at = (dp, tr, tc, dp) if blocks else (0, 0, 0, 0)
    place = jnp.stack([jnp.int32(v) for v in (*at, tc, valid_len[0] - masked, masked, tr)])

    def feed(up, up_bias, down, down_bias):
        rows, units = 2 * up.shape[0] + 16, up.shape[1]
        args = [up, up_bias[None], down, down_bias[None]]
        (packed,) = call(pack_feed_body, [((rows, units), BF)], args)
        return lax.all_gather(packed, ("tr", "tc"), axis=0, tiled=True)

    enc = [encoder_up, encoder_upbias, encoder_down, encoder_downbias]
    dec = [decoder_up, decoder_upbias, decoder_down, decoder_downbias]
    if blocks:
        one, two, three = call(
            pack_body,
            [((48, 3 * width // 2 + 128), BF), ((48, width // 2 + width2 // 2), BF),
             ((16, 4 * width2 + 128), BF)],
            [encoder_gains.T, encoder_biases.T, encoder_inproj, encoder_outproj, embed_weight,
             decoder_gains.T, decoder_biases.T, mask_token[None], decoder_inproj, decoder_outproj],
        )
        one = Flight(gather_lanes(one, CUT))
        two, three = Flight(gather_all(two, GATHER_C)), Flight(gather_all(three, GATHER_D))
        place, enc, dec = land([one, two, three], (place, enc, dec))
        enc, dec = feed(*enc), feed(*dec)
        (tokens_in,) = land([one], (tokens_in,))
        sentence = Sentence(place, tokens_in, mask_pos, cotangent)
        sentence.land([one, two], ["x"])
        sentence.land([one], ["x"])
        sentence.land([one, two], ["x"])
        one_a, one_b = one.result
    else:
        def whole(v):
            return lax.all_gather(v, ALL, axis=0, tiled=True)

        e_par = whole(jnp.concatenate([encoder_gains, encoder_biases], axis=1))
        d_par = whole(jnp.concatenate([decoder_gains, decoder_biases, mask_token[:, None]], axis=1))
        one_a, one_b, two = whole_weights(
            e_par, whole(encoder_inproj), whole(encoder_outproj), whole(embed_weight)
        )
        (three,) = whole_weights(d_par, whole(decoder_inproj), whole(decoder_outproj))
        one_a, one_b = cut_gathered(one_a, GATHER_A, True), cut_gathered(one_b, GATHER_B, True)
        two = cut_gathered(two, GATHER_C, True)
        three = cut_gathered(three, GATHER_D, False)
        enc, dec = feed(*enc), feed(*dec)
        sentence = Sentence(place, tokens_in, mask_pos, cotangent)

    def feed_out(rows, units, halves):
        outs = []
        for part, pair in enumerate(halves):
            count = units // len(halves)
            outs = pl.pallas_call(
                partial(out_feed_body, part),
                out_shape=[jax.ShapeDtypeStruct((rows, units), F32), jax.ShapeDtypeStruct((units, rows), F32)],
                in_specs=[pl.BlockSpec(memory_space=pltpu.SMEM)]
                + [pl.BlockSpec(memory_space=pltpu.VMEM)] * 2 + [pl.BlockSpec(memory_space=pltpu.HBM)] * len(outs),
                out_specs=[pl.BlockSpec(memory_space=pltpu.HBM)] * 2,
                scratch_shapes=[pltpu.VMEM((rows, count), F32), pltpu.VMEM((rows, count), F32),
                                pltpu.VMEM((count, rows), F32), pltpu.SemaphoreType.DMA((2,))],
                input_output_aliases={3: 0, 4: 1} if outs else {},
                compiler_params=vmem([((rows, count), F32)] * 3),
                cost_estimate=cost(LAST),
            )(place, *pair, *outs)
        return outs

    def dec_out():
        n, n2 = width // 32, width2 // 32
        return call(
            out_dec_body,
            [((n2, 3 * width2), F32), ((n2, width2), F32), ((2, n2), F32), ((6, n2), F32), ((1, n2), F32),
             ((n, width2), F32)],
            finish(gi2)[0],
            us=LAST,
        )

    def bias_out(biases):
        sizes = [hidden // 2, width // 2, hidden2 // 2, width2 // 2]
        outs = call2(out_bias_body, [((1, n), F32) for n in sizes], [place, biases], us=LAST)
        return [v[0] for v in outs]

    gathers = [two, three] if blocks else []
    sentence.enc_attn(one_a, one_b)
    sentence.land(gathers, ["att_t", "e_par"])
    sentence.land(gathers, ["att_t", "e_par"])
    two = two.result if blocks else two
    sentence.enc_feed(two, enc)
    sentence.land(gathers[1:], ["e_low", "embed"])
    sentence.land(gathers[1:], ["e_low", "embed"])
    three = three.result if blocks else three
    sentence.dec_attn(three)
    sentence.dec_feed(dec)

    if blocks:
        sentence.land([], ["g_middle2", "g_att2", "ff2"])
        ff2 = Flight(reduce_feed(*sentence.ff2))
        sentence.land([ff2], ["g_middle2", "g_att2"])
        sentence.dec_attn_back()
        sentence.land([ff2], ["g_enc", "gi2"])
        gi2 = Flight(scatter_lanes(*sentence.gi2))
        sentence.land([gi2], ["g_enc"])
        sentence.enc_feed_back_one()
        sentence.land([ff2, gi2], ["total", "biases1", "ffa"])
        ffa = Flight(reduce_feed(*sentence.ffa))
        sentence.land([ffa], ["total", "biases1"])
        sentence.enc_feed_back_two()
        sentence.land([ffa, ff2, gi2], ["g_middle", "g_att", "small", "go", "biases", "ffb"])
        ffb = Flight(reduce_feed(*sentence.ffb))
        sentence.land([ffb], ["g_middle", "g_att", "small", "biases"])
        sentence.enc_attn_back_one()
        sentence.land([ffa, ffb, ff2, gi2], ["g_packed"])
        sentence.enc_attn_back_two()
        sentence.land([ffb, ffa, ff2, gi2], ["gi", "g_stream"])
        gi = Flight(scatter_lanes(*sentence.gi, sentence.biases))
        sentence.land([gi])
        dec_outs = dec_out()
        sentence.output, sentence.g_tokens = sentence.spread()
        for flight in (ffb, ffa, ff2, ffb):
            land([flight])
        dec_outs, (sentence.output, sentence.g_tokens) = land(
            [gi], (dec_outs, (sentence.output, sentence.g_tokens))
        )
        for flight in (ffa, ffb, ff2, ffa):
            land([flight])
        land([gi])
        outs2 = feed_out(width2 // 2, hidden2 // 2, [finish(ff2)])
        outs2 = land([gi], outs2)
        for flight in (ffb, ffa, ffb):
            land([flight])
        land([gi])
        outs = feed_out(width // 2, hidden // 2, [finish(ffa), finish(ffb)])
        bias_outs = bias_out(finish(gi)[1][0])
    else:
        sentence.dec_attn_back()
        sentence.enc_feed_back_one()
        sentence.enc_feed_back_two()
        sentence.enc_attn_back_one()
        sentence.enc_attn_back_two()

        def halves_of(ups, downs):
            sums = []
            for v in (ups, downs):
                near, far = add(v[0], swap(v[1], "tc")), add(v[2], swap(v[3], "tc"))
                v = lax.psum(add(near, swap(far, "tr")), "dp")
                sums.append(v.reshape(8, -1, v.shape[1]))
            v = jnp.concatenate(sums, axis=1)
            return [v[:4], v[4:]]

        outs2 = feed_out(width2 // 2, hidden2 // 2, [halves_of(*sentence.ff2)])
        halves = [halves_of(*sentence.ffa), halves_of(*sentence.ffb)]
        outs = feed_out(width // 2, hidden // 2, halves)
        bias_outs = bias_out(lax.psum(sentence.biases, ALL))
        sentence.output, sentence.g_tokens = sentence.spread()

    (g_up2, g_down2), (g_up, g_down) = outs2, outs
    b_up, b_down, b_up2, b_down2 = bias_outs
    if blocks:
        n = width // 32
        g_in2, g_out2, g_gains2, g_biases2, g_token, g_embed = dec_outs
        g_in, g_out, g_gains, g_biases = call(
            out_enc_body,
            [((n, 3 * width), F32), ((n, width), F32), ((2, n), F32), ((5, n), F32)],
            finish(gi)[0],
            us=LAST,
        )
        g_gains, g_biases, g_gains2, g_biases2 = g_gains.T, g_biases.T, g_gains2.T, g_biases2.T
        g_token = g_token[0]
    else:
        def scatter(v):
            return lax.psum_scatter(v, ALL, scatter_dimension=0, tiled=True).astype(F32)

        a = join_scattered(sentence.gi[0], SCATTER_A, True)
        b = join_scattered(sentence.gi[1], SCATTER_B, True)
        m = 3 * width // 2 - CUT_BACK
        k = CUT_BACK + width // 2
        g_in = [a[:, :CUT_BACK], b[:, :m], a[:, k : k + CUT_BACK], b[:, m + 128 : 2 * m + 128]]
        g_in = scatter(jnp.concatenate(g_in, axis=1))
        small = scatter(b[:, m : m + 128])
        g_gains, g_biases = small[:, :2], small[:, 2:7]
        g_out = scatter(jnp.concatenate([a[:, CUT_BACK:k], a[:, k + CUT_BACK :]], axis=1))
        g_in2 = scatter(join_scattered(sentence.gi2[0], SCATTER_A, False))
        k = width2 + 128
        v = join_scattered([g[:, :k] for g in sentence.gi2[1]], SCATTER_B, False)
        g_out2, small = scatter(v[:, :width2]), scatter(v[:, width2:])
        g_gains2, g_biases2, g_token = small[:, :2], small[:, 2:8], small[:, 8]
        v = [g[:, k:].reshape(16, -1, 3, width2 // 2).transpose(0, 2, 1, 3) for g in sentence.gi2[1]]
        v = [g.reshape(-1, width2 // 2) for g in v]
        g_embed = scatter(join_scattered(v, SCATTER_B, True))
    return (
        sentence.output, sentence.g_tokens, g_gains, g_biases, g_in, g_out, g_up, b_up, g_down, b_down,
        g_embed, g_token, g_gains2, g_biases2, g_in2, g_out2, g_up2, b_up2, g_down2, b_down2,
    )


def solution(mesh):
    rows = P(ALL, None)
    attention = (rows, rows, rows, rows)
    feed = (P("tc", "tr"), P("tr"), P("tr", "tc"), P("tc"))
    in_specs = (
        (rows, P(ALL), rows) + attention + feed + (rows, P(ALL)) + attention + feed + (rows,)
    )
    out_specs = (rows, rows) + attention + feed + (rows, P(ALL)) + attention + feed
    return jax.shard_map(local, mesh=mesh, in_specs=in_specs, out_specs=out_specs, check_vma=False)
```

time: 461 us -> 348 us (0.75)
  waiting for transfers between devices: 140 us -> 100 us
  starting transfers between devices: 116 us -> 78.1 us
  Pallas kernels: 146 us -> 116 us
  other arithmetic: 27.9 us -> 7.88 us
  between operations: 3.82 us -> 17.3 us
    ppermute x125 -> x85, waiting for transfers between devices: 140 us -> 100 us  [swap(): lax.ppermute(v, axis, [(i, i ^ distance) for i in range(lax.axis_size(axi...]
    ppermute x125 -> x85, starting transfers between devices: 116 us -> 78 us  [swap(): lax.ppermute(v, axis, [(i, i ^ distance) for i in range(lax.axis_size(axi...]
    pallas_call x17 -> x20, Pallas kernels: 146 us -> 116 us  [the longest x17 109 us: call(): pl.pallas_call(kernel, out_shape=[jax.ShapeDtypeStruct(s, d) for s, d in...]
    unnamed x187 -> x140, local copies, waits for them, and re-layouts: 11.5 us -> 22.2 us
    convert_element_type x53 -> x40, other arithmetic: 15.1 us -> 5.35 us  [add(): return (a.astype(F32) + b.astype(F32)).astype(BF)]
    slice x30 -> x20, local copies, waits for them, and re-layouts: 5.74 us -> 0.5 us  [the longest x4 0.13 us: scatter_lanes(): a[half:]]
  transfers between devices with their start and end apart: 125 -> 87, of which waited for: 48 -> 36; matrix products, arithmetic and copies ran while one was open for 9% -> 2% of each run, Pallas kernels for 24% -> 29%
where the time goes in v2:
time: 348 us; the launch traced here: 344 us
  Pallas kernels  116 us (33%)
  waiting for transfers between devices  100 us (29%)
  starting transfers between devices  78.1 us (22%)
  local copies, waits for them, and re-layouts  24.2 us (7%)
  between operations  17.3 us (5%)
  other arithmetic  7.88 us (2%)
    pallas_call x17, Pallas kernels, call(): pl.pallas_call(kernel, out_shape=[jax.ShapeDtypeStruct(s, d) for s, d in...  109 us
    ppermute x85, waiting for transfers between devices, swap(): lax.ppermute(v, axis, [(i, i ^ distance) for i in range(lax.axis_size(axi...  100 us
    ppermute x85, starting transfers between devices, swap(): lax.ppermute(v, axis, [(i, i ^ distance) for i in range(lax.axis_size(axi...  78 us
    unnamed x140, local copies, waits for them, and re-layouts  22.2 us
    pallas_call x3, Pallas kernels, feed_out(): pl.pallas_call(partial(out_feed_body, part), out_shape=[jax.ShapeDtypeStr...  7.1 us
  transfers between devices with their start and end apart: 87, of which 36 were waited for; matrix products, arithmetic and copies ran while one was open for 2% of the time, Pallas kernels for 29%

profile of v2, /device:TPU:0, one launch (start us, length us, event | category | flops | bytes accessed | tf_op | source)
XLA Modules:
  0.0 344.1 jit_solution(14031994711213137121)
XLA Ops:
  14.7 3.0 collective-permute-start
  26.5 2.9 collective-permute-start.6
  30.8 14.4 %collective-permute-done.3 = bf16[96,1280]{1,0:T(8,128)(2,1)S(1)} collective-permute-done((bf16[96,1280]{1,0:T(8,128)(2,1)S(1)}, bf16[96,1280]{1,0:T(8,128)(2,1)S(1)}, u32[]{:S(2)}, u32[]{:S(2)}) %collective-permute-start.3) | collective-permute-done | bytes 245792 | tf_op jit(solution)/shard_map/ppermute | solution.py:835
  49.3 2.9 collective-permute-done.5
  56.9 10.6 %collective-permute-done.8.refs_7_ = bf16[384,640]{1,0:T(8,128)(2,1)S(1)} collective-permute-done((bf16[384,640]{1,0:T(8,128)(2,1)S(1)}, bf16[384,640]{1,0:T(8,128)(2,1)S(1)}, u32[]{:S(2)}, u32[]{:S(2)}) %collective-permute-start.8) | collective-permute-done | bytes 491552 | tf_op jit(solution)/shard_map/ppermute | solution.py:835
  68.2 2.5 collective-permute-done.13
  70.7 3.7 %collective-permute-start.15 = (bf16[32,2176]{1,0:T(8,128)(2,1)S(1)}, bf16[32,2176]{1,0:T(8,128)(2,1)S(1)}, u32[]{:S(2)}, u32[]{:S(2)}) collective-permute-start(bf16[32,2176]{1,0:T(8,128)(2,1)S(1)} %pad_maximum_fusion.16), channel_id=1, source_target_pairs={{0,16},{4,20},{8,24},{12,28},{16,0},{20,4},{24,8},{28,12},{1,17},{... | collective-permute-start | bytes 417800 | tf_op jit(solution)/shard_map/ppermute | solution.py:835
  76.6 12.1 %shard_map.367 = (bf16[400,768]{1,0:T(8,128)(2,1)}, bf16[400,2304]{1,0:T(8,128)(2,1)}, bf16[768,400]{1,0:T(8,128)(2,1)}, f32[6,800]{1,0:T(8,128)}, bf16[768,2304]{1,0:T(8,128)(2,1)}, /*index=5*/f32[16,768]{1,0:T(8,128)}) custom-call(s32[8]{0:T(128)} %stack.26.refs_0_, bf16[400,768]{1,0:T(8,128)(2,1)} %copy-done.20, bf16[384,640]{1,0:T(8,128)(2,1)} %copy-done.44, ...), custom_call_target="tpu_custom_call" | custom-call | flops 12000000000 | bytes 36000000 | tf_op jit(solution)/shard_map/pallas_call | solution.py:82
  90.4 7.9 %collective-permute-done.18 = bf16[64,2176]{1,0:T(8,128)(2,1)S(1)} collective-permute-done((bf16[64,2176]{1,0:T(8,128)(2,1)S(1)}, bf16[64,2176]{1,0:T(8,128)(2,1)S(1)}, u32[]{:S(2)}, u32[]{:S(2)}) %collective-permute-start.18) | collective-permute-done | bytes 278560 | tf_op jit(solution)/shard_map/ppermute | solution.py:835
  100.7 16.4 %shard_map.369 = (f32[400,768]{1,0:T(8,128)}, bf16[400,768]{1,0:T(8,128)(2,1)}, bf16[400,3072]{1,0:T(8,128)(2,1)}, bf16[400,3072]{1,0:T(8,128)(2,1)}, bf16[400,7...) custom-call(s32[8]{0:T(128)} %stack.26.refs_0_, bf16[400,768]{1,0:T(8,128)(2,1)} %copy-done.20, ...), custom_call_target="tpu_custom_call" | custom-call | flops 15000000512 | bytes 45000000 | tf_op jit(solution)/shard_map/pallas_call | solution.py:82
  120.0 10.5 %shard_map.370 = (f32[400,512]{1,0:T(8,128)}, bf16[400,512]{1,0:T(8,128)(2,1)}, bf16[400,1536]{1,0:T(8,128)(2,1)}, bf16[512,400]{1,0:T(8,128)(2,1)}, f32[4,1600]...) custom-call(s32[8]{0:T(128)} %stack.26.refs_0_, ...), custom_call_target="tpu_custom_call" | custom-call | flops 11000000512 | bytes 33000000 | tf_op jit(solution)/shard_map/pallas_call | solution.py:82
  136.8 12.2 %shard_map.372 = (f32[400,512]{1,0:T(8,128)S(1)}, bf16[256,1024]{1,0:T(8,128)(2,1)S(1)}, bf16[256,1024]{1,0:T(8,128)(2,1)S(1)}, bf16[256,1024]{1,0:T(8,128)(2,1)...) custom-call(s32[8]{0:T(128)S(1)} %copy-done, ...), custom_call_target="tpu_custom_call" | custom-call | flops 16000000000 | bytes 48000000 | tf_op jit(solution)/shard_map/pallas_call | solution.py:82
  157.5 12.6 %shard_map.373 = (bf16[256,1536]{1,0:T(8,128)(2,1)S(1)}, bf16[256,1536]{1,0:T(8,128)(2,1)S(1)}, bf16[256,1408]{1,0:T(8,128)(2,1)S(1)}, bf16[256,1408]{1,0:T(8,12...) custom-call(s32[8]{0:T(128)S(1)} %copy-done, bf16[400,1536]{1,0:T(8,128)(2,1)S(1)} %copy-done.28, ...), custom_call_target="tpu_custom_call" | custom-call | flops 16000000000 | bytes 48000000 | tf_op jit(solution)/shard_map/pallas_call | solution.py:82
  176.1 9.2 %shard_map.374 = (bf16[384,768]{1,0:T(8,128)(2,1)S(1)}, bf16[384,768]{1,0:T(8,128)(2,1)S(1)}, bf16[384,768]{1,0:T(8,128)(2,1)S(1)}, bf16[384,768]{1,0:T(8,128)(2...) custom-call(s32[8]{0:T(128)S(1)} %copy-done, ...), custom_call_target="tpu_custom_call" | custom-call | flops 14000000000 | bytes 42000000 | tf_op jit(solution)/shard_map/pallas_call | solution.py:82
  185.3 2.7 collective-permute-done.34
  196.6 3.7 %copy-done.2 = bf16[3136,1536]{1,0:T(8,128)(2,1)S(1)} copy-done((bf16[3136,1536]{1,0:T(8,128)(2,1)S(1)}, bf16[3136,1536]{1,0:T(8,128)(2,1)}, u32[]{:S(2)}) %copy-start.2) | copy-done | bytes 9633816
  200.3 11.2 %shard_map.375 = (bf16[384,768]{1,0:T(8,128)(2,1)S(1)}, bf16[384,768]{1,0:T(8,128)(2,1)S(1)}, bf16[384,768]{1,0:T(8,128)(2,1)S(1)}, bf16[384,768]{1,0:T(8,128)(2...) custom-call(s32[8]{0:T(128)S(1)} %copy-done, ...), custom_call_target="tpu_custom_call" | custom-call | flops 19000000512 | bytes 57000000 | tf_op jit(solution)/shard_map/pallas_call | solution.py:82
  225.4 9.1 %shard_map.376.refs_1_ = bf16[400,2304]{1,0:T(8,128)(2,1)S(1)} custom-call(s32[8]{0:T(128)S(1)} %copy-done, bf16[400,2304]{1,0:T(8,128)(2,1)S(1)} %copy-done.25, bf16[400,768]{1,0:T(8,128)(2,1)S(1)} %get-tuple-element.472.refs_2_, f32[6,800]{1,0:T(8,128)S(1)} %copy-done.42), custom_call_target="tpu_custom_call" | custom-call | flops 12000000000 | bytes 36000000 | tf_op jit(solution)/shard_map/pallas_call | solution.py:82
  234.5 4.5 %collective-permute-done.52 = bf16[192,768]{1,0:T(8,128)(2,1)S(1)} collective-permute-done((bf16[192,768]{1,0:T(8,128)(2,1)S(1)}, bf16[192,768]{1,0:T(8,128)(2,1)S(1)}, u32[]{:S(2)}, u32[]{:S(2)}) %collective-permute-start.52) | collective-permute-done | bytes 294944 | tf_op jit(solution)/shard_map/ppermute | solution.py:835
  240.5 2.3 collective-permute-start.59
  246.4 5.8 %shard_map.377 = (bf16[768,896]{1,0:T(8,128)(2,1)S(1)}, bf16[768,896]{1,0:T(8,128)(2,1)S(1)}, bf16[768,768]{1,0:T(8,128)(2,1)S(1)}, bf16[768,768]{1,0:T(8,128)(2...) custom-call(s32[8]{0:T(128)S(1)} %copy-done, bf16[400,2304]{1,0:T(8,128)(2,1)S(1)} %shard_map.376.refs_1_, ...), custom_call_target="tpu_custom_call" | custom-call | flops 8999999488 | bytes 27000000 | tf_op jit(solution)/shard_map/pallas_call | solution.py:82
  252.8 2.7 collective-permute-done.58
  258.3 3.6 %shard_map.379 = (f32[529,512]{1,0:T(8,128)}, f32[529,768]{1,0:T(8,128)}) custom-call(s32[529,1]{1,0:T(8,128)S(1)} %get-tuple-element.514.refs_0_, f32[400,512]{1,0:T(8,128)S(1)} %get-tuple-element.515.refs_1_, f32[400,768]{1,0:T(8,128)S(1)} %get-tuple-element.516.refs_2_), custom_call_target="tpu_custom_call" | custom-call | flops 10000000 | bytes 30000 | tf_op jit(solution)/shard_map/pallas_call | solution.py:82
  261.9 4.3 %collective-permute-done.81 = bf16[1,96,768]{2,1,0:T(8,128)(2,1)S(1)} collective-permute-done((bf16[1,96,768]{2,1,0:T(8,128)(2,1)S(1)}, bf16[1,96,768]{2,1,0:T(8,128)(2,1)S(1)}, u32[]{:S(2)}, u32[]{:S(2)}) %collective-permute-start.81) | collective-permute-done | bytes 147488 | tf_op jit(solution)/shard_map/ppermute | solution.py:835
  275.7 9.6 %collective-permute-done.77 = bf16[1,96,768]{2,1,0:T(8,128)(2,1)S(1)} collective-permute-done((bf16[1,96,768]{2,1,0:T(8,128)(2,1)S(1)}, bf16[1,96,768]{2,1,0:T(8,128)(2,1)S(1)}, u32[]{:S(2)}, u32[]{:S(2)}) %collective-permute-start.77) | collective-permute-done | bytes 147488 | tf_op jit(solution)/shard_map/ppermute | solution.py:835
  286.6 2.8 collective-permute-done.66
  295.3 3.2 collective-permute-done.69
  304.0 7.0 %collective-permute-done.71.refs_2_ = bf16[4,64,1024]{2,1,0:T(8,128)(2,1)S(1)} collective-permute-done((bf16[4,64,1024]{2,1,0:T(8,128)(2,1)S(1)}, bf16[4,64,1024]{2,1,0:T(8,128)(2,1)S(1)}, u32[]{:S(2)}, u32[]{:S(2)}) %collective-permute-start.71) | collective-permute-done | bytes 524320 | tf_op jit(solution)/shard_map/ppermute | solution.py:835
  320.5 3.2 collective-permute-done.84.refs_2_
  323.7 2.4 shard_map.382
  326.1 5.2 %collective-permute-done.80.refs_2_ = bf16[4,96,768]{2,1,0:T(8,128)(2,1)S(1)} collective-permute-done((bf16[4,96,768]{2,1,0:T(8,128)(2,1)S(1)}, bf16[4,96,768]{2,1,0:T(8,128)(2,1)S(1)}, u32[]{:S(2)}, u32[]{:S(2)}) %collective-permute-start.80) | collective-permute-done | bytes 589856 | tf_op jit(solution)/shard_map/ppermute | solution.py:835
  331.2 2.4 shard_map.383
  (403 shorter events, 120.1 us)
Async XLA Ops:
  7.2 93.5 %all-gather.3.cloned.1.call-start = ((), (), s32[]{:S(2)}) async-start(), calls=%async_computation | async-start | bytes 12042240 | tf_op jit(solution)/shard_map/all_gather | solution.py:1184
  25.7 104.9 %all-gather.5.cloned.1.call-start = ((), (), s32[]{:S(2)}) async-start(), calls=%async_computation.1 | async-start | bytes 5406720 | tf_op jit(solution)/shard_map/all_gather | solution.py:1184
  26.5 22.8 %collective-permute-start.6 = (bf16[96,640]{1,0:T(8,128)(2,1)S(1)}, bf16[96,640]{1,0:T(8,128)(2,1)S(1)}, u32[]{:S(2)}, u32[]{:S(2)}) collective-permute-start(bf16[96,640]{1,0:T(8,128)(2,1)S(1)} %pad_maximum_fusion.17), channel_id=1, source_target_pairs={{0,16},{4,20},{8,24},{12,28},{16,0},{20,4},{24,8},{28,12},{1,17},{... | collective-permute-start | bytes 368648 | tf_op jit(solution)/shard_map/ppermute | solution.py:835
  29.4 15.7 %collective-permute-start.3 = (bf16[96,1280]{1,0:T(8,128)(2,1)S(1)}, bf16[96,1280]{1,0:T(8,128)(2,1)S(1)}, u32[]{:S(2)}, u32[]{:S(2)}) collective-permute-start(bf16[96,1280]{1,0:T(8,128)(2,1)S(1)} %pad_maximum_fusion.13), channel_id=1, source_target_pairs={{0,16},{4,20},{8,24},{12,28},{16,0},{20,4},{24,8},{28,12},{1,17},{... | collective-permute-start | bytes 737288 | tf_op jit(solution)/shard_map/ppermute | solution.py:835
  55.8 18.6 %collective-permute-start.11 = (bf16[384,640]{1,0:T(8,128)(2,1)S(1)}, bf16[384,640]{1,0:T(8,128)(2,1)S(1)}, u32[]{:S(2)}, u32[]{:S(2)}) collective-permute-start(bf16[384,640]{1,0:T(8,128)(2,1)S(1)} %pad_maximum_fusion.4.refs_6_), channel_id=1, source_target_pairs={{0,1},{1,0},{2,3},{3,2},{4,5},{5,4},{6,7},{7,6},{8,9},{9,8},{10,11... | collective-permute-start | bytes 1474568 | tf_op jit(solution)/shard_map/ppermute | solution.py:835
  55.9 18.6 %collective-permute-start.9 = (bf16[384,640]{1,0:T(8,128)(2,1)S(1)}, bf16[384,640]{1,0:T(8,128)(2,1)S(1)}, u32[]{:S(2)}, u32[]{:S(2)}) collective-permute-start(bf16[384,640]{1,0:T(8,128)(2,1)S(1)} %pad_maximum_fusion.3.refs_2_), channel_id=1, source_target_pairs={{0,1},{1,0},{2,3},{3,2},{4,5},{5,4},{6,7},{7,6},{8,9},{9,8},{10,11... | collective-permute-start | bytes 1474568 | tf_op jit(solution)/shard_map/ppermute | solution.py:835
  56.4 14.3 %collective-permute-start.13 = (bf16[192,640]{1,0:T(8,128)(2,1)S(1)}, bf16[192,640]{1,0:T(8,128)(2,1)S(1)}, u32[]{:S(2)}, u32[]{:S(2)}) collective-permute-start(bf16[192,640]{1,0:T(8,128)(2,1)S(1)} %pad_maximum_fusion.14), channel_id=1, source_target_pairs={{0,8},{4,12},{8,0},{12,4},{16,24},{20,28},{24,16},{28,20},{1,9},{5... | collective-permute-start | bytes 737288 | tf_op jit(solution)/shard_map/ppermute | solution.py:835
  70.7 18.0 %collective-permute-start.15 = (bf16[32,2176]{1,0:T(8,128)(2,1)S(1)}, bf16[32,2176]{1,0:T(8,128)(2,1)S(1)}, u32[]{:S(2)}, u32[]{:S(2)}) collective-permute-start(bf16[32,2176]{1,0:T(8,128)(2,1)S(1)} %pad_maximum_fusion.16), channel_id=1, source_target_pairs={{0,16},{4,20},{8,24},{12,28},{16,0},{20,4},{24,8},{28,12},{1,17},{... | collective-permute-start | bytes 417800 | tf_op jit(solution)/shard_map/ppermute | solution.py:835
  75.4 15.0 %collective-permute-start.16 = (bf16[384,640]{1,0:T(8,128)(2,1)S(1)}, bf16[384,640]{1,0:T(8,128)(2,1)S(1)}, u32[]{:S(2)}, u32[]{:S(2)}) collective-permute-start(bf16[384,640]{1,0:T(8,128)(2,1)S(1)} %constant_dynamic-update-slice_fusion.3.refs_3_), channel_id=1, source_target_pairs={{0,1},{1,0},{2,3},{3,2},{4,5},{5,4},{6,7},{7,6},{8,9},{9,8},{10,11... | collective-permute-start | bytes 1474568 | tf_op jit(solution)/shard_map/ppermute | solution.py:835
  99.1 18.2 %collective-permute-start.20 = (bf16[128,2176]{1,0:T(8,128)(2,1)S(1)}, bf16[128,2176]{1,0:T(8,128)(2,1)S(1)}, u32[]{:S(2)}, u32[]{:S(2)}) collective-permute-start(bf16[128,2176]{1,0:T(8,128)(2,1)S(1)} %constant_dynamic-update-slice_fusion.7.refs_3_), channel_id=1, source_target_pairs={{0,1},{1,0},{2,3},{3,2},{4,5},{5,4},{6,7},{7,6},{8,9},{9,8},{10,11... | collective-permute-start | bytes 1671176 | tf_op jit(solution)/shard_map/ppermute | solution.py:835
  99.2 17.9 %collective-permute-start.19 = (bf16[128,2176]{1,0:T(8,128)(2,1)S(1)}, bf16[128,2176]{1,0:T(8,128)(2,1)S(1)}, u32[]{:S(2)}, u32[]{:S(2)}) collective-permute-start(bf16[128,2176]{1,0:T(8,128)(2,1)S(1)} %constant_dynamic-update-slice_fusion.7.refs_3_), channel_id=1, source_target_pairs={{0,8},{4,12},{8,0},{12,4},{16,24},{20,28},{24,16},{28,20},{1,9},{5... | collective-permute-start | bytes 1671176 | tf_op jit(solution)/shard_map/ppermute | solution.py:835
  153.8 16.4 %collective-permute-start.28 = (bf16[128,1024]{1,0:T(8,128)(2,1)S(1)}, bf16[128,1024]{1,0:T(8,128)(2,1)S(1)}, u32[]{:S(2)}, u32[]{:S(2)}) collective-permute-start(bf16[128,1024]{1,0:T(8,128)(2,1)S(1)} %slice.227), channel_id=1, source_target_pairs={{0,4},{4,0},{8,12},{12,8},{16,20},{20,16},{24,28},{28,24},{1,5},{5... | collective-permute-start | bytes 786440 | tf_op jit(solution)/shard_map/ppermute | solution.py:835
  154.8 15.3 %collective-permute-start.27 = (bf16[128,1024]{1,0:T(8,128)(2,1)S(1)}, bf16[128,1024]{1,0:T(8,128)(2,1)S(1)}, u32[]{:S(2)}, u32[]{:S(2)}) collective-permute-start(bf16[128,1024]{1,0:T(8,128)(2,1)S(1)} %slice.226), channel_id=1, source_target_pairs={{0,4},{4,0},{8,12},{12,8},{16,20},{20,16},{24,28},{28,24},{1,5},{5... | collective-permute-start | bytes 786440 | tf_op jit(solution)/shard_map/ppermute | solution.py:835
  190.6 20.9 %collective-permute-start.43 = (bf16[64,1536]{1,0:T(8,128)(2,1)S(1)}, bf16[64,1536]{1,0:T(8,128)(2,1)S(1)}, u32[]{:S(2)}, u32[]{:S(2)}) collective-permute-start(bf16[64,1536]{1,0:T(8,128)(2,1)S(1)} %slice.240), channel_id=1, source_target_pairs={{0,2},{2,0},{1,3},{3,1},{4,6},{6,4},{5,7},{7,5},{8,10},{10,8},{9,1... | collective-permute-start | bytes 589832 | tf_op jit(solution)/shard_map/ppermute | solution.py:835
  191.4 20.2 %collective-permute-start.42 = (bf16[2,64,1024]{2,1,0:T(8,128)(2,1)S(1)}, bf16[2,64,1024]{2,1,0:T(8,128)(2,1)S(1)}, u32[]{:S(2)}, u32[]{:S(2)}) collective-permute-start(bf16[2,64,1024]{2,1,0:T(8,128)(2,1)S(1)} %fusion.3), channel_id=1, source_target_pairs={{0,8},{4,12},{8,0},{12,4},{16,24},{20,28},{24,16},{28,20},{1,9},{5... | collective-permute-start | bytes 786440 | tf_op jit(solution)/shard_map/ppermute | solution.py:835
  193.2 18.4 %collective-permute-start.41 = (bf16[192,768]{1,0:T(8,128)(2,1)S(1)}, bf16[192,768]{1,0:T(8,128)(2,1)S(1)}, u32[]{:S(2)}, u32[]{:S(2)}) collective-permute-start(bf16[192,768]{1,0:T(8,128)(2,1)S(1)} %slice.235), channel_id=1, source_target_pairs={{0,4},{4,0},{8,12},{12,8},{16,20},{20,16},{24,28},{28,24},{1,5},{5... | collective-permute-start | bytes 884744 | tf_op jit(solution)/shard_map/ppermute | solution.py:835
  194.3 17.3 %collective-permute-start.40 = (bf16[192,768]{1,0:T(8,128)(2,1)S(1)}, bf16[192,768]{1,0:T(8,128)(2,1)S(1)}, u32[]{:S(2)}, u32[]{:S(2)}) collective-permute-start(bf16[192,768]{1,0:T(8,128)(2,1)S(1)} %slice.234), channel_id=1, source_target_pairs={{0,4},{4,0},{8,12},{12,8},{16,20},{20,16},{24,28},{28,24},{1,5},{5... | collective-permute-start | bytes 884744 | tf_op jit(solution)/shard_map/ppermute | solution.py:835
  196.0 15.6 %collective-permute-start.39 = (bf16[384,768]{1,0:T(8,128)(2,1)S(1)}, bf16[384,768]{1,0:T(8,128)(2,1)S(1)}, u32[]{:S(2)}, u32[]{:S(2)}) collective-permute-start(bf16[384,768]{1,0:T(8,128)(2,1)S(1)} %add_convert_fusion.15), channel_id=1, source_target_pairs={{0,2},{2,0},{1,3},{3,1},{4,6},{6,4},{5,7},{7,5},{8,10},{10,8},{9,1... | collective-permute-start | bytes 1769480 | tf_op jit(solution)/shard_map/ppermute | solution.py:835
  217.6 16.9 %collective-permute-start.49 = (bf16[192,768]{1,0:T(8,128)(2,1)S(1)}, bf16[192,768]{1,0:T(8,128)(2,1)S(1)}, u32[]{:S(2)}, u32[]{:S(2)}) collective-permute-start(bf16[192,768]{1,0:T(8,128)(2,1)S(1)} %slice.246), channel_id=1, source_target_pairs={{0,4},{4,0},{8,12},{12,8},{16,20},{20,16},{24,28},{28,24},{1,5},{5... | collective-permute-start | bytes 884744 | tf_op jit(solution)/shard_map/ppermute | solution.py:835
  218.5 16.1 %collective-permute-start.50 = (bf16[192,768]{1,0:T(8,128)(2,1)S(1)}, bf16[192,768]{1,0:T(8,128)(2,1)S(1)}, u32[]{:S(2)}, u32[]{:S(2)}) collective-permute-start(bf16[192,768]{1,0:T(8,128)(2,1)S(1)} %add_convert_fusion.35), channel_id=1, source_target_pairs={{0,2},{2,0},{1,3},{3,1},{4,6},{6,4},{5,7},{7,5},{8,10},{10,8},{9,1... | collective-permute-start | bytes 884744 | tf_op jit(solution)/shard_map/ppermute | solution.py:835
  219.7 14.8 %collective-permute-start.53 = (bf16[192,768]{1,0:T(8,128)(2,1)S(1)}, bf16[192,768]{1,0:T(8,128)(2,1)S(1)}, u32[]{:S(2)}, u32[]{:S(2)}) collective-permute-start(bf16[192,768]{1,0:T(8,128)(2,1)S(1)} %slice.249), channel_id=1, source_target_pairs={{0,4},{4,0},{8,12},{12,8},{16,20},{20,16},{24,28},{28,24},{1,5},{5... | collective-permute-start | bytes 884744 | tf_op jit(solution)/shard_map/ppermute | solution.py:835
  221.0 18.1 %collective-permute-start.52 = (bf16[192,768]{1,0:T(8,128)(2,1)S(1)}, bf16[192,768]{1,0:T(8,128)(2,1)S(1)}, u32[]{:S(2)}, u32[]{:S(2)}) collective-permute-start(bf16[192,768]{1,0:T(8,128)(2,1)S(1)} %slice.248), channel_id=1, source_target_pairs={{0,4},{4,0},{8,12},{12,8},{16,20},{20,16},{24,28},{28,24},{1,5},{5... | collective-permute-start | bytes 884744 | tf_op jit(solution)/shard_map/ppermute | solution.py:835
  224.0 15.6 %collective-permute-start.51 = (bf16[384,768]{1,0:T(8,128)(2,1)S(1)}, bf16[384,768]{1,0:T(8,128)(2,1)S(1)}, u32[]{:S(2)}, u32[]{:S(2)}) collective-permute-start(bf16[384,768]{1,0:T(8,128)(2,1)S(1)} %add_convert_fusion.10), channel_id=1, source_target_pairs={{0,2},{2,0},{1,3},{3,1},{4,6},{6,4},{5,7},{7,5},{8,10},{10,8},{9,1... | collective-permute-start | bytes 1769480 | tf_op jit(solution)/shard_map/ppermute | solution.py:835
  268.8 20.6 %collective-permute-start.65 = (bf16[384,768]{1,0:T(8,128)(2,1)S(1)}, bf16[384,768]{1,0:T(8,128)(2,1)S(1)}, u32[]{:S(2)}, u32[]{:S(2)}) collective-permute-start(bf16[384,768]{1,0:T(8,128)(2,1)S(1)} %slice.261), channel_id=1, source_target_pairs={{0,2},{2,0},{1,3},{3,1},{4,6},{6,4},{5,7},{7,5},{8,10},{10,8},{9,1... | collective-permute-start | bytes 1769480 | tf_op jit(solution)/shard_map/ppermute | solution.py:835
  270.2 19.2 %collective-permute-start.64 = (bf16[384,896]{1,0:T(8,128)(2,1)S(1)}, bf16[384,896]{1,0:T(8,128)(2,1)S(1)}, u32[]{:S(2)}, u32[]{:S(2)}) collective-permute-start(bf16[384,896]{1,0:T(8,128)(2,1)S(1)} %slice.260), channel_id=1, source_target_pairs={{0,4},{4,0},{8,12},{12,8},{16,20},{20,16},{24,28},{28,24},{1,5},{5... | collective-permute-start | bytes 2064392 | tf_op jit(solution)/shard_map/ppermute | solution.py:835
  272.8 20.6 %collective-permute-start.82 = (bf16[1,96,768]{2,1,0:T(8,128)(2,1)S(1)}, bf16[1,96,768]{2,1,0:T(8,128)(2,1)S(1)}, u32[]{:S(2)}, u32[]{:S(2)}) collective-permute-start(bf16[1,96,768]{2,1,0:T(8,128)(2,1)S(1)} %add_convert_fusion.44), channel_id=1, source_target_pairs={{0,16},{4,20},{8,24},{12,28},{16,0},{20,4},{24,8},{28,12},{1,17},{... | collective-permute-start | bytes 442376 | tf_op jit(solution)/shard_map/ppermute | solution.py:835
  291.9 19.1 %collective-permute-start.71 = (bf16[4,64,1024]{2,1,0:T(8,128)(2,1)S(1)}, bf16[4,64,1024]{2,1,0:T(8,128)(2,1)S(1)}, u32[]{:S(2)}, u32[]{:S(2)}) collective-permute-start(bf16[4,64,1024]{2,1,0:T(8,128)(2,1)S(1)} %pad_maximum_fusion.2.refs_1_), channel_id=1, source_target_pairs={{0,4},{4,0},{8,12},{12,8},{16,20},{20,16},{24,28},{28,24},{1,5},{5... | collective-permute-start | bytes 1572872 | tf_op jit(solution)/shard_map/ppermute | solution.py:835
  298.6 14.7 %collective-permute-start.79 = (bf16[2,96,768]{2,1,0:T(8,128)(2,1)S(1)}, bf16[2,96,768]{2,1,0:T(8,128)(2,1)S(1)}, u32[]{:S(2)}, u32[]{:S(2)}) collective-permute-start(bf16[2,96,768]{2,1,0:T(8,128)(2,1)S(1)} %pad_maximum_fusion.8), channel_id=1, source_target_pairs={{0,8},{4,12},{8,0},{12,4},{16,24},{20,28},{24,16},{28,20},{1,9},{5... | collective-permute-start | bytes 884744 | tf_op jit(solution)/shard_map/ppermute | solution.py:835
  300.6 16.7 %collective-permute-start.72 = (bf16[96,1664]{1,0:T(8,128)(2,1)S(1)}, bf16[96,1664]{1,0:T(8,128)(2,1)S(1)}, u32[]{:S(2)}, u32[]{:S(2)}) collective-permute-start(bf16[96,1664]{1,0:T(8,128)(2,1)S(1)} %pad_maximum_fusion.5), channel_id=1, source_target_pairs={{0,8},{4,12},{8,0},{12,4},{16,24},{20,28},{24,16},{28,20},{1,9},{5... | collective-permute-start | bytes 958472 | tf_op jit(solution)/shard_map/ppermute | solution.py:835
  301.8 21.8 %collective-permute-start.84 = (bf16[4,96,768]{2,1,0:T(8,128)(2,1)S(1)}, bf16[4,96,768]{2,1,0:T(8,128)(2,1)S(1)}, u32[]{:S(2)}, u32[]{:S(2)}) collective-permute-start(bf16[4,96,768]{2,1,0:T(8,128)(2,1)S(1)} %pad_maximum_fusion.1.refs_1_), channel_id=1, source_target_pairs={{0,4},{4,0},{8,12},{12,8},{16,20},{20,16},{24,28},{28,24},{1,5},{5... | collective-permute-start | bytes 1769480 | tf_op jit(solution)/shard_map/ppermute | solution.py:835
  314.1 17.1 %collective-permute-start.80 = (bf16[4,96,768]{2,1,0:T(8,128)(2,1)S(1)}, bf16[4,96,768]{2,1,0:T(8,128)(2,1)S(1)}, u32[]{:S(2)}, u32[]{:S(2)}) collective-permute-start(bf16[4,96,768]{2,1,0:T(8,128)(2,1)S(1)} %pad_maximum_fusion.refs_1_), channel_id=1, source_target_pairs={{0,4},{4,0},{8,12},{12,8},{16,20},{20,16},{24,28},{28,24},{1,5},{5... | collective-permute-start | bytes 1769480 | tf_op jit(solution)/shard_map/ppermute | solution.py:835
  317.4 16.3 %collective-permute-start.74 = (bf16[48,1664]{1,0:T(8,128)(2,1)S(1)}, bf16[48,1664]{1,0:T(8,128)(2,1)S(1)}, u32[]{:S(2)}, u32[]{:S(2)}) collective-permute-start(bf16[48,1664]{1,0:T(8,128)(2,1)S(1)} %get-tuple-element.568), channel_id=1, source_target_pairs={{0,16},{4,20},{8,24},{12,28},{16,0},{20,4},{24,8},{28,12},{1,17},{... | collective-permute-start | bytes 479240 | tf_op jit(solution)/shard_map/ppermute | solution.py:835
  (121 other events, 814.3 us)
Sparse Core Ops, SparseCore 0:
  25.8 66.8 all-gather.2
  94.8 35.2 all-gather.4

commit v3 on v2

--- a/solution.py
+++ b/solution.py
@@ -51,7 +51,7 @@
             entry["started"] = True
 
 
-def call(body, outs, args, scratch=(), smem=0, hbm_args=0, sems=0, keep=(), us=2, alone=False):
+def call(body, outs, args, scratch=(), smem=0, hbm_args=0, sems=0, keep=(), us=2, alone=False, from_hbm=False):
     count = len(args) - smem - hbm_args
     specs = [pl.BlockSpec(memory_space=pltpu.SMEM)] * smem
     specs += [pl.BlockSpec(memory_space=pltpu.VMEM)] * count
@@ -78,10 +78,15 @@
         for entry in entries:
             pltpu.make_async_copy(entry["buffer"], entry["out"], entry["sem"]).wait()
 
+    args = list(args)
+    for k in range(smem if from_hbm else len(args) - hbm_args, len(args)):
+        args[k] = pltpu.with_memory_space_constraint(args[k], pltpu.HBM)
     spaces = [pltpu.HBM if k in keep else pltpu.VMEM for k in range(len(outs))]
     return pl.pallas_call(
         kernel,
-        out_shape=[jax.ShapeDtypeStruct(s, d) for s, d in outs],
+        out_shape=[
+            pltpu.HBM(s, d) if k in keep else jax.ShapeDtypeStruct(s, d) for k, (s, d) in enumerate(outs)
+        ],
         in_specs=specs,
         out_specs=[pl.BlockSpec(memory_space=space) for space in spaces],
         scratch_shapes=shapes,
@@ -228,7 +233,7 @@
 GATHER_A = (("tr", 1), ("dp", 4), ("dp", 2), ("dp", 1))
 GATHER_B = (("tr", 1), ("dp", 4), ("dp", 1), ("dp", 2))
 GATHER_C = (("tr", 1), ("dp", 4), ("dp", 2), ("dp", 1))
-GATHER_D = (("tr", 1), ("dp", 4), ("dp", 1), ("dp", 2))
+GATHER_D = (("tr", 1), ("dp", 1), ("dp", 4), ("dp", 2))
 SCATTER_A = (("dp", 1), ("tr", 1), ("dp", 2), ("dp", 4))
 SCATTER_B = (("tr", 1), ("dp", 1), ("dp", 2), ("dp", 4))
 FEED = (("dp", 1), ("dp", 2), ("dp", 4))
@@ -444,6 +449,7 @@
 
 def load_feed(place, gathered, up, down, sems, part=0, biases=None):
     copies = []
+    groups = []
     half = up.shape[0] // 2
     units = up.shape[1] // 2
     block = gathered.shape[0] // 4
@@ -471,21 +477,27 @@
                 )
             if biases is not None:
                 start(gathered.at[rows(2 * half, 16), :], biases.at[2 * tr + core])
-    return copies
+        groups.append(copies[sum(len(g) for g in groups) :])
+    return groups
+
+
+def wait(copies):
+    for copy in copies:
+        copy.wait()
 
 
 def bias_rows(biases, half):
-    up = jnp.concatenate([biases[0, 0:1, :], biases[2, 0:1, :]], axis=1)
-    down = jnp.concatenate([biases[0, 1:2, :half], biases[1, 1:2, :half]], axis=1)
-    return up.astype(F32), down.astype(F32)
+    return jnp.concatenate([biases[0, 1:2, :half], biases[1, 1:2, :half]], axis=1).astype(F32)
 
 
 def middle_of(stream, att_t, outproj, params):
     return stream + dot_nn(att_t[...].T, outproj[...]) + params[5:6, :]
 
 
-def feed_forward(normed_two, up, up_bias, down, active_out, slope_out, total, step):
-    hidden_units = up.shape[1]
+def feed_forward(
+    normed_two, up, up_bias, down, active_out, slope_out, total, step, copies, biases
+):
+    units = up.shape[1] // 2
     total[...] = jnp.zeros_like(total)
 
     def chunk(c, carry):
@@ -501,7 +513,10 @@
         total[...] += dot_nn(active, down[pl.ds(at, step), :])
         return carry
 
-    lax.fori_loop(0, hidden_units // step, chunk, 0)
+    for tr in range(2):
+        wait(copies[tr])
+        up_bias[:, tr * units : (tr + 1) * units] = biases[2 * tr, 0:1, :].astype(F32)
+        lax.fori_loop(tr * units // step, (tr + 1) * units // step, chunk, 0)
 
 
 def order_feed(place, source, target):
@@ -514,7 +529,7 @@
 
 
 def feed_backward(
-    place, part, parts, g_result, normed_two, active, slope, up, down,
+    copies, place, part, parts, g_result, normed_two, active, slope, up, down,
     g_ups, g_downs, g_upbias, g_normed, step, rows_t, ordered_n, ordered_g,
 ):
     width = normed_two.shape[1]
@@ -526,6 +541,7 @@
     rows_t[...] = g_result[...].T
     order_feed(place, rows_t, ordered_g)
     for tr in range(2):
+        wait(copies[tr])
         base = tr * units + part * count
         out_base = pl.multiple_of((place[7] ^ tr) * units + part * count, 128)
 
@@ -583,10 +599,8 @@
     normed_two[...] = n2
     for ref in (middle, normed_two, outproj, embed):
         save(ref)
-    for copy in copies:
-        copy.wait()
-    up_bias[...], down_bias = bias_rows(biases, width // 2)
-    feed_forward(n2, up, up_bias, down, active, slope, total, 512)
+    feed_forward(n2, up, up_bias, down, active, slope, total, 512, copies, biases)
+    down_bias = bias_rows(biases, width // 2)
     result = (total[...] + down_bias).astype(BF)
     e_low[...] = (middle[...] + result.astype(F32)).astype(BF)
 
@@ -602,10 +616,8 @@
     u, r = norm_parts(mid)
     n2 = (u * params[1:2, :] + params[6:7, :]).astype(BF)
     n2_s[...] = n2
-    for copy in copies:
-        copy.wait()
-    up_bias[...], down_bias = bias_rows(biases, up.shape[0] // 2)
-    feed_forward(n2, up, up_bias, down, active, slope, total, 512)
+    feed_forward(n2, up, up_bias, down, active, slope, total, 512, copies, biases)
+    down_bias = bias_rows(biases, up.shape[0] // 2)
     result = (total[...] + down_bias).astype(BF)
     out[...] = mid + result.astype(F32)
     save(out)
@@ -616,7 +628,7 @@
     g_biases[:, units:] = jnp.sum(g_res[...].astype(F32), axis=0, keepdims=True)
     total[...] = jnp.zeros_like(total)
     feed_backward(
-        place, 0, 1, g_res, n2_s, active, slope, up, down, (gu0, gu1, gu2, gu3), (gd0, gd1, gd2, gd3),
+        ((), ()), place, 0, 1, g_res, n2_s, active, slope, up, down, (gu0, gu1, gu2, gu3), (gd0, gd1, gd2, gd3),
         g_biases, total, 512, rows_t, ordered_n, ordered_g,
     )
     branch = after_feed_backward(
@@ -635,10 +647,8 @@
     g_res[...] = g_enc[...].astype(BF)
     total[...] = jnp.zeros_like(total)
     biases[:, 2 * up.shape[1] :] = jnp.sum(g_res[...].astype(F32), axis=0, keepdims=True)
-    for copy in copies:
-        copy.wait()
     feed_backward(
-        place, 0, 2, g_res, normed_two, active, slope, up, down, (gu0, gu1, gu2, gu3),
+        copies, place, 0, 2, g_res, normed_two, active, slope, up, down, (gu0, gu1, gu2, gu3),
         (gd0, gd1, gd2, gd3), biases, total, 384, rows_t, ordered_n, ordered_g,
     )
 
@@ -656,10 +666,8 @@
     biases[:, :count] = biases_in[...]
     biases[:, count:] = biases_dec[...]
     small[...] = jnp.zeros_like(small)
-    for copy in copies:
-        copy.wait()
     feed_backward(
-        place, 1, 2, g_res, normed_two, active, slope, up, down, (gu0, gu1, gu2, gu3),
+        copies, place, 1, 2, g_res, normed_two, active, slope, up, down, (gu0, gu1, gu2, gu3),
         (gd0, gd1, gd2, gd3), biases, total, 384, rows_t, ordered_n, ordered_g,
     )
     branch = after_feed_backward(
@@ -989,8 +997,7 @@
              ((16, width), F32)],
             [self.place, self.x, *one_a, *one_b],
             scratch=[((width, 128), BF)],
-            keep=(0, 1, 3, 4),
-            alone=True,
+            keep=(0, 1, 2, 3, 4, 5),
             us=12,
         )
 
@@ -1007,8 +1014,8 @@
                      ((4, 16, units), BF), ((1, hidden), F32)],
             hbm_args=1,
             sems=8 + 8 * units // width,
-            keep=(0, 1, 2, 3, 5),
-            alone=True,
+            keep=(0, 1, 2, 3, 4, 5, 6),
+            from_hbm=True,
             us=15,
         )
 
@@ -1022,8 +1029,8 @@
              ((width, width), BF), ((16, width), F32)],
             [self.place, self.e_low, self.embed, *three],
             scratch=[((width, 128), BF)],
-            keep=(1, 2, 4, 5),
-            alone=True,
+            keep=(0, 1, 2, 3, 4, 5, 6, 7),
+            from_hbm=True,
             us=11,
         )
 
@@ -1045,6 +1052,7 @@
             hbm_args=1,
             sems=8 + 8 * units // width,
             keep=(0,),
+            from_hbm=True,
             us=16,
         )
         self.ff2 = (g_ff[:4], g_ff[4:])
@@ -1180,7 +1188,7 @@
     def feed(up, up_bias, down, down_bias):
         rows, units = 2 * up.shape[0] + 16, up.shape[1]
         args = [up, up_bias[None], down, down_bias[None]]
-        (packed,) = call(pack_feed_body, [((rows, units), BF)], args)
+        (packed,) = call(pack_feed_body, [((rows, units), BF)], args, from_hbm=True)
         return lax.all_gather(packed, ("tr", "tc"), axis=0, tiled=True)
 
     enc = [encoder_up, encoder_upbias, encoder_down, encoder_downbias]
@@ -1192,16 +1200,18 @@
              ((16, 4 * width2 + 128), BF)],
             [encoder_gains.T, encoder_biases.T, encoder_inproj, encoder_outproj, embed_weight,
              decoder_gains.T, decoder_biases.T, mask_token[None], decoder_inproj, decoder_outproj],
-        )
+            from_hbm=True,
+        )
+        enc = feed(*enc)
         one = Flight(gather_lanes(one, CUT))
         two, three = Flight(gather_all(two, GATHER_C)), Flight(gather_all(three, GATHER_D))
-        place, enc, dec = land([one, two, three], (place, enc, dec))
-        enc, dec = feed(*enc), feed(*dec)
-        (tokens_in,) = land([one], (tokens_in,))
+        place, dec = land([one], (place, dec))
+        dec = feed(*dec)
+        (tokens_in,) = land([one, two, three], (tokens_in,))
         sentence = Sentence(place, tokens_in, mask_pos, cotangent)
-        sentence.land([one, two], ["x"])
         sentence.land([one], ["x"])
         sentence.land([one, two], ["x"])
+        sentence.land([one, two, three], ["x"])
         one_a, one_b = one.result
     else:
         def whole(v):
@@ -1255,7 +1265,7 @@
     gathers = [two, three] if blocks else []
     sentence.enc_attn(one_a, one_b)
     sentence.land(gathers, ["att_t", "e_par"])
-    sentence.land(gathers, ["att_t", "e_par"])
+    sentence.land(gathers[:1], ["att_t", "e_par"])
     two = two.result if blocks else two
     sentence.enc_feed(two, enc)
     sentence.land(gathers[1:], ["e_low", "embed"])

time: 348 us -> 329 us (0.945)
  local copies, waits for them, and re-layouts: 24.2 us -> 7.23 us
  waiting for transfers between devices: 100 us -> 90.7 us
  starting transfers between devices: 78.1 us -> 84.7 us
    unnamed x140 -> x78, local copies, waits for them, and re-layouts: 22.2 us -> 2.09 us
    ppermute x85, waiting for transfers between devices: 100 us -> 88.2 us  [swap(): lax.ppermute(v, axis, [(i, i ^ distance) for i in range(lax.axis_size(axi...]
    ppermute x85, starting transfers between devices: 78 us -> 84.6 us  [swap(): lax.ppermute(v, axis, [(i, i ^ distance) for i in range(lax.axis_size(axi...]
    broadcast_in_dim x4, local copies, waits for them, and re-layouts: 0.02 us -> 3.69 us  [feed(): args = [up, up_bias[None], down, down_bias[None]]]
  transfers between devices with their start and end apart: 87 -> 87, of which waited for: 36 -> 37; matrix products, arithmetic and copies ran while one was open for 2% -> 3% of each run, Pallas kernels for 29% -> 31%
where the time goes in v3:
time: 329 us; the launch traced here: 326 us
  Pallas kernels  118 us (36%)
  waiting for transfers between devices  90.7 us (28%)
  starting transfers between devices  84.7 us (26%)
  between operations  17.1 us (5%)
  other arithmetic  7.96 us (2%)
  local copies, waits for them, and re-layouts  7.23 us (2%)
    pallas_call x17, Pallas kernels, call(): pl.pallas_call(kernel, out_shape=[pltpu.HBM(s, d) if k in keep else jax.S...  111 us
    ppermute x85, waiting for transfers between devices, swap(): lax.ppermute(v, axis, [(i, i ^ distance) for i in range(lax.axis_size(axi...  88.2 us
    ppermute x85, starting transfers between devices, swap(): lax.ppermute(v, axis, [(i, i ^ distance) for i in range(lax.axis_size(axi...  84.6 us
    pallas_call x3, Pallas kernels, feed_out(): pl.pallas_call(partial(out_feed_body, part), out_shape=[jax.ShapeDtypeStr...  7.1 us
  transfers between devices with their start and end apart: 87, of which 37 were waited for; matrix products, arithmetic and copies ran while one was open for 3% of the time, Pallas kernels for 31%

profile of v3, /device:TPU:0, one launch (start us, length us, event | category | flops | bytes accessed | tf_op | source)
XLA Modules:
  0.0 325.9 jit_solution(15798600274291303423)
XLA Ops:
  9.8 3.3 %shard_map.368 = bf16[784,1536]{1,0:T(8,128)(2,1)} custom-call(bf16[384,1536]{1,0:T(8,128)(2,1)} %refs_0_.1, bf16[1,1536]{1,0:T(2,128)(2,1)} %broadcast_in_dim.16.refs_1_, bf16[1536,384]{1,0:T(8,128)(2,1)} %refs_2_.4, bf16[1,384]{1,0:T(2,128)(2,1)} %broadcast_in_dim.17.refs_3_), custom_call_target="tpu_custom_call" | custom-call | flops 2000000000 | bytes 6000000 | tf_op jit(solution)/shard_map/pallas_call | solution.py:85
  14.4 3.0 collective-permute-start.2
  23.8 3.2 collective-permute-start.1
  30.6 6.9 %collective-permute-done.1 = bf16[96,1280]{1,0:T(8,128)(2,1)S(1)} collective-permute-done((bf16[96,1280]{1,0:T(8,128)(2,1)S(1)}, bf16[96,1280]{1,0:T(8,128)(2,1)S(1)}, u32[]{:S(2)}, u32[]{:S(2)}) %collective-permute-start.1) | collective-permute-done | bytes 245792 | tf_op jit(solution)/shard_map/ppermute | solution.py:843
  41.9 2.5 collective-permute-done.5
  48.2 3.4 %collective-permute-start.8 = (bf16[96,640]{1,0:T(8,128)(2,1)S(1)}, bf16[96,640]{1,0:T(8,128)(2,1)S(1)}, u32[]{:S(2)}, u32[]{:S(2)}) collective-permute-start(bf16[96,640]{1,0:T(8,128)(2,1)S(1)} %pad_maximum_fusion.17), channel_id=1, source_target_pairs={{0,16},{4,20},{8,24},{12,28},{16,0},{20,4},{24,8},{28,12},{1,17},{... | collective-permute-start | bytes 368648 | tf_op jit(solution)/shard_map/ppermute | solution.py:843
  53.2 6.7 %collective-permute-done.8 = bf16[96,640]{1,0:T(8,128)(2,1)S(1)} collective-permute-done((bf16[96,640]{1,0:T(8,128)(2,1)S(1)}, bf16[96,640]{1,0:T(8,128)(2,1)S(1)}, u32[]{:S(2)}, u32[]{:S(2)}) %collective-permute-start.8) | collective-permute-done | bytes 122912 | tf_op jit(solution)/shard_map/ppermute | solution.py:843
  60.9 3.5 %collective-permute-start.13 = (bf16[192,640]{1,0:T(8,128)(2,1)S(1)}, bf16[192,640]{1,0:T(8,128)(2,1)S(1)}, u32[]{:S(2)}, u32[]{:S(2)}) collective-permute-start(bf16[192,640]{1,0:T(8,128)(2,1)S(1)} %pad_maximum_fusion.14), channel_id=1, source_target_pairs={{0,8},{4,12},{8,0},{12,4},{16,24},{20,28},{24,16},{28,20},{1,9},{5... | collective-permute-start | bytes 737288 | tf_op jit(solution)/shard_map/ppermute | solution.py:843
  65.0 6.0 %collective-permute-done.13 = bf16[192,640]{1,0:T(8,128)(2,1)S(1)} collective-permute-done((bf16[192,640]{1,0:T(8,128)(2,1)S(1)}, bf16[192,640]{1,0:T(8,128)(2,1)S(1)}, u32[]{:S(2)}, u32[]{:S(2)}) %collective-permute-start.13) | collective-permute-done | bytes 245792 | tf_op jit(solution)/shard_map/ppermute | solution.py:843
  72.6 10.0 %shard_map.367 = (bf16[400,768]{1,0:T(8,128)(2,1)}, bf16[400,2304]{1,0:T(8,128)(2,1)}, bf16[768,400]{1,0:T(8,128)(2,1)}, f32[6,800]{1,0:T(8,128)}, bf16[768,2304]{1,0:T(8,128)(2,1)}, /*index=5*/f32[16,768]{1,0:T(8,128)}) custom-call(s32[8]{0:T(128)S(1)} %stack.26.refs_0_, bf16[400,768]{1,0:T(8,128)(2,1)S(1)} %get-tuple-element.309.refs_1_.refs_2_, ...), custom_call_target="tpu_custom_call" | custom-call | flops 12000000000 | bytes 36000000 | tf_op jit(solution)/shard_map/pallas_call | solution.py:85
  82.7 4.8 %collective-permute-done.16 = bf16[64,2176]{1,0:T(8,128)(2,1)S(1)} collective-permute-done((bf16[64,2176]{1,0:T(8,128)(2,1)S(1)}, bf16[64,2176]{1,0:T(8,128)(2,1)S(1)}, u32[]{:S(2)}, u32[]{:S(2)}) %collective-permute-start.16) | collective-permute-done | bytes 278560 | tf_op jit(solution)/shard_map/ppermute | solution.py:843
  89.5 14.4 %shard_map.369 = (f32[400,768]{1,0:T(8,128)}, bf16[400,768]{1,0:T(8,128)(2,1)}, bf16[400,3072]{1,0:T(8,128)(2,1)}, bf16[400,3072]{1,0:T(8,128)(2,1)}, bf16[400,7...) custom-call(s32[8]{0:T(128)S(1)} %stack.26.refs_0_, bf16[400,768]{1,0:T(8,128)(2,1)} %copy-done.5, ...), custom_call_target="tpu_custom_call" | custom-call | flops 15000000512 | bytes 45000000 | tf_op jit(solution)/shard_map/pallas_call | solution.py:85
  106.7 9.6 %shard_map.370 = (f32[400,512]{1,0:T(8,128)}, bf16[400,512]{1,0:T(8,128)(2,1)}, bf16[400,1536]{1,0:T(8,128)(2,1)}, bf16[512,400]{1,0:T(8,128)(2,1)}, f32[4,1600]...) custom-call(s32[8]{0:T(128)S(1)} %stack.26.refs_0_, ...), custom_call_target="tpu_custom_call" | custom-call | flops 11000000512 | bytes 33000000 | tf_op jit(solution)/shard_map/pallas_call | solution.py:85
  118.7 13.5 %shard_map.372 = (f32[400,512]{1,0:T(8,128)}, bf16[256,1024]{1,0:T(8,128)(2,1)S(1)}, bf16[256,1024]{1,0:T(8,128)(2,1)S(1)}, bf16[256,1024]{1,0:T(8,128)(2,1)S(1)...) custom-call(s32[8]{0:T(128)S(1)} %stack.26.refs_0_, ...), custom_call_target="tpu_custom_call" | custom-call | flops 16000000000 | bytes 48000000 | tf_op jit(solution)/shard_map/pallas_call | solution.py:85
  139.7 12.6 %shard_map.373 = (bf16[256,1536]{1,0:T(8,128)(2,1)S(1)}, bf16[256,1536]{1,0:T(8,128)(2,1)S(1)}, bf16[256,1408]{1,0:T(8,128)(2,1)S(1)}, bf16[256,1408]{1,0:T(8,12...) custom-call(s32[8]{0:T(128)S(1)} %stack.26.refs_0_, bf16[400,1536]{1,0:T(8,128)(2,1)S(1)} %copy-done.13, ...), custom_call_target="tpu_custom_call" | custom-call | flops 16000000000 | bytes 48000000 | tf_op jit(solution)/shard_map/pallas_call | solution.py:85
  159.6 9.8 %shard_map.374 = (bf16[384,768]{1,0:T(8,128)(2,1)S(1)}, bf16[384,768]{1,0:T(8,128)(2,1)S(1)}, bf16[384,768]{1,0:T(8,128)(2,1)S(1)}, bf16[384,768]{1,0:T(8,128)(2...) custom-call(s32[8]{0:T(128)S(1)} %stack.26.refs_0_, ...), custom_call_target="tpu_custom_call" | custom-call | flops 14000000000 | bytes 42000000 | tf_op jit(solution)/shard_map/pallas_call | solution.py:85
  180.3 12.1 %shard_map.375 = (bf16[384,768]{1,0:T(8,128)(2,1)S(1)}, bf16[384,768]{1,0:T(8,128)(2,1)S(1)}, bf16[384,768]{1,0:T(8,128)(2,1)S(1)}, bf16[384,768]{1,0:T(8,128)(2...) custom-call(s32[8]{0:T(128)S(1)} %stack.26.refs_0_, ...), custom_call_target="tpu_custom_call" | custom-call | flops 19000000512 | bytes 57000000 | tf_op jit(solution)/shard_map/pallas_call | solution.py:85
  193.6 2.5 collective-permute-start.54
  206.5 9.1 %shard_map.376.refs_1_ = bf16[400,2304]{1,0:T(8,128)(2,1)S(1)} custom-call(s32[8]{0:T(128)S(1)} %stack.26.refs_0_, bf16[400,2304]{1,0:T(8,128)(2,1)S(1)} %copy-done.10, bf16[400,768]{1,0:T(8,128)(2,1)S(1)} %get-tuple-element.464.refs_2_, f32[6,800]{1,0:T(8,128)S(1)} %copy-done.25), custom_call_target="tpu_custom_call" | custom-call | flops 12000000000 | bytes 36000000 | tf_op jit(solution)/shard_map/pallas_call | solution.py:85
  215.8 5.2 %collective-permute-done.52 = bf16[192,768]{1,0:T(8,128)(2,1)S(1)} collective-permute-done((bf16[192,768]{1,0:T(8,128)(2,1)S(1)}, bf16[192,768]{1,0:T(8,128)(2,1)S(1)}, u32[]{:S(2)}, u32[]{:S(2)}) %collective-permute-start.52) | collective-permute-done | bytes 294944 | tf_op jit(solution)/shard_map/ppermute | solution.py:843
  222.4 2.4 collective-permute-start.59
  229.0 5.8 %shard_map.377 = (bf16[768,896]{1,0:T(8,128)(2,1)S(1)}, bf16[768,896]{1,0:T(8,128)(2,1)S(1)}, bf16[768,768]{1,0:T(8,128)(2,1)S(1)}, bf16[768,768]{1,0:T(8,128)(2...) custom-call(s32[8]{0:T(128)S(1)} %stack.26.refs_0_, bf16[400,2304]{1,0:T(8,128)(2,1)S(1)} %shard_map.376.refs_1_, ...), custom_call_target="tpu_custom_call" | custom-call | flops 8999999488 | bytes 27000000 | tf_op jit(solution)/shard_map/pallas_call | solution.py:85
  237.0 2.6 collective-permute-start.81
  240.3 3.6 %shard_map.379 = (f32[529,512]{1,0:T(8,128)}, f32[529,768]{1,0:T(8,128)}) custom-call(s32[529,1]{1,0:T(8,128)S(1)} %get-tuple-element.506.refs_0_, f32[400,512]{1,0:T(8,128)S(1)} %copy-done, f32[400,768]{1,0:T(8,128)S(1)} %get-tuple-element.508.refs_2_), custom_call_target="tpu_custom_call" | custom-call | flops 10000000 | bytes 30000 | tf_op jit(solution)/shard_map/pallas_call | solution.py:85
  244.0 2.7 collective-permute-done.81
  246.7 3.6 %collective-permute-start.70 = (bf16[2,64,1024]{2,1,0:T(8,128)(2,1)S(1)}, bf16[2,64,1024]{2,1,0:T(8,128)(2,1)S(1)}, u32[]{:S(2)}, u32[]{:S(2)}) collective-permute-start(bf16[2,64,1024]{2,1,0:T(8,128)(2,1)S(1)} %pad_maximum_fusion.12), channel_id=1, source_target_pairs={{0,8},{4,12},{8,0},{12,4},{16,24},{20,28},{24,16},{28,20},{1,9},{5... | collective-permute-start | bytes 786440 | tf_op jit(solution)/shard_map/ppermute | solution.py:843
  257.2 10.6 %collective-permute-done.77 = bf16[1,96,768]{2,1,0:T(8,128)(2,1)S(1)} collective-permute-done((bf16[1,96,768]{2,1,0:T(8,128)(2,1)S(1)}, bf16[1,96,768]{2,1,0:T(8,128)(2,1)S(1)}, u32[]{:S(2)}, u32[]{:S(2)}) %collective-permute-start.77) | collective-permute-done | bytes 147488 | tf_op jit(solution)/shard_map/ppermute | solution.py:843
  269.6 2.5 collective-permute-done.66
  277.4 4.3 %collective-permute-done.69 = f32[1,6400]{1,0:T(1,128)S(1)} collective-permute-done((f32[1,6400]{1,0:T(1,128)S(1)}, f32[1,6400]{1,0:T(1,128)S(1)}, u32[]{:S(2)}, u32[]{:S(2)}) %collective-permute-start.69) | collective-permute-done | bytes 25632 | tf_op jit(solution)/shard_map/ppermute | solution.py:843
  287.5 6.2 %collective-permute-done.71.refs_2_ = bf16[4,64,1024]{2,1,0:T(8,128)(2,1)S(1)} collective-permute-done((bf16[4,64,1024]{2,1,0:T(8,128)(2,1)S(1)}, bf16[4,64,1024]{2,1,0:T(8,128)(2,1)S(1)}, u32[]{:S(2)}, u32[]{:S(2)}) %collective-permute-start.71) | collective-permute-done | bytes 524320 | tf_op jit(solution)/shard_map/ppermute | solution.py:843
  303.2 3.2 collective-permute-done.84.refs_2_
  308.8 4.2 %collective-permute-done.80.refs_2_ = bf16[4,96,768]{2,1,0:T(8,128)(2,1)S(1)} collective-permute-done((bf16[4,96,768]{2,1,0:T(8,128)(2,1)S(1)}, bf16[4,96,768]{2,1,0:T(8,128)(2,1)S(1)}, u32[]{:S(2)}, u32[]{:S(2)}) %collective-permute-start.80) | collective-permute-done | bytes 589856 | tf_op jit(solution)/shard_map/ppermute | solution.py:843
  (340 shorter events, 114.8 us)
Async XLA Ops:
  7.2 82.3 %all-gather.3.cloned.1.call-start = ((), (), s32[]{:S(2)}) async-start(), calls=%async_computation | async-start | bytes 12042240 | tf_op jit(solution)/shard_map/all_gather | solution.py:1192
  13.1 105.7 %all-gather.5.cloned.1.call-start = ((), (), s32[]{:S(2)}) async-start(), calls=%async_computation.1 | async-start | bytes 5406720 | tf_op jit(solution)/shard_map/all_gather | solution.py:1192
  14.4 16.2 %collective-permute-start.2 = (bf16[48,640]{1,0:T(8,128)(2,1)S(1)}, bf16[48,640]{1,0:T(8,128)(2,1)S(1)}, u32[]{:S(2)}, u32[]{:S(2)}) collective-permute-start(bf16[48,640]{1,0:T(8,128)(2,1)S(1)} %get-tuple-element.292), channel_id=1, source_target_pairs={{0,2},{2,0},{1,3},{3,1},{4,6},{6,4},{5,7},{7,5},{8,10},{10,8},{9,1... | collective-permute-start | bytes 184328 | tf_op jit(solution)/shard_map/ppermute | solution.py:843
  45.8 14.8 %collective-permute-start.7 = (bf16[384,640]{1,0:T(8,128)(2,1)S(1)}, bf16[384,640]{1,0:T(8,128)(2,1)S(1)}, u32[]{:S(2)}, u32[]{:S(2)}) collective-permute-start(bf16[384,640]{1,0:T(8,128)(2,1)S(1)} %pad_maximum_fusion.4.refs_6_), channel_id=1, source_target_pairs={{0,8},{4,12},{8,0},{12,4},{16,24},{20,28},{24,16},{28,20},{1,9},{5... | collective-permute-start | bytes 1474568 | tf_op jit(solution)/shard_map/ppermute | solution.py:843
  71.1 17.0 %collective-permute-start.17 = (bf16[384,640]{1,0:T(8,128)(2,1)S(1)}, bf16[384,640]{1,0:T(8,128)(2,1)S(1)}, u32[]{:S(2)}, u32[]{:S(2)}) collective-permute-start(bf16[384,640]{1,0:T(8,128)(2,1)S(1)} %constant_dynamic-update-slice_fusion.3.refs_3_), channel_id=1, source_target_pairs={{0,1},{1,0},{2,3},{3,2},{4,5},{5,4},{6,7},{7,6},{8,9},{9,8},{10,11... | collective-permute-start | bytes 1474568 | tf_op jit(solution)/shard_map/ppermute | solution.py:843
  71.2 16.3 %collective-permute-start.15 = (bf16[384,640]{1,0:T(8,128)(2,1)S(1)}, bf16[384,640]{1,0:T(8,128)(2,1)S(1)}, u32[]{:S(2)}, u32[]{:S(2)}) collective-permute-start(bf16[384,640]{1,0:T(8,128)(2,1)S(1)} %constant_dynamic-update-slice_fusion.3.refs_3_), channel_id=1, source_target_pairs={{0,4},{4,0},{8,12},{12,8},{16,20},{20,16},{24,28},{28,24},{1,5},{5... | collective-permute-start | bytes 1474568 | tf_op jit(solution)/shard_map/ppermute | solution.py:843
  71.8 15.7 %collective-permute-start.16 = (bf16[64,2176]{1,0:T(8,128)(2,1)S(1)}, bf16[64,2176]{1,0:T(8,128)(2,1)S(1)}, u32[]{:S(2)}, u32[]{:S(2)}) collective-permute-start(bf16[64,2176]{1,0:T(8,128)(2,1)S(1)} %pad_maximum_fusion.10), channel_id=1, source_target_pairs={{0,16},{4,20},{8,24},{12,28},{16,0},{20,4},{24,8},{28,12},{1,17},{... | collective-permute-start | bytes 835592 | tf_op jit(solution)/shard_map/ppermute | solution.py:843
  87.5 16.5 %collective-permute-start.20 = (bf16[128,2176]{1,0:T(8,128)(2,1)S(1)}, bf16[128,2176]{1,0:T(8,128)(2,1)S(1)}, u32[]{:S(2)}, u32[]{:S(2)}) collective-permute-start(bf16[128,2176]{1,0:T(8,128)(2,1)S(1)} %constant_dynamic-update-slice_fusion.7.refs_3_), channel_id=1, source_target_pairs={{0,1},{1,0},{2,3},{3,2},{4,5},{5,4},{6,7},{7,6},{8,9},{9,8},{10,11... | collective-permute-start | bytes 1671176 | tf_op jit(solution)/shard_map/ppermute | solution.py:843
  88.1 15.8 %collective-permute-start.19 = (bf16[128,2176]{1,0:T(8,128)(2,1)S(1)}, bf16[128,2176]{1,0:T(8,128)(2,1)S(1)}, u32[]{:S(2)}, u32[]{:S(2)}) collective-permute-start(bf16[128,2176]{1,0:T(8,128)(2,1)S(1)} %constant_dynamic-update-slice_fusion.7.refs_3_), channel_id=1, source_target_pairs={{0,8},{4,12},{8,0},{12,4},{16,24},{20,28},{24,16},{28,20},{1,9},{5... | collective-permute-start | bytes 1671176 | tf_op jit(solution)/shard_map/ppermute | solution.py:843
  137.0 15.3 %collective-permute-start.28 = (bf16[128,1024]{1,0:T(8,128)(2,1)S(1)}, bf16[128,1024]{1,0:T(8,128)(2,1)S(1)}, u32[]{:S(2)}, u32[]{:S(2)}) collective-permute-start(bf16[128,1024]{1,0:T(8,128)(2,1)S(1)} %slice.227), channel_id=1, source_target_pairs={{0,4},{4,0},{8,12},{12,8},{16,20},{20,16},{24,28},{28,24},{1,5},{5... | collective-permute-start | bytes 786440 | tf_op jit(solution)/shard_map/ppermute | solution.py:843
  153.7 15.6 %collective-permute-start.31 = (bf16[128,1024]{1,0:T(8,128)(2,1)S(1)}, bf16[128,1024]{1,0:T(8,128)(2,1)S(1)}, u32[]{:S(2)}, u32[]{:S(2)}) collective-permute-start(bf16[128,1024]{1,0:T(8,128)(2,1)S(1)} %slice.229), channel_id=1, source_target_pairs={{0,4},{4,0},{8,12},{12,8},{16,20},{20,16},{24,28},{28,24},{1,5},{5... | collective-permute-start | bytes 786440 | tf_op jit(solution)/shard_map/ppermute | solution.py:843
  173.5 18.8 %collective-permute-start.43 = (bf16[64,1536]{1,0:T(8,128)(2,1)S(1)}, bf16[64,1536]{1,0:T(8,128)(2,1)S(1)}, u32[]{:S(2)}, u32[]{:S(2)}) collective-permute-start(bf16[64,1536]{1,0:T(8,128)(2,1)S(1)} %slice.240), channel_id=1, source_target_pairs={{0,2},{2,0},{1,3},{3,1},{4,6},{6,4},{5,7},{7,5},{8,10},{10,8},{9,1... | collective-permute-start | bytes 589832 | tf_op jit(solution)/shard_map/ppermute | solution.py:843
  174.9 17.5 %collective-permute-start.42 = (bf16[2,64,1024]{2,1,0:T(8,128)(2,1)S(1)}, bf16[2,64,1024]{2,1,0:T(8,128)(2,1)S(1)}, u32[]{:S(2)}, u32[]{:S(2)}) collective-permute-start(bf16[2,64,1024]{2,1,0:T(8,128)(2,1)S(1)} %fusion.3), channel_id=1, source_target_pairs={{0,8},{4,12},{8,0},{12,4},{16,24},{20,28},{24,16},{28,20},{1,9},{5... | collective-permute-start | bytes 786440 | tf_op jit(solution)/shard_map/ppermute | solution.py:843
  176.9 15.6 %collective-permute-start.41 = (bf16[192,768]{1,0:T(8,128)(2,1)S(1)}, bf16[192,768]{1,0:T(8,128)(2,1)S(1)}, u32[]{:S(2)}, u32[]{:S(2)}) collective-permute-start(bf16[192,768]{1,0:T(8,128)(2,1)S(1)} %slice.235), channel_id=1, source_target_pairs={{0,4},{4,0},{8,12},{12,8},{16,20},{20,16},{24,28},{28,24},{1,5},{5... | collective-permute-start | bytes 884744 | tf_op jit(solution)/shard_map/ppermute | solution.py:843
  178.1 14.3 %collective-permute-start.40 = (bf16[192,768]{1,0:T(8,128)(2,1)S(1)}, bf16[192,768]{1,0:T(8,128)(2,1)S(1)}, u32[]{:S(2)}, u32[]{:S(2)}) collective-permute-start(bf16[192,768]{1,0:T(8,128)(2,1)S(1)} %slice.234), channel_id=1, source_target_pairs={{0,4},{4,0},{8,12},{12,8},{16,20},{20,16},{24,28},{28,24},{1,5},{5... | collective-permute-start | bytes 884744 | tf_op jit(solution)/shard_map/ppermute | solution.py:843
  179.1 14.3 %collective-permute-start.39 = (bf16[384,768]{1,0:T(8,128)(2,1)S(1)}, bf16[384,768]{1,0:T(8,128)(2,1)S(1)}, u32[]{:S(2)}, u32[]{:S(2)}) collective-permute-start(bf16[384,768]{1,0:T(8,128)(2,1)S(1)} %add_convert_fusion.15), channel_id=1, source_target_pairs={{0,2},{2,0},{1,3},{3,1},{4,6},{6,4},{5,7},{7,5},{8,10},{10,8},{9,1... | collective-permute-start | bytes 1769480 | tf_op jit(solution)/shard_map/ppermute | solution.py:843
  199.6 16.0 %collective-permute-start.49 = (bf16[192,768]{1,0:T(8,128)(2,1)S(1)}, bf16[192,768]{1,0:T(8,128)(2,1)S(1)}, u32[]{:S(2)}, u32[]{:S(2)}) collective-permute-start(bf16[192,768]{1,0:T(8,128)(2,1)S(1)} %slice.246), channel_id=1, source_target_pairs={{0,4},{4,0},{8,12},{12,8},{16,20},{20,16},{24,28},{28,24},{1,5},{5... | collective-permute-start | bytes 884744 | tf_op jit(solution)/shard_map/ppermute | solution.py:843
  200.4 15.2 %collective-permute-start.50 = (bf16[192,768]{1,0:T(8,128)(2,1)S(1)}, bf16[192,768]{1,0:T(8,128)(2,1)S(1)}, u32[]{:S(2)}, u32[]{:S(2)}) collective-permute-start(bf16[192,768]{1,0:T(8,128)(2,1)S(1)} %add_convert_fusion.35), channel_id=1, source_target_pairs={{0,2},{2,0},{1,3},{3,1},{4,6},{6,4},{5,7},{7,5},{8,10},{10,8},{9,1... | collective-permute-start | bytes 884744 | tf_op jit(solution)/shard_map/ppermute | solution.py:843
  203.6 17.4 %collective-permute-start.52 = (bf16[192,768]{1,0:T(8,128)(2,1)S(1)}, bf16[192,768]{1,0:T(8,128)(2,1)S(1)}, u32[]{:S(2)}, u32[]{:S(2)}) collective-permute-start(bf16[192,768]{1,0:T(8,128)(2,1)S(1)} %slice.248), channel_id=1, source_target_pairs={{0,4},{4,0},{8,12},{12,8},{16,20},{20,16},{24,28},{28,24},{1,5},{5... | collective-permute-start | bytes 884744 | tf_op jit(solution)/shard_map/ppermute | solution.py:843
  205.0 16.6 %collective-permute-start.51 = (bf16[384,768]{1,0:T(8,128)(2,1)S(1)}, bf16[384,768]{1,0:T(8,128)(2,1)S(1)}, u32[]{:S(2)}, u32[]{:S(2)}) collective-permute-start(bf16[384,768]{1,0:T(8,128)(2,1)S(1)} %add_convert_fusion.10), channel_id=1, source_target_pairs={{0,2},{2,0},{1,3},{3,1},{4,6},{6,4},{5,7},{7,5},{8,10},{10,8},{9,1... | collective-permute-start | bytes 1769480 | tf_op jit(solution)/shard_map/ppermute | solution.py:843
  236.0 14.4 %collective-permute-start.61 = (bf16[768,896]{1,0:T(8,128)(2,1)S(1)}, bf16[768,896]{1,0:T(8,128)(2,1)S(1)}, u32[]{:S(2)}, u32[]{:S(2)}) collective-permute-start(bf16[768,896]{1,0:T(8,128)(2,1)S(1)} %get-tuple-element.512), channel_id=1, source_target_pairs={{0,1},{1,0},{2,3},{3,2},{4,5},{5,4},{6,7},{7,6},{8,9},{9,8},{10,11... | collective-permute-start | bytes 4128776 | tf_op jit(solution)/shard_map/ppermute | solution.py:843
  236.0 14.3 %collective-permute-start.62 = (bf16[768,768]{1,0:T(8,128)(2,1)S(1)}, bf16[768,768]{1,0:T(8,128)(2,1)S(1)}, u32[]{:S(2)}, u32[]{:S(2)}) collective-permute-start(bf16[768,768]{1,0:T(8,128)(2,1)S(1)} %get-tuple-element.513), channel_id=1, source_target_pairs={{0,1},{1,0},{2,3},{3,2},{4,5},{5,4},{6,7},{7,6},{8,9},{9,8},{10,11... | collective-permute-start | bytes 3538952 | tf_op jit(solution)/shard_map/ppermute | solution.py:843
  250.7 21.4 %collective-permute-start.65 = (bf16[384,768]{1,0:T(8,128)(2,1)S(1)}, bf16[384,768]{1,0:T(8,128)(2,1)S(1)}, u32[]{:S(2)}, u32[]{:S(2)}) collective-permute-start(bf16[384,768]{1,0:T(8,128)(2,1)S(1)} %slice.261), channel_id=1, source_target_pairs={{0,2},{2,0},{1,3},{3,1},{4,6},{6,4},{5,7},{7,5},{8,10},{10,8},{9,1... | collective-permute-start | bytes 1769480 | tf_op jit(solution)/shard_map/ppermute | solution.py:843
  252.5 19.6 %collective-permute-start.64 = (bf16[384,896]{1,0:T(8,128)(2,1)S(1)}, bf16[384,896]{1,0:T(8,128)(2,1)S(1)}, u32[]{:S(2)}, u32[]{:S(2)}) collective-permute-start(bf16[384,896]{1,0:T(8,128)(2,1)S(1)} %slice.260), channel_id=1, source_target_pairs={{0,4},{4,0},{8,12},{12,8},{16,20},{20,16},{24,28},{28,24},{1,5},{5... | collective-permute-start | bytes 2064392 | tf_op jit(solution)/shard_map/ppermute | solution.py:843
  253.3 14.6 %collective-permute-start.77 = (bf16[1,96,768]{2,1,0:T(8,128)(2,1)S(1)}, bf16[1,96,768]{2,1,0:T(8,128)(2,1)S(1)}, u32[]{:S(2)}, u32[]{:S(2)}) collective-permute-start(bf16[1,96,768]{2,1,0:T(8,128)(2,1)S(1)} %slice.277), channel_id=1, source_target_pairs={{0,16},{4,20},{8,24},{12,28},{16,0},{20,4},{24,8},{28,12},{1,17},{... | collective-permute-start | bytes 442376 | tf_op jit(solution)/shard_map/ppermute | solution.py:843
  254.1 21.7 %collective-permute-start.82 = (bf16[1,96,768]{2,1,0:T(8,128)(2,1)S(1)}, bf16[1,96,768]{2,1,0:T(8,128)(2,1)S(1)}, u32[]{:S(2)}, u32[]{:S(2)}) collective-permute-start(bf16[1,96,768]{2,1,0:T(8,128)(2,1)S(1)} %add_convert_fusion.44), channel_id=1, source_target_pairs={{0,16},{4,20},{8,24},{12,28},{16,0},{20,4},{24,8},{28,12},{1,17},{... | collective-permute-start | bytes 442376 | tf_op jit(solution)/shard_map/ppermute | solution.py:843
  275.3 18.5 %collective-permute-start.71 = (bf16[4,64,1024]{2,1,0:T(8,128)(2,1)S(1)}, bf16[4,64,1024]{2,1,0:T(8,128)(2,1)S(1)}, u32[]{:S(2)}, u32[]{:S(2)}) collective-permute-start(bf16[4,64,1024]{2,1,0:T(8,128)(2,1)S(1)} %pad_maximum_fusion.2.refs_1_), channel_id=1, source_target_pairs={{0,4},{4,0},{8,12},{12,8},{16,20},{20,16},{24,28},{28,24},{1,5},{5... | collective-permute-start | bytes 1572872 | tf_op jit(solution)/shard_map/ppermute | solution.py:843
  282.7 17.3 %collective-permute-start.72 = (bf16[96,1664]{1,0:T(8,128)(2,1)S(1)}, bf16[96,1664]{1,0:T(8,128)(2,1)S(1)}, u32[]{:S(2)}, u32[]{:S(2)}) collective-permute-start(bf16[96,1664]{1,0:T(8,128)(2,1)S(1)} %pad_maximum_fusion.5), channel_id=1, source_target_pairs={{0,8},{4,12},{8,0},{12,4},{16,24},{20,28},{24,16},{28,20},{1,9},{5... | collective-permute-start | bytes 958472 | tf_op jit(solution)/shard_map/ppermute | solution.py:843
  285.9 20.4 %collective-permute-start.84 = (bf16[4,96,768]{2,1,0:T(8,128)(2,1)S(1)}, bf16[4,96,768]{2,1,0:T(8,128)(2,1)S(1)}, u32[]{:S(2)}, u32[]{:S(2)}) collective-permute-start(bf16[4,96,768]{2,1,0:T(8,128)(2,1)S(1)} %pad_maximum_fusion.1.refs_1_), channel_id=1, source_target_pairs={{0,4},{4,0},{8,12},{12,8},{16,20},{20,16},{24,28},{28,24},{1,5},{5... | collective-permute-start | bytes 1769480 | tf_op jit(solution)/shard_map/ppermute | solution.py:843
  296.2 16.8 %collective-permute-start.80 = (bf16[4,96,768]{2,1,0:T(8,128)(2,1)S(1)}, bf16[4,96,768]{2,1,0:T(8,128)(2,1)S(1)}, u32[]{:S(2)}, u32[]{:S(2)}) collective-permute-start(bf16[4,96,768]{2,1,0:T(8,128)(2,1)S(1)} %pad_maximum_fusion.refs_1_), channel_id=1, source_target_pairs={{0,4},{4,0},{8,12},{12,8},{16,20},{20,16},{24,28},{28,24},{1,5},{5... | collective-permute-start | bytes 1769480 | tf_op jit(solution)/shard_map/ppermute | solution.py:843
  300.1 15.4 %collective-permute-start.74 = (bf16[48,1664]{1,0:T(8,128)(2,1)S(1)}, bf16[48,1664]{1,0:T(8,128)(2,1)S(1)}, u32[]{:S(2)}, u32[]{:S(2)}) collective-permute-start(bf16[48,1664]{1,0:T(8,128)(2,1)S(1)} %get-tuple-element.560), channel_id=1, source_target_pairs={{0,16},{4,20},{8,24},{12,28},{16,0},{20,4},{24,8},{28,12},{1,17},{... | collective-permute-start | bytes 479240 | tf_op jit(solution)/shard_map/ppermute | solution.py:843
  300.9 14.6 %collective-permute-start.75 = (f32[1,6400]{1,0:T(1,128)S(1)}, f32[1,6400]{1,0:T(1,128)S(1)}, u32[]{:S(2)}, u32[]{:S(2)}) collective-permute-start(f32[1,6400]{1,0:T(1,128)S(1)} %add.199), channel_id=1, source_target_pairs={{0,16},{4,20},{8,24},{12,28},{16,0},{20,4},{24,8},{28,12},{1,17},{... | collective-permute-start | bytes 76808 | tf_op jit(solution)/shard_map/ppermute | solution.py:843
  (90 other events, 634.1 us)
Sparse Core Ops, SparseCore 0:
  13.2 68.0 all-gather.2
  83.4 35.2 all-gather.4

commit v4 on v3

--- a/solution.py
+++ b/solution.py
@@ -775,14 +775,15 @@
         target[...] = dot_nn(pick, hi) + dot_nn(pick, mid) + dot_nn(pick, low)
 
 
-def out_feed_body(part, *refs):
-    place, halves = refs[0], refs[1:3]
+def out_feed_body(part, count, *refs):
+    place, arrays = refs[0], refs[1 : 1 + count]
     g_up, g_down, up, turned, down, sems = refs[-6:]
     units = up.shape[1]
-    for x, ref in enumerate(halves):
+    for k, ref in enumerate(arrays):
         block = ref.shape[1] // 2
-        for m in range(4):
-            at = pl.multiple_of((place[3] ^ feed_block(4 * x + m)) * block, block)
+        for m in range(ref.shape[0]):
+            dp = place[3] ^ feed_block(ref.shape[0] * k + m)
+            at = pl.multiple_of(dp * block, block)
             rows = ref[m].astype(F32)
             up[pl.ds(at, block), :] = rows[:block]
             turned[pl.ds(at, block), :] = rows[block:]
@@ -914,7 +915,7 @@
     return v, [v + w for v, w in zip(extra, got)]
 
 
-def reduce_feed(ups, downs):
+def reduce_feed(ups, downs, x_last):
     got = yield tuple(swap(v, "tc") for v in (ups[1], ups[3], downs[1], downs[3]))
     up, up_far, down, down_far = (
         add(v, w) for v, w in zip((ups[0], ups[2], downs[0], downs[2]), got)
@@ -932,11 +933,16 @@
         half = v.shape[0] // 2
         (got,) = yield (swap(v[half:], "dp", distance),)
         v = add(v[:half], got)
-    for distance in (4, 2):
-        (got,) = yield (swap(v, "dp", distance),)
+    (got,) = yield (swap(v, "dp", 4),)
+    v = jnp.concatenate([v, got], axis=0)
+    if x_last:
+        (got,) = yield (swap(v, "dp", 2),)
         v = jnp.concatenate([v, got], axis=0)
-    (got,) = yield (swap(v, "dp", 1),)
-    return v, got
+        (got,) = yield (swap(v, "dp", 1),)
+        return v, got
+    (w,) = yield (swap(v, "dp", 1),)
+    one, two = yield (swap(v, "dp", 2), swap(w, "dp", 2))
+    return v, one, w, two
 
 
 def chip_axes(order):
@@ -1234,14 +1240,14 @@
         for part, pair in enumerate(halves):
             count = units // len(halves)
             outs = pl.pallas_call(
-                partial(out_feed_body, part),
+                partial(out_feed_body, part, len(pair)),
                 out_shape=[jax.ShapeDtypeStruct((rows, units), F32), jax.ShapeDtypeStruct((units, rows), F32)],
                 in_specs=[pl.BlockSpec(memory_space=pltpu.SMEM)]
-                + [pl.BlockSpec(memory_space=pltpu.VMEM)] * 2 + [pl.BlockSpec(memory_space=pltpu.HBM)] * len(outs),
+                + [pl.BlockSpec(memory_space=pltpu.VMEM)] * len(pair) + [pl.BlockSpec(memory_space=pltpu.HBM)] * len(outs),
                 out_specs=[pl.BlockSpec(memory_space=pltpu.HBM)] * 2,
                 scratch_shapes=[pltpu.VMEM((rows, count), F32), pltpu.VMEM((rows, count), F32),
                                 pltpu.VMEM((count, rows), F32), pltpu.SemaphoreType.DMA((2,))],
-                input_output_aliases={3: 0, 4: 1} if outs else {},
+                input_output_aliases={len(pair) + 1: 0, len(pair) + 2: 1} if outs else {},
                 compiler_params=vmem([((rows, count), F32)] * 3),
                 cost_estimate=cost(LAST),
             )(place, *pair, *outs)
@@ -1276,7 +1282,7 @@
 
     if blocks:
         sentence.land([], ["g_middle2", "g_att2", "ff2"])
-        ff2 = Flight(reduce_feed(*sentence.ff2))
+        ff2 = Flight(reduce_feed(*sentence.ff2, True))
         sentence.land([ff2], ["g_middle2", "g_att2"])
         sentence.dec_attn_back()
         sentence.land([ff2], ["g_enc", "gi2"])
@@ -1284,18 +1290,18 @@
         sentence.land([gi2], ["g_enc"])
         sentence.enc_feed_back_one()
         sentence.land([ff2, gi2], ["total", "biases1", "ffa"])
-        ffa = Flight(reduce_feed(*sentence.ffa))
+        ffa = Flight(reduce_feed(*sentence.ffa, True))
         sentence.land([ffa], ["total", "biases1"])
         sentence.enc_feed_back_two()
         sentence.land([ffa, ff2, gi2], ["g_middle", "g_att", "small", "go", "biases", "ffb"])
-        ffb = Flight(reduce_feed(*sentence.ffb))
+        ffb = Flight(reduce_feed(*sentence.ffb, False))
         sentence.land([ffb], ["g_middle", "g_att", "small", "biases"])
         sentence.enc_attn_back_one()
         sentence.land([ffa, ffb, ff2, gi2], ["g_packed"])
         sentence.enc_attn_back_two()
         sentence.land([ffb, ffa, ff2, gi2], ["gi", "g_stream"])
         gi = Flight(scatter_lanes(*sentence.gi, sentence.biases))
-        sentence.land([gi])
+        sentence.land([gi], ["g_stream"])
         dec_outs = dec_out()
         sentence.output, sentence.g_tokens = sentence.spread()
         for flight in (ffb, ffa, ff2, ffb):

time: 329 us -> 321 us (0.976)
  starting transfers between devices: 84.7 us -> 80.1 us
  waiting for transfers between devices: 90.7 us -> 86.5 us
    ppermute x85 -> x86, starting transfers between devices: 84.6 us -> 80.1 us  [swap(): lax.ppermute(v, axis, [(i, i ^ distance) for i in range(lax.axis_size(axi...]
    ppermute x85 -> x86, waiting for transfers between devices: 88.2 us -> 84.1 us  [swap(): lax.ppermute(v, axis, [(i, i ^ distance) for i in range(lax.axis_size(axi...]
  transfers between devices with their start and end apart: 87 -> 88, of which waited for: 37 -> 37; matrix products, arithmetic and copies ran while one was open for 3% -> 3% of each run, Pallas kernels for 31% -> 31%
where the time goes in v4:
time: 321 us; the launch traced here: 317 us
  Pallas kernels  118 us (37%)
  waiting for transfers between devices  86.5 us (27%)
  starting transfers between devices  80.1 us (25%)
  between operations  17.1 us (5%)
  other arithmetic  7.78 us (2%)
  local copies, waits for them, and re-layouts  7.22 us (2%)
    pallas_call x17, Pallas kernels, call(): pl.pallas_call(kernel, out_shape=[pltpu.HBM(s, d) if k in keep else jax.S...  111 us
    ppermute x86, waiting for transfers between devices, swap(): lax.ppermute(v, axis, [(i, i ^ distance) for i in range(lax.axis_size(axi...  84.1 us
    ppermute x86, starting transfers between devices, swap(): lax.ppermute(v, axis, [(i, i ^ distance) for i in range(lax.axis_size(axi...  80.1 us
    pallas_call x3, Pallas kernels, feed_out(): pl.pallas_call(partial(out_feed_body, part, len(pair)), out_shape=[jax.Sh...  7.11 us
  transfers between devices with their start and end apart: 88, of which 37 were waited for; matrix products, arithmetic and copies ran while one was open for 3% of the time, Pallas kernels for 31%

profile of v4, /device:TPU:0, one launch (start us, length us, event | category | flops | bytes accessed | tf_op | source)
XLA Modules:
  0.0 317.1 jit_solution(7499708816450598222)
XLA Ops:
  9.8 3.3 %shard_map.368 = bf16[784,1536]{1,0:T(8,128)(2,1)} custom-call(bf16[384,1536]{1,0:T(8,128)(2,1)} %refs_0_.1, bf16[1,1536]{1,0:T(2,128)(2,1)} %broadcast_in_dim.16.refs_1_, bf16[1536,384]{1,0:T(8,128)(2,1)} %refs_2_.4, bf16[1,384]{1,0:T(2,128)(2,1)} %broadcast_in_dim.17.refs_3_), custom_call_target="tpu_custom_call" | custom-call | flops 2000000000 | bytes 6000000 | tf_op jit(solution)/shard_map/pallas_call | solution.py:85
  14.4 3.0 collective-permute-start.2
  23.8 3.2 collective-permute-start.1
  28.1 2.4 shard_map.371
  30.6 6.9 %collective-permute-done.1 = bf16[96,1280]{1,0:T(8,128)(2,1)S(1)} collective-permute-done((bf16[96,1280]{1,0:T(8,128)(2,1)S(1)}, bf16[96,1280]{1,0:T(8,128)(2,1)S(1)}, u32[]{:S(2)}, u32[]{:S(2)}) %collective-permute-start.1) | collective-permute-done | bytes 245792 | tf_op jit(solution)/shard_map/ppermute | solution.py:844
  41.9 2.5 collective-permute-done.5
  48.2 3.4 %collective-permute-start.8 = (bf16[96,640]{1,0:T(8,128)(2,1)S(1)}, bf16[96,640]{1,0:T(8,128)(2,1)S(1)}, u32[]{:S(2)}, u32[]{:S(2)}) collective-permute-start(bf16[96,640]{1,0:T(8,128)(2,1)S(1)} %pad_maximum_fusion.16), channel_id=1, source_target_pairs={{0,16},{4,20},{8,24},{12,28},{16,0},{20,4},{24,8},{28,12},{1,17},{... | collective-permute-start | bytes 368648 | tf_op jit(solution)/shard_map/ppermute | solution.py:844
  53.2 6.7 %collective-permute-done.8 = bf16[96,640]{1,0:T(8,128)(2,1)S(1)} collective-permute-done((bf16[96,640]{1,0:T(8,128)(2,1)S(1)}, bf16[96,640]{1,0:T(8,128)(2,1)S(1)}, u32[]{:S(2)}, u32[]{:S(2)}) %collective-permute-start.8) | collective-permute-done | bytes 122912 | tf_op jit(solution)/shard_map/ppermute | solution.py:844
  61.0 3.5 %collective-permute-start.13 = (bf16[192,640]{1,0:T(8,128)(2,1)S(1)}, bf16[192,640]{1,0:T(8,128)(2,1)S(1)}, u32[]{:S(2)}, u32[]{:S(2)}) collective-permute-start(bf16[192,640]{1,0:T(8,128)(2,1)S(1)} %pad_maximum_fusion.13), channel_id=1, source_target_pairs={{0,8},{4,12},{8,0},{12,4},{16,24},{20,28},{24,16},{28,20},{1,9},{5... | collective-permute-start | bytes 737288 | tf_op jit(solution)/shard_map/ppermute | solution.py:844
  65.0 6.0 %collective-permute-done.13 = bf16[192,640]{1,0:T(8,128)(2,1)S(1)} collective-permute-done((bf16[192,640]{1,0:T(8,128)(2,1)S(1)}, bf16[192,640]{1,0:T(8,128)(2,1)S(1)}, u32[]{:S(2)}, u32[]{:S(2)}) %collective-permute-start.13) | collective-permute-done | bytes 245792 | tf_op jit(solution)/shard_map/ppermute | solution.py:844
  72.6 10.0 %shard_map.367 = (bf16[400,768]{1,0:T(8,128)(2,1)}, bf16[400,2304]{1,0:T(8,128)(2,1)}, bf16[768,400]{1,0:T(8,128)(2,1)}, f32[6,800]{1,0:T(8,128)}, bf16[768,2304]{1,0:T(8,128)(2,1)}, /*index=5*/f32[16,768]{1,0:T(8,128)}) custom-call(s32[8]{0:T(128)S(1)} %stack.26.refs_0_, bf16[400,768]{1,0:T(8,128)(2,1)S(1)} %get-tuple-element.312.refs_1_.refs_2_, ...), custom_call_target="tpu_custom_call" | custom-call | flops 12000000000 | bytes 36000000 | tf_op jit(solution)/shard_map/pallas_call | solution.py:85
  82.7 4.8 %collective-permute-done.16 = bf16[64,2176]{1,0:T(8,128)(2,1)S(1)} collective-permute-done((bf16[64,2176]{1,0:T(8,128)(2,1)S(1)}, bf16[64,2176]{1,0:T(8,128)(2,1)S(1)}, u32[]{:S(2)}, u32[]{:S(2)}) %collective-permute-start.16) | collective-permute-done | bytes 278560 | tf_op jit(solution)/shard_map/ppermute | solution.py:844
  89.5 14.4 %shard_map.369 = (f32[400,768]{1,0:T(8,128)}, bf16[400,768]{1,0:T(8,128)(2,1)}, bf16[400,3072]{1,0:T(8,128)(2,1)}, bf16[400,3072]{1,0:T(8,128)(2,1)}, bf16[400,7...) custom-call(s32[8]{0:T(128)S(1)} %stack.26.refs_0_, bf16[400,768]{1,0:T(8,128)(2,1)} %copy-done.5, ...), custom_call_target="tpu_custom_call" | custom-call | flops 15000000512 | bytes 45000000 | tf_op jit(solution)/shard_map/pallas_call | solution.py:85
  106.7 9.6 %shard_map.370 = (f32[400,512]{1,0:T(8,128)}, bf16[400,512]{1,0:T(8,128)(2,1)}, bf16[400,1536]{1,0:T(8,128)(2,1)}, bf16[512,400]{1,0:T(8,128)(2,1)}, f32[4,1600]...) custom-call(s32[8]{0:T(128)S(1)} %stack.26.refs_0_, ...), custom_call_target="tpu_custom_call" | custom-call | flops 11000000512 | bytes 33000000 | tf_op jit(solution)/shard_map/pallas_call | solution.py:85
  118.8 13.5 %shard_map.372 = (f32[400,512]{1,0:T(8,128)}, bf16[256,1024]{1,0:T(8,128)(2,1)S(1)}, bf16[256,1024]{1,0:T(8,128)(2,1)S(1)}, bf16[256,1024]{1,0:T(8,128)(2,1)S(1)...) custom-call(s32[8]{0:T(128)S(1)} %stack.26.refs_0_, ...), custom_call_target="tpu_custom_call" | custom-call | flops 16000000000 | bytes 48000000 | tf_op jit(solution)/shard_map/pallas_call | solution.py:85
  139.7 12.6 %shard_map.373 = (bf16[256,1536]{1,0:T(8,128)(2,1)S(1)}, bf16[256,1536]{1,0:T(8,128)(2,1)S(1)}, bf16[256,1408]{1,0:T(8,128)(2,1)S(1)}, bf16[256,1408]{1,0:T(8,12...) custom-call(s32[8]{0:T(128)S(1)} %stack.26.refs_0_, bf16[400,1536]{1,0:T(8,128)(2,1)S(1)} %copy-done.13, ...), custom_call_target="tpu_custom_call" | custom-call | flops 16000000000 | bytes 48000000 | tf_op jit(solution)/shard_map/pallas_call | solution.py:85
  159.6 9.8 %shard_map.374 = (bf16[384,768]{1,0:T(8,128)(2,1)S(1)}, bf16[384,768]{1,0:T(8,128)(2,1)S(1)}, bf16[384,768]{1,0:T(8,128)(2,1)S(1)}, bf16[384,768]{1,0:T(8,128)(2...) custom-call(s32[8]{0:T(128)S(1)} %stack.26.refs_0_, ...), custom_call_target="tpu_custom_call" | custom-call | flops 14000000000 | bytes 42000000 | tf_op jit(solution)/shard_map/pallas_call | solution.py:85
  180.3 12.1 %shard_map.375 = (bf16[384,768]{1,0:T(8,128)(2,1)S(1)}, bf16[384,768]{1,0:T(8,128)(2,1)S(1)}, bf16[384,768]{1,0:T(8,128)(2,1)S(1)}, bf16[384,768]{1,0:T(8,128)(2...) custom-call(s32[8]{0:T(128)S(1)} %stack.26.refs_0_, ...), custom_call_target="tpu_custom_call" | custom-call | flops 19000000512 | bytes 57000000 | tf_op jit(solution)/shard_map/pallas_call | solution.py:85
  193.6 2.5 collective-permute-start.54
  206.5 9.1 %shard_map.376.refs_1_ = bf16[400,2304]{1,0:T(8,128)(2,1)S(1)} custom-call(s32[8]{0:T(128)S(1)} %stack.26.refs_0_, bf16[400,2304]{1,0:T(8,128)(2,1)S(1)} %copy-done.10, bf16[400,768]{1,0:T(8,128)(2,1)S(1)} %get-tuple-element.467.refs_2_, f32[6,800]{1,0:T(8,128)S(1)} %copy-done.25), custom_call_target="tpu_custom_call" | custom-call | flops 12000000000 | bytes 36000000 | tf_op jit(solution)/shard_map/pallas_call | solution.py:85
  215.8 5.2 %collective-permute-done.52 = bf16[192,768]{1,0:T(8,128)(2,1)S(1)} collective-permute-done((bf16[192,768]{1,0:T(8,128)(2,1)S(1)}, bf16[192,768]{1,0:T(8,128)(2,1)S(1)}, u32[]{:S(2)}, u32[]{:S(2)}) %collective-permute-start.52) | collective-permute-done | bytes 294944 | tf_op jit(solution)/shard_map/ppermute | solution.py:844
  222.4 2.4 collective-permute-start.59
  229.0 5.8 %shard_map.377 = (bf16[768,896]{1,0:T(8,128)(2,1)S(1)}, bf16[768,896]{1,0:T(8,128)(2,1)S(1)}, bf16[768,768]{1,0:T(8,128)(2,1)S(1)}, bf16[768,768]{1,0:T(8,128)(2...) custom-call(s32[8]{0:T(128)S(1)} %stack.26.refs_0_, bf16[400,2304]{1,0:T(8,128)(2,1)S(1)} %shard_map.376.refs_1_, ...), custom_call_target="tpu_custom_call" | custom-call | flops 8999999488 | bytes 27000000 | tf_op jit(solution)/shard_map/pallas_call | solution.py:85
  246.6 4.7 %collective-permute-done.76 = bf16[2,96,768]{2,1,0:T(8,128)(2,1)S(1)} collective-permute-done((bf16[2,96,768]{2,1,0:T(8,128)(2,1)S(1)}, bf16[2,96,768]{2,1,0:T(8,128)(2,1)S(1)}, u32[]{:S(2)}, u32[]{:S(2)}) %collective-permute-start.76) | collective-permute-done | bytes 294944 | tf_op jit(solution)/shard_map/ppermute | solution.py:844
  252.3 5.6 %collective-permute-done.70 = bf16[2,64,1024]{2,1,0:T(8,128)(2,1)S(1)} collective-permute-done((bf16[2,64,1024]{2,1,0:T(8,128)(2,1)S(1)}, bf16[2,64,1024]{2,1,0:T(8,128)(2,1)S(1)}, u32[]{:S(2)}, u32[]{:S(2)}) %collective-permute-start.70) | collective-permute-done | bytes 262176 | tf_op jit(solution)/shard_map/ppermute | solution.py:844
  260.0 3.7 %shard_map.379 = (f32[529,512]{1,0:T(8,128)}, f32[529,768]{1,0:T(8,128)}) custom-call(s32[529,1]{1,0:T(8,128)S(1)} %get-tuple-element.509.refs_0_, f32[400,512]{1,0:T(8,128)S(1)} %copy-done, f32[400,768]{1,0:T(8,128)S(1)} %get-tuple-element.515.refs_2_), custom_call_target="tpu_custom_call" | custom-call | flops 10000000 | bytes 30000 | tf_op jit(solution)/shard_map/pallas_call | solution.py:85
  269.4 4.9 %collective-permute-done.78 = bf16[1,96,768]{2,1,0:T(8,128)(2,1)S(1)} collective-permute-done((bf16[1,96,768]{2,1,0:T(8,128)(2,1)S(1)}, bf16[1,96,768]{2,1,0:T(8,128)(2,1)S(1)}, u32[]{:S(2)}, u32[]{:S(2)}) %collective-permute-start.78) | collective-permute-done | bytes 147488 | tf_op jit(solution)/shard_map/ppermute | solution.py:844
  277.8 6.4 %collective-permute-done.84 = bf16[2,96,768]{2,1,0:T(8,128)(2,1)S(1)} collective-permute-done((bf16[2,96,768]{2,1,0:T(8,128)(2,1)S(1)}, bf16[2,96,768]{2,1,0:T(8,128)(2,1)S(1)}, u32[]{:S(2)}, u32[]{:S(2)}) %collective-permute-start.84) | collective-permute-done | bytes 294944 | tf_op jit(solution)/shard_map/ppermute | solution.py:844
  287.9 3.3 %collective-permute-done.80.refs_3_ = bf16[2,96,768]{2,1,0:T(8,128)(2,1)S(1)} collective-permute-done((bf16[2,96,768]{2,1,0:T(8,128)(2,1)S(1)}, bf16[2,96,768]{2,1,0:T(8,128)(2,1)S(1)}, u32[]{:S(2)}, u32[]{:S(2)}) %collective-permute-start.80) | collective-permute-done | bytes 294944 | tf_op jit(solution)/shard_map/ppermute | solution.py:844
  292.5 5.7 %collective-permute-done.73 = f32[1,6400]{1,0:T(1,128)S(1)} collective-permute-done((f32[1,6400]{1,0:T(1,128)S(1)}, f32[1,6400]{1,0:T(1,128)S(1)}, u32[]{:S(2)}, u32[]{:S(2)}) %collective-permute-start.73) | collective-permute-done | bytes 25632 | tf_op jit(solution)/shard_map/ppermute | solution.py:844
  301.6 2.4 shard_map.382
  304.0 2.4 shard_map.383
  (341 shorter events, 108.1 us)
Async XLA Ops:
  7.2 82.3 %all-gather.3.cloned.1.call-start = ((), (), s32[]{:S(2)}) async-start(), calls=%async_computation | async-start | bytes 12042240 | tf_op jit(solution)/shard_map/all_gather | solution.py:1198
  13.1 105.7 %all-gather.5.cloned.1.call-start = ((), (), s32[]{:S(2)}) async-start(), calls=%async_computation.1 | async-start | bytes 5406720 | tf_op jit(solution)/shard_map/all_gather | solution.py:1198
  14.4 16.2 %collective-permute-start.2 = (bf16[48,640]{1,0:T(8,128)(2,1)S(1)}, bf16[48,640]{1,0:T(8,128)(2,1)S(1)}, u32[]{:S(2)}, u32[]{:S(2)}) collective-permute-start(bf16[48,640]{1,0:T(8,128)(2,1)S(1)} %get-tuple-element.295), channel_id=1, source_target_pairs={{0,2},{2,0},{1,3},{3,1},{4,6},{6,4},{5,7},{7,5},{8,10},{10,8},{9,1... | collective-permute-start | bytes 184328 | tf_op jit(solution)/shard_map/ppermute | solution.py:844
  23.8 13.7 %collective-permute-start.1 = (bf16[96,1280]{1,0:T(8,128)(2,1)S(1)}, bf16[96,1280]{1,0:T(8,128)(2,1)S(1)}, u32[]{:S(2)}, u32[]{:S(2)}) collective-permute-start(bf16[96,1280]{1,0:T(8,128)(2,1)S(1)} %pad_maximum_fusion.12), channel_id=1, source_target_pairs={{0,16},{4,20},{8,24},{12,28},{16,0},{20,4},{24,8},{28,12},{1,17},{... | collective-permute-start | bytes 737288 | tf_op jit(solution)/shard_map/ppermute | solution.py:844
  45.8 14.8 %collective-permute-start.7 = (bf16[384,640]{1,0:T(8,128)(2,1)S(1)}, bf16[384,640]{1,0:T(8,128)(2,1)S(1)}, u32[]{:S(2)}, u32[]{:S(2)}) collective-permute-start(bf16[384,640]{1,0:T(8,128)(2,1)S(1)} %pad_maximum_fusion.3.refs_6_), channel_id=1, source_target_pairs={{0,8},{4,12},{8,0},{12,4},{16,24},{20,28},{24,16},{28,20},{1,9},{5... | collective-permute-start | bytes 1474568 | tf_op jit(solution)/shard_map/ppermute | solution.py:844
  71.1 17.0 %collective-permute-start.17 = (bf16[384,640]{1,0:T(8,128)(2,1)S(1)}, bf16[384,640]{1,0:T(8,128)(2,1)S(1)}, u32[]{:S(2)}, u32[]{:S(2)}) collective-permute-start(bf16[384,640]{1,0:T(8,128)(2,1)S(1)} %constant_dynamic-update-slice_fusion.3.refs_3_), channel_id=1, source_target_pairs={{0,1},{1,0},{2,3},{3,2},{4,5},{5,4},{6,7},{7,6},{8,9},{9,8},{10,11... | collective-permute-start | bytes 1474568 | tf_op jit(solution)/shard_map/ppermute | solution.py:844
  71.2 16.3 %collective-permute-start.15 = (bf16[384,640]{1,0:T(8,128)(2,1)S(1)}, bf16[384,640]{1,0:T(8,128)(2,1)S(1)}, u32[]{:S(2)}, u32[]{:S(2)}) collective-permute-start(bf16[384,640]{1,0:T(8,128)(2,1)S(1)} %constant_dynamic-update-slice_fusion.3.refs_3_), channel_id=1, source_target_pairs={{0,4},{4,0},{8,12},{12,8},{16,20},{20,16},{24,28},{28,24},{1,5},{5... | collective-permute-start | bytes 1474568 | tf_op jit(solution)/shard_map/ppermute | solution.py:844
  71.8 15.7 %collective-permute-start.16 = (bf16[64,2176]{1,0:T(8,128)(2,1)S(1)}, bf16[64,2176]{1,0:T(8,128)(2,1)S(1)}, u32[]{:S(2)}, u32[]{:S(2)}) collective-permute-start(bf16[64,2176]{1,0:T(8,128)(2,1)S(1)} %pad_maximum_fusion.9), channel_id=1, source_target_pairs={{0,16},{4,20},{8,24},{12,28},{16,0},{20,4},{24,8},{28,12},{1,17},{... | collective-permute-start | bytes 835592 | tf_op jit(solution)/shard_map/ppermute | solution.py:844
  87.5 16.5 %collective-permute-start.20 = (bf16[128,2176]{1,0:T(8,128)(2,1)S(1)}, bf16[128,2176]{1,0:T(8,128)(2,1)S(1)}, u32[]{:S(2)}, u32[]{:S(2)}) collective-permute-start(bf16[128,2176]{1,0:T(8,128)(2,1)S(1)} %constant_dynamic-update-slice_fusion.7.refs_3_), channel_id=1, source_target_pairs={{0,1},{1,0},{2,3},{3,2},{4,5},{5,4},{6,7},{7,6},{8,9},{9,8},{10,11... | collective-permute-start | bytes 1671176 | tf_op jit(solution)/shard_map/ppermute | solution.py:844
  88.1 15.8 %collective-permute-start.19 = (bf16[128,2176]{1,0:T(8,128)(2,1)S(1)}, bf16[128,2176]{1,0:T(8,128)(2,1)S(1)}, u32[]{:S(2)}, u32[]{:S(2)}) collective-permute-start(bf16[128,2176]{1,0:T(8,128)(2,1)S(1)} %constant_dynamic-update-slice_fusion.7.refs_3_), channel_id=1, source_target_pairs={{0,8},{4,12},{8,0},{12,4},{16,24},{20,28},{24,16},{28,20},{1,9},{5... | collective-permute-start | bytes 1671176 | tf_op jit(solution)/shard_map/ppermute | solution.py:844
  137.0 15.3 %collective-permute-start.28 = (bf16[128,1024]{1,0:T(8,128)(2,1)S(1)}, bf16[128,1024]{1,0:T(8,128)(2,1)S(1)}, u32[]{:S(2)}, u32[]{:S(2)}) collective-permute-start(bf16[128,1024]{1,0:T(8,128)(2,1)S(1)} %slice.227), channel_id=1, source_target_pairs={{0,4},{4,0},{8,12},{12,8},{16,20},{20,16},{24,28},{28,24},{1,5},{5... | collective-permute-start | bytes 786440 | tf_op jit(solution)/shard_map/ppermute | solution.py:844
  138.6 13.8 %collective-permute-start.27 = (bf16[128,1024]{1,0:T(8,128)(2,1)S(1)}, bf16[128,1024]{1,0:T(8,128)(2,1)S(1)}, u32[]{:S(2)}, u32[]{:S(2)}) collective-permute-start(bf16[128,1024]{1,0:T(8,128)(2,1)S(1)} %slice.226), channel_id=1, source_target_pairs={{0,4},{4,0},{8,12},{12,8},{16,20},{20,16},{24,28},{28,24},{1,5},{5... | collective-permute-start | bytes 786440 | tf_op jit(solution)/shard_map/ppermute | solution.py:844
  153.7 15.6 %collective-permute-start.31 = (bf16[128,1024]{1,0:T(8,128)(2,1)S(1)}, bf16[128,1024]{1,0:T(8,128)(2,1)S(1)}, u32[]{:S(2)}, u32[]{:S(2)}) collective-permute-start(bf16[128,1024]{1,0:T(8,128)(2,1)S(1)} %slice.229), channel_id=1, source_target_pairs={{0,4},{4,0},{8,12},{12,8},{16,20},{20,16},{24,28},{28,24},{1,5},{5... | collective-permute-start | bytes 786440 | tf_op jit(solution)/shard_map/ppermute | solution.py:844
  155.3 14.0 %collective-permute-start.32 = (bf16[128,1024]{1,0:T(8,128)(2,1)S(1)}, bf16[128,1024]{1,0:T(8,128)(2,1)S(1)}, u32[]{:S(2)}, u32[]{:S(2)}) collective-permute-start(bf16[128,1024]{1,0:T(8,128)(2,1)S(1)} %add_convert_fusion.40), channel_id=1, source_target_pairs={{0,2},{2,0},{1,3},{3,1},{4,6},{6,4},{5,7},{7,5},{8,10},{10,8},{9,1... | collective-permute-start | bytes 786440 | tf_op jit(solution)/shard_map/ppermute | solution.py:844
  156.9 14.1 %collective-permute-start.34 = (bf16[128,1408]{1,0:T(8,128)(2,1)S(1)}, bf16[128,1408]{1,0:T(8,128)(2,1)S(1)}, u32[]{:S(2)}, u32[]{:S(2)}) collective-permute-start(bf16[128,1408]{1,0:T(8,128)(2,1)S(1)} %slice.232), channel_id=1, source_target_pairs={{0,2},{2,0},{1,3},{3,1},{4,6},{6,4},{5,7},{7,5},{8,10},{10,8},{9,1... | collective-permute-start | bytes 1081352 | tf_op jit(solution)/shard_map/ppermute | solution.py:844
  173.6 18.9 %collective-permute-start.43 = (bf16[64,1536]{1,0:T(8,128)(2,1)S(1)}, bf16[64,1536]{1,0:T(8,128)(2,1)S(1)}, u32[]{:S(2)}, u32[]{:S(2)}) collective-permute-start(bf16[64,1536]{1,0:T(8,128)(2,1)S(1)} %slice.240), channel_id=1, source_target_pairs={{0,2},{2,0},{1,3},{3,1},{4,6},{6,4},{5,7},{7,5},{8,10},{10,8},{9,1... | collective-permute-start | bytes 589832 | tf_op jit(solution)/shard_map/ppermute | solution.py:844
  175.0 17.5 %collective-permute-start.42 = (bf16[2,64,1024]{2,1,0:T(8,128)(2,1)S(1)}, bf16[2,64,1024]{2,1,0:T(8,128)(2,1)S(1)}, u32[]{:S(2)}, u32[]{:S(2)}) collective-permute-start(bf16[2,64,1024]{2,1,0:T(8,128)(2,1)S(1)} %fusion.3), channel_id=1, source_target_pairs={{0,8},{4,12},{8,0},{12,4},{16,24},{20,28},{24,16},{28,20},{1,9},{5... | collective-permute-start | bytes 786440 | tf_op jit(solution)/shard_map/ppermute | solution.py:844
  176.9 15.6 %collective-permute-start.41 = (bf16[192,768]{1,0:T(8,128)(2,1)S(1)}, bf16[192,768]{1,0:T(8,128)(2,1)S(1)}, u32[]{:S(2)}, u32[]{:S(2)}) collective-permute-start(bf16[192,768]{1,0:T(8,128)(2,1)S(1)} %slice.235), channel_id=1, source_target_pairs={{0,4},{4,0},{8,12},{12,8},{16,20},{20,16},{24,28},{28,24},{1,5},{5... | collective-permute-start | bytes 884744 | tf_op jit(solution)/shard_map/ppermute | solution.py:844
  178.1 14.3 %collective-permute-start.40 = (bf16[192,768]{1,0:T(8,128)(2,1)S(1)}, bf16[192,768]{1,0:T(8,128)(2,1)S(1)}, u32[]{:S(2)}, u32[]{:S(2)}) collective-permute-start(bf16[192,768]{1,0:T(8,128)(2,1)S(1)} %slice.234), channel_id=1, source_target_pairs={{0,4},{4,0},{8,12},{12,8},{16,20},{20,16},{24,28},{28,24},{1,5},{5... | collective-permute-start | bytes 884744 | tf_op jit(solution)/shard_map/ppermute | solution.py:844
  179.1 14.3 %collective-permute-start.39 = (bf16[384,768]{1,0:T(8,128)(2,1)S(1)}, bf16[384,768]{1,0:T(8,128)(2,1)S(1)}, u32[]{:S(2)}, u32[]{:S(2)}) collective-permute-start(bf16[384,768]{1,0:T(8,128)(2,1)S(1)} %add_convert_fusion.15), channel_id=1, source_target_pairs={{0,2},{2,0},{1,3},{3,1},{4,6},{6,4},{5,7},{7,5},{8,10},{10,8},{9,1... | collective-permute-start | bytes 1769480 | tf_op jit(solution)/shard_map/ppermute | solution.py:844
  199.6 16.0 %collective-permute-start.49 = (bf16[192,768]{1,0:T(8,128)(2,1)S(1)}, bf16[192,768]{1,0:T(8,128)(2,1)S(1)}, u32[]{:S(2)}, u32[]{:S(2)}) collective-permute-start(bf16[192,768]{1,0:T(8,128)(2,1)S(1)} %slice.246), channel_id=1, source_target_pairs={{0,4},{4,0},{8,12},{12,8},{16,20},{20,16},{24,28},{28,24},{1,5},{5... | collective-permute-start | bytes 884744 | tf_op jit(solution)/shard_map/ppermute | solution.py:844
  200.4 15.2 %collective-permute-start.50 = (bf16[192,768]{1,0:T(8,128)(2,1)S(1)}, bf16[192,768]{1,0:T(8,128)(2,1)S(1)}, u32[]{:S(2)}, u32[]{:S(2)}) collective-permute-start(bf16[192,768]{1,0:T(8,128)(2,1)S(1)} %add_convert_fusion.35), channel_id=1, source_target_pairs={{0,2},{2,0},{1,3},{3,1},{4,6},{6,4},{5,7},{7,5},{8,10},{10,8},{9,1... | collective-permute-start | bytes 884744 | tf_op jit(solution)/shard_map/ppermute | solution.py:844
  203.5 17.5 %collective-permute-start.52 = (bf16[192,768]{1,0:T(8,128)(2,1)S(1)}, bf16[192,768]{1,0:T(8,128)(2,1)S(1)}, u32[]{:S(2)}, u32[]{:S(2)}) collective-permute-start(bf16[192,768]{1,0:T(8,128)(2,1)S(1)} %slice.248), channel_id=1, source_target_pairs={{0,4},{4,0},{8,12},{12,8},{16,20},{20,16},{24,28},{28,24},{1,5},{5... | collective-permute-start | bytes 884744 | tf_op jit(solution)/shard_map/ppermute | solution.py:844
  205.0 16.6 %collective-permute-start.51 = (bf16[384,768]{1,0:T(8,128)(2,1)S(1)}, bf16[384,768]{1,0:T(8,128)(2,1)S(1)}, u32[]{:S(2)}, u32[]{:S(2)}) collective-permute-start(bf16[384,768]{1,0:T(8,128)(2,1)S(1)} %add_convert_fusion.10), channel_id=1, source_target_pairs={{0,2},{2,0},{1,3},{3,1},{4,6},{6,4},{5,7},{7,5},{8,10},{10,8},{9,1... | collective-permute-start | bytes 1769480 | tf_op jit(solution)/shard_map/ppermute | solution.py:844
  241.2 22.5 %collective-permute-start.64 = (bf16[384,896]{1,0:T(8,128)(2,1)S(1)}, bf16[384,896]{1,0:T(8,128)(2,1)S(1)}, u32[]{:S(2)}, u32[]{:S(2)}) collective-permute-start(bf16[384,896]{1,0:T(8,128)(2,1)S(1)} %slice.260), channel_id=1, source_target_pairs={{0,4},{4,0},{8,12},{12,8},{16,20},{20,16},{24,28},{28,24},{1,5},{5... | collective-permute-start | bytes 2064392 | tf_op jit(solution)/shard_map/ppermute | solution.py:844
  243.1 20.6 %collective-permute-start.65 = (bf16[384,768]{1,0:T(8,128)(2,1)S(1)}, bf16[384,768]{1,0:T(8,128)(2,1)S(1)}, u32[]{:S(2)}, u32[]{:S(2)}) collective-permute-start(bf16[384,768]{1,0:T(8,128)(2,1)S(1)} %slice.261), channel_id=1, source_target_pairs={{0,2},{2,0},{1,3},{3,1},{4,6},{6,4},{5,7},{7,5},{8,10},{10,8},{9,1... | collective-permute-start | bytes 1769480 | tf_op jit(solution)/shard_map/ppermute | solution.py:844
  267.3 17.6 %collective-permute-start.71 = (bf16[4,64,1024]{2,1,0:T(8,128)(2,1)S(1)}, bf16[4,64,1024]{2,1,0:T(8,128)(2,1)S(1)}, u32[]{:S(2)}, u32[]{:S(2)}) collective-permute-start(bf16[4,64,1024]{2,1,0:T(8,128)(2,1)S(1)} %pad_maximum_fusion.1.refs_1_), channel_id=1, source_target_pairs={{0,4},{4,0},{8,12},{12,8},{16,20},{20,16},{24,28},{28,24},{1,5},{5... | collective-permute-start | bytes 1572872 | tf_op jit(solution)/shard_map/ppermute | solution.py:844
  274.5 23.7 %collective-permute-start.72 = (bf16[96,1664]{1,0:T(8,128)(2,1)S(1)}, bf16[96,1664]{1,0:T(8,128)(2,1)S(1)}, u32[]{:S(2)}, u32[]{:S(2)}) collective-permute-start(bf16[96,1664]{1,0:T(8,128)(2,1)S(1)} %pad_maximum_fusion.4), channel_id=1, source_target_pairs={{0,8},{4,12},{8,0},{12,4},{16,24},{20,28},{24,16},{28,20},{1,9},{5... | collective-permute-start | bytes 958472 | tf_op jit(solution)/shard_map/ppermute | solution.py:844
  276.6 14.6 %collective-permute-start.80 = (bf16[2,96,768]{2,1,0:T(8,128)(2,1)S(1)}, bf16[2,96,768]{2,1,0:T(8,128)(2,1)S(1)}, u32[]{:S(2)}, u32[]{:S(2)}) collective-permute-start(bf16[2,96,768]{2,1,0:T(8,128)(2,1)S(1)} %pad_maximum_fusion.7.refs_1_), channel_id=1, source_target_pairs={{0,4},{4,0},{8,12},{12,8},{16,20},{20,16},{24,28},{28,24},{1,5},{5... | collective-permute-start | bytes 884744 | tf_op jit(solution)/shard_map/ppermute | solution.py:844
  277.8 23.6 %collective-permute-start.79 = (bf16[2,96,768]{2,1,0:T(8,128)(2,1)S(1)}, bf16[2,96,768]{2,1,0:T(8,128)(2,1)S(1)}, u32[]{:S(2)}, u32[]{:S(2)}) collective-permute-start(bf16[2,96,768]{2,1,0:T(8,128)(2,1)S(1)} %pad_maximum_fusion.7.refs_1_), channel_id=1, source_target_pairs={{0,8},{4,12},{8,0},{12,4},{16,24},{20,28},{24,16},{28,20},{1,9},{5... | collective-permute-start | bytes 884744 | tf_op jit(solution)/shard_map/ppermute | solution.py:844
  284.3 13.9 %collective-permute-start.73 = (f32[1,6400]{1,0:T(1,128)S(1)}, f32[1,6400]{1,0:T(1,128)S(1)}, u32[]{:S(2)}, u32[]{:S(2)}) collective-permute-start(f32[1,6400]{1,0:T(1,128)S(1)} %add.197), channel_id=1, source_target_pairs={{0,8},{4,12},{8,0},{12,4},{16,24},{20,28},{24,16},{28,20},{1,9},{5... | collective-permute-start | bytes 76808 | tf_op jit(solution)/shard_map/ppermute | solution.py:844
  284.9 16.7 %collective-permute-start.85 = (bf16[4,96,768]{2,1,0:T(8,128)(2,1)S(1)}, bf16[4,96,768]{2,1,0:T(8,128)(2,1)S(1)}, u32[]{:S(2)}, u32[]{:S(2)}) collective-permute-start(bf16[4,96,768]{2,1,0:T(8,128)(2,1)S(1)} %pad_maximum_fusion.refs_1_), channel_id=1, source_target_pairs={{0,4},{4,0},{8,12},{12,8},{16,20},{20,16},{24,28},{28,24},{1,5},{5... | collective-permute-start | bytes 1769480 | tf_op jit(solution)/shard_map/ppermute | solution.py:844
  (91 other events, 633.3 us)
Sparse Core Ops, SparseCore 0:
  13.2 68.0 all-gather.2
  83.4 35.2 all-gather.4

commit v5 on v4

--- a/solution.py
+++ b/solution.py
@@ -775,26 +775,29 @@
         target[...] = dot_nn(pick, hi) + dot_nn(pick, mid) + dot_nn(pick, low)
 
 
-def out_feed_body(part, count, *refs):
-    place, arrays = refs[0], refs[1 : 1 + count]
+def out_feed_body(counts, *refs):
+    place = refs[0]
     g_up, g_down, up, turned, down, sems = refs[-6:]
-    units = up.shape[1]
-    for k, ref in enumerate(arrays):
-        block = ref.shape[1] // 2
-        for m in range(ref.shape[0]):
-            dp = place[3] ^ feed_block(ref.shape[0] * k + m)
-            at = pl.multiple_of(dp * block, block)
-            rows = ref[m].astype(F32)
-            up[pl.ds(at, block), :] = rows[:block]
-            turned[pl.ds(at, block), :] = rows[block:]
-    here = pl.ds(part * units, units)
-    first = pltpu.make_async_copy(up, g_up.at[:, here], sems.at[0])
-    first.start()
-    down[...] = turned[...].T
-    second = pltpu.make_async_copy(down, g_down.at[here, :], sems.at[1])
-    second.start()
-    first.wait()
-    second.wait()
+    units = up.shape[2]
+    copies, first = [], 1
+    for part, count in enumerate(counts):
+        for k, ref in enumerate(refs[first : first + count]):
+            block = ref.shape[1] // 2
+            for m in range(ref.shape[0]):
+                dp = place[3] ^ feed_block(ref.shape[0] * k + m)
+                at = pl.multiple_of(dp * block, block)
+                rows = ref[m].astype(F32)
+                up[part, pl.ds(at, block), :] = rows[:block]
+                turned[pl.ds(at, block), :] = rows[block:]
+        first += count
+        here = pl.ds(part * units, units)
+        copies.append(pltpu.make_async_copy(up.at[part], g_up.at[:, here], sems.at[2 * part]))
+        copies[-1].start()
+        down[part] = turned[...].T
+        copies.append(pltpu.make_async_copy(down.at[part], g_down.at[here, :], sems.at[2 * part + 1]))
+        copies[-1].start()
+    for copy in copies:
+        copy.wait()
 
 
 def out_dec_body(mine, theirs, g_in, g_out, g_gains, g_biases, g_token, g_embed):
@@ -1236,22 +1239,20 @@
         sentence = Sentence(place, tokens_in, mask_pos, cotangent)
 
     def feed_out(rows, units, halves):
-        outs = []
-        for part, pair in enumerate(halves):
-            count = units // len(halves)
-            outs = pl.pallas_call(
-                partial(out_feed_body, part, len(pair)),
-                out_shape=[jax.ShapeDtypeStruct((rows, units), F32), jax.ShapeDtypeStruct((units, rows), F32)],
-                in_specs=[pl.BlockSpec(memory_space=pltpu.SMEM)]
-                + [pl.BlockSpec(memory_space=pltpu.VMEM)] * len(pair) + [pl.BlockSpec(memory_space=pltpu.HBM)] * len(outs),
-                out_specs=[pl.BlockSpec(memory_space=pltpu.HBM)] * 2,
-                scratch_shapes=[pltpu.VMEM((rows, count), F32), pltpu.VMEM((rows, count), F32),
-                                pltpu.VMEM((count, rows), F32), pltpu.SemaphoreType.DMA((2,))],
-                input_output_aliases={len(pair) + 1: 0, len(pair) + 2: 1} if outs else {},
-                compiler_params=vmem([((rows, count), F32)] * 3),
-                cost_estimate=cost(LAST),
-            )(place, *pair, *outs)
-        return outs
+        parts = len(halves)
+        count = units // parts
+        arrays = [v for part in halves for v in part]
+        return pl.pallas_call(
+            partial(out_feed_body, tuple(len(part) for part in halves)),
+            out_shape=[jax.ShapeDtypeStruct((rows, units), F32), jax.ShapeDtypeStruct((units, rows), F32)],
+            in_specs=[pl.BlockSpec(memory_space=pltpu.SMEM)]
+            + [pl.BlockSpec(memory_space=pltpu.VMEM)] * len(arrays),
+            out_specs=[pl.BlockSpec(memory_space=pltpu.HBM)] * 2,
+            scratch_shapes=[pltpu.VMEM((parts, rows, count), F32), pltpu.VMEM((rows, count), F32),
+                            pltpu.VMEM((parts, count, rows), F32), pltpu.SemaphoreType.DMA((2 * parts,))],
+            compiler_params=vmem([((rows, units), F32)] * 3),
+            cost_estimate=cost(LAST),
+        )(place, *arrays)
 
     def dec_out():
         n, n2 = width // 32, width2 // 32

time: 321 us -> 321 us (level)
    pallas_call x3 -> x2, Pallas kernels: 7.11 us -> 5.52 us  [feed_out(): pl.pallas_call(partial(out_feed_body, tuple((len(part) for part in halves...]
where the time goes in v5:
time: 321 us; the launch traced here: 317 us
  Pallas kernels  117 us (36%)
  waiting for transfers between devices  88 us (27%)
  starting transfers between devices  80.2 us (25%)
  between operations  17.1 us (5%)
  other arithmetic  7.8 us (2%)
  local copies, waits for them, and re-layouts  7.23 us (2%)
    pallas_call x17, Pallas kernels, call(): pl.pallas_call(kernel, out_shape=[pltpu.HBM(s, d) if k in keep else jax.S...  111 us
    ppermute x86, waiting for transfers between devices, swap(): lax.ppermute(v, axis, [(i, i ^ distance) for i in range(lax.axis_size(axi...  85.6 us
    ppermute x86, starting transfers between devices, swap(): lax.ppermute(v, axis, [(i, i ^ distance) for i in range(lax.axis_size(axi...  80.1 us
  transfers between devices with their start and end apart: 88, of which 37 were waited for; matrix products, arithmetic and copies ran while one was open for 3% of the time, Pallas kernels for 31%

profile of v5, /device:TPU:0, one launch (start us, length us, event | category | flops | bytes accessed | tf_op | source)
XLA Modules:
  0.0 317.1 jit_solution(12671528958973363985)
XLA Ops:
  9.8 3.3 %shard_map.368 = bf16[784,1536]{1,0:T(8,128)(2,1)} custom-call(bf16[384,1536]{1,0:T(8,128)(2,1)} %refs_0_.1, bf16[1,1536]{1,0:T(2,128)(2,1)} %broadcast_in_dim.16.refs_1_, bf16[1536,384]{1,0:T(8,128)(2,1)} %refs_2_.4, bf16[1,384]{1,0:T(2,128)(2,1)} %broadcast_in_dim.17.refs_3_), custom_call_target="tpu_custom_call" | custom-call | flops 2000000000 | bytes 6000000 | tf_op jit(solution)/shard_map/pallas_call | solution.py:85
  14.4 3.0 collective-permute-start.2
  23.8 3.2 collective-permute-start.1
  28.1 2.4 shard_map.371
  30.6 6.9 %collective-permute-done.1 = bf16[96,1280]{1,0:T(8,128)(2,1)S(1)} collective-permute-done((bf16[96,1280]{1,0:T(8,128)(2,1)S(1)}, bf16[96,1280]{1,0:T(8,128)(2,1)S(1)}, u32[]{:S(2)}, u32[]{:S(2)}) %collective-permute-start.1) | collective-permute-done | bytes 245792 | tf_op jit(solution)/shard_map/ppermute | solution.py:847
  41.9 2.5 collective-permute-done.5
  48.2 3.4 %collective-permute-start.8 = (bf16[96,640]{1,0:T(8,128)(2,1)S(1)}, bf16[96,640]{1,0:T(8,128)(2,1)S(1)}, u32[]{:S(2)}, u32[]{:S(2)}) collective-permute-start(bf16[96,640]{1,0:T(8,128)(2,1)S(1)} %pad_maximum_fusion.16), channel_id=1, source_target_pairs={{0,16},{4,20},{8,24},{12,28},{16,0},{20,4},{24,8},{28,12},{1,17},{... | collective-permute-start | bytes 368648 | tf_op jit(solution)/shard_map/ppermute | solution.py:847
  53.2 6.7 %collective-permute-done.8 = bf16[96,640]{1,0:T(8,128)(2,1)S(1)} collective-permute-done((bf16[96,640]{1,0:T(8,128)(2,1)S(1)}, bf16[96,640]{1,0:T(8,128)(2,1)S(1)}, u32[]{:S(2)}, u32[]{:S(2)}) %collective-permute-start.8) | collective-permute-done | bytes 122912 | tf_op jit(solution)/shard_map/ppermute | solution.py:847
  60.9 3.5 %collective-permute-start.13 = (bf16[192,640]{1,0:T(8,128)(2,1)S(1)}, bf16[192,640]{1,0:T(8,128)(2,1)S(1)}, u32[]{:S(2)}, u32[]{:S(2)}) collective-permute-start(bf16[192,640]{1,0:T(8,128)(2,1)S(1)} %pad_maximum_fusion.13), channel_id=1, source_target_pairs={{0,8},{4,12},{8,0},{12,4},{16,24},{20,28},{24,16},{28,20},{1,9},{5... | collective-permute-start | bytes 737288 | tf_op jit(solution)/shard_map/ppermute | solution.py:847
  65.0 6.0 %collective-permute-done.13 = bf16[192,640]{1,0:T(8,128)(2,1)S(1)} collective-permute-done((bf16[192,640]{1,0:T(8,128)(2,1)S(1)}, bf16[192,640]{1,0:T(8,128)(2,1)S(1)}, u32[]{:S(2)}, u32[]{:S(2)}) %collective-permute-start.13) | collective-permute-done | bytes 245792 | tf_op jit(solution)/shard_map/ppermute | solution.py:847
  72.6 10.0 %shard_map.367 = (bf16[400,768]{1,0:T(8,128)(2,1)}, bf16[400,2304]{1,0:T(8,128)(2,1)}, bf16[768,400]{1,0:T(8,128)(2,1)}, f32[6,800]{1,0:T(8,128)}, bf16[768,2304]{1,0:T(8,128)(2,1)}, /*index=5*/f32[16,768]{1,0:T(8,128)}) custom-call(s32[8]{0:T(128)S(1)} %stack.26.refs_0_, bf16[400,768]{1,0:T(8,128)(2,1)S(1)} %get-tuple-element.310.refs_1_.refs_2_, ...), custom_call_target="tpu_custom_call" | custom-call | flops 12000000000 | bytes 36000000 | tf_op jit(solution)/shard_map/pallas_call | solution.py:85
  82.7 4.8 %collective-permute-done.16 = bf16[64,2176]{1,0:T(8,128)(2,1)S(1)} collective-permute-done((bf16[64,2176]{1,0:T(8,128)(2,1)S(1)}, bf16[64,2176]{1,0:T(8,128)(2,1)S(1)}, u32[]{:S(2)}, u32[]{:S(2)}) %collective-permute-start.16) | collective-permute-done | bytes 278560 | tf_op jit(solution)/shard_map/ppermute | solution.py:847
  89.5 14.4 %shard_map.369 = (f32[400,768]{1,0:T(8,128)}, bf16[400,768]{1,0:T(8,128)(2,1)}, bf16[400,3072]{1,0:T(8,128)(2,1)}, bf16[400,3072]{1,0:T(8,128)(2,1)}, bf16[400,7...) custom-call(s32[8]{0:T(128)S(1)} %stack.26.refs_0_, bf16[400,768]{1,0:T(8,128)(2,1)} %copy-done.5, ...), custom_call_target="tpu_custom_call" | custom-call | flops 15000000512 | bytes 45000000 | tf_op jit(solution)/shard_map/pallas_call | solution.py:85
  106.7 9.6 %shard_map.370 = (f32[400,512]{1,0:T(8,128)}, bf16[400,512]{1,0:T(8,128)(2,1)}, bf16[400,1536]{1,0:T(8,128)(2,1)}, bf16[512,400]{1,0:T(8,128)(2,1)}, f32[4,1600]...) custom-call(s32[8]{0:T(128)S(1)} %stack.26.refs_0_, ...), custom_call_target="tpu_custom_call" | custom-call | flops 11000000512 | bytes 33000000 | tf_op jit(solution)/shard_map/pallas_call | solution.py:85
  116.4 2.4 all-gather.5.cloned.1.call-done.refs_6_
  118.7 13.5 %shard_map.372 = (f32[400,512]{1,0:T(8,128)}, bf16[256,1024]{1,0:T(8,128)(2,1)S(1)}, bf16[256,1024]{1,0:T(8,128)(2,1)S(1)}, bf16[256,1024]{1,0:T(8,128)(2,1)S(1)...) custom-call(s32[8]{0:T(128)S(1)} %stack.26.refs_0_, ...), custom_call_target="tpu_custom_call" | custom-call | flops 16000000000 | bytes 48000000 | tf_op jit(solution)/shard_map/pallas_call | solution.py:85
  139.7 12.6 %shard_map.373 = (bf16[256,1536]{1,0:T(8,128)(2,1)S(1)}, bf16[256,1536]{1,0:T(8,128)(2,1)S(1)}, bf16[256,1408]{1,0:T(8,128)(2,1)S(1)}, bf16[256,1408]{1,0:T(8,12...) custom-call(s32[8]{0:T(128)S(1)} %stack.26.refs_0_, bf16[400,1536]{1,0:T(8,128)(2,1)S(1)} %copy-done.13, ...), custom_call_target="tpu_custom_call" | custom-call | flops 16000000000 | bytes 48000000 | tf_op jit(solution)/shard_map/pallas_call | solution.py:85
  159.5 9.8 %shard_map.374 = (bf16[384,768]{1,0:T(8,128)(2,1)S(1)}, bf16[384,768]{1,0:T(8,128)(2,1)S(1)}, bf16[384,768]{1,0:T(8,128)(2,1)S(1)}, bf16[384,768]{1,0:T(8,128)(2...) custom-call(s32[8]{0:T(128)S(1)} %stack.26.refs_0_, ...), custom_call_target="tpu_custom_call" | custom-call | flops 14000000000 | bytes 42000000 | tf_op jit(solution)/shard_map/pallas_call | solution.py:85
  180.3 12.1 %shard_map.375 = (bf16[384,768]{1,0:T(8,128)(2,1)S(1)}, bf16[384,768]{1,0:T(8,128)(2,1)S(1)}, bf16[384,768]{1,0:T(8,128)(2,1)S(1)}, bf16[384,768]{1,0:T(8,128)(2...) custom-call(s32[8]{0:T(128)S(1)} %stack.26.refs_0_, ...), custom_call_target="tpu_custom_call" | custom-call | flops 19000000512 | bytes 57000000 | tf_op jit(solution)/shard_map/pallas_call | solution.py:85
  193.6 2.5 collective-permute-start.54
  206.5 9.1 %shard_map.376.refs_1_ = bf16[400,2304]{1,0:T(8,128)(2,1)S(1)} custom-call(s32[8]{0:T(128)S(1)} %stack.26.refs_0_, bf16[400,2304]{1,0:T(8,128)(2,1)S(1)} %copy-done.10, bf16[400,768]{1,0:T(8,128)(2,1)S(1)} %get-tuple-element.465.refs_2_, f32[6,800]{1,0:T(8,128)S(1)} %copy-done.25), custom_call_target="tpu_custom_call" | custom-call | flops 12000000000 | bytes 36000000 | tf_op jit(solution)/shard_map/pallas_call | solution.py:85
  215.8 5.2 %collective-permute-done.52 = bf16[192,768]{1,0:T(8,128)(2,1)S(1)} collective-permute-done((bf16[192,768]{1,0:T(8,128)(2,1)S(1)}, bf16[192,768]{1,0:T(8,128)(2,1)S(1)}, u32[]{:S(2)}, u32[]{:S(2)}) %collective-permute-start.52) | collective-permute-done | bytes 294944 | tf_op jit(solution)/shard_map/ppermute | solution.py:847
  222.4 2.4 collective-permute-start.59
  229.0 5.8 %shard_map.377 = (bf16[768,896]{1,0:T(8,128)(2,1)S(1)}, bf16[768,896]{1,0:T(8,128)(2,1)S(1)}, bf16[768,768]{1,0:T(8,128)(2,1)S(1)}, bf16[768,768]{1,0:T(8,128)(2...) custom-call(s32[8]{0:T(128)S(1)} %stack.26.refs_0_, bf16[400,2304]{1,0:T(8,128)(2,1)S(1)} %shard_map.376.refs_1_, ...), custom_call_target="tpu_custom_call" | custom-call | flops 8999999488 | bytes 27000000 | tf_op jit(solution)/shard_map/pallas_call | solution.py:85
  246.6 4.7 %collective-permute-done.80 = bf16[2,96,768]{2,1,0:T(8,128)(2,1)S(1)} collective-permute-done((bf16[2,96,768]{2,1,0:T(8,128)(2,1)S(1)}, bf16[2,96,768]{2,1,0:T(8,128)(2,1)S(1)}, u32[]{:S(2)}, u32[]{:S(2)}) %collective-permute-start.80) | collective-permute-done | bytes 294944 | tf_op jit(solution)/shard_map/ppermute | solution.py:847
  252.3 5.6 %collective-permute-done.70 = bf16[2,64,1024]{2,1,0:T(8,128)(2,1)S(1)} collective-permute-done((bf16[2,64,1024]{2,1,0:T(8,128)(2,1)S(1)}, bf16[2,64,1024]{2,1,0:T(8,128)(2,1)S(1)}, u32[]{:S(2)}, u32[]{:S(2)}) %collective-permute-start.70) | collective-permute-done | bytes 262176 | tf_op jit(solution)/shard_map/ppermute | solution.py:847
  260.0 3.7 %shard_map.379 = (f32[529,512]{1,0:T(8,128)}, f32[529,768]{1,0:T(8,128)}) custom-call(s32[529,1]{1,0:T(8,128)S(1)} %get-tuple-element.507.refs_0_, f32[400,512]{1,0:T(8,128)S(1)} %copy-done, f32[400,768]{1,0:T(8,128)S(1)} %get-tuple-element.513.refs_2_), custom_call_target="tpu_custom_call" | custom-call | flops 10000000 | bytes 30000 | tf_op jit(solution)/shard_map/pallas_call | solution.py:85
  269.4 4.9 %collective-permute-done.82 = bf16[1,96,768]{2,1,0:T(8,128)(2,1)S(1)} collective-permute-done((bf16[1,96,768]{2,1,0:T(8,128)(2,1)S(1)}, bf16[1,96,768]{2,1,0:T(8,128)(2,1)S(1)}, u32[]{:S(2)}, u32[]{:S(2)}) %collective-permute-start.82) | collective-permute-done | bytes 147488 | tf_op jit(solution)/shard_map/ppermute | solution.py:847
  277.9 6.4 %collective-permute-done.78 = bf16[2,96,768]{2,1,0:T(8,128)(2,1)S(1)} collective-permute-done((bf16[2,96,768]{2,1,0:T(8,128)(2,1)S(1)}, bf16[2,96,768]{2,1,0:T(8,128)(2,1)S(1)}, u32[]{:S(2)}, u32[]{:S(2)}) %collective-permute-start.78) | collective-permute-done | bytes 294944 | tf_op jit(solution)/shard_map/ppermute | solution.py:847
  287.9 3.3 %collective-permute-done.84.refs_5_ = bf16[2,96,768]{2,1,0:T(8,128)(2,1)S(1)} collective-permute-done((bf16[2,96,768]{2,1,0:T(8,128)(2,1)S(1)}, bf16[2,96,768]{2,1,0:T(8,128)(2,1)S(1)}, u32[]{:S(2)}, u32[]{:S(2)}) %collective-permute-start.84) | collective-permute-done | bytes 294944 | tf_op jit(solution)/shard_map/ppermute | solution.py:847
  292.5 5.7 %collective-permute-done.73 = f32[1,6400]{1,0:T(1,128)S(1)} collective-permute-done((f32[1,6400]{1,0:T(1,128)S(1)}, f32[1,6400]{1,0:T(1,128)S(1)}, u32[]{:S(2)}, u32[]{:S(2)}) %collective-permute-start.73) | collective-permute-done | bytes 25632 | tf_op jit(solution)/shard_map/ppermute | solution.py:847
  301.6 3.2 %shard_map.382 = (f32[384,1536]{1,0:T(8,128)}, f32[1536,384]{1,0:T(8,128)}) custom-call(s32[8]{0:T(128)S(1)} %stack.26.refs_0_, bf16[4,96,768]{2,1,0:T(8,128)(2,1)S(1)} %pad_maximum_fusion.refs_1_, bf16[4,96,768]{2,1,0:T(8,128)(2,1)S(1)} %collective-permute-done.79.refs_2_, bf16[2,96,768]{2,1,0:T(8,128)(2,1)S(1)} %pad_maximum_fusion.8.refs_3_, ...), custom_call_target="tpu_custom_call" | custom-call | flops 10000000 | bytes 30000 | tf_op jit(solution)/shard_map/pallas_call | solution.py:1245
  (340 shorter events, 107.3 us)
Async XLA Ops:
  7.2 82.3 %all-gather.3.cloned.1.call-start = ((), (), s32[]{:S(2)}) async-start(), calls=%async_computation | async-start | bytes 12042240 | tf_op jit(solution)/shard_map/all_gather | solution.py:1201
  13.1 105.7 %all-gather.5.cloned.1.call-start = ((), (), s32[]{:S(2)}) async-start(), calls=%async_computation.1 | async-start | bytes 5406720 | tf_op jit(solution)/shard_map/all_gather | solution.py:1201
  14.4 16.2 %collective-permute-start.2 = (bf16[48,640]{1,0:T(8,128)(2,1)S(1)}, bf16[48,640]{1,0:T(8,128)(2,1)S(1)}, u32[]{:S(2)}, u32[]{:S(2)}) collective-permute-start(bf16[48,640]{1,0:T(8,128)(2,1)S(1)} %get-tuple-element.293), channel_id=1, source_target_pairs={{0,2},{2,0},{1,3},{3,1},{4,6},{6,4},{5,7},{7,5},{8,10},{10,8},{9,1... | collective-permute-start | bytes 184328 | tf_op jit(solution)/shard_map/ppermute | solution.py:847
  23.8 13.7 %collective-permute-start.1 = (bf16[96,1280]{1,0:T(8,128)(2,1)S(1)}, bf16[96,1280]{1,0:T(8,128)(2,1)S(1)}, u32[]{:S(2)}, u32[]{:S(2)}) collective-permute-start(bf16[96,1280]{1,0:T(8,128)(2,1)S(1)} %pad_maximum_fusion.12), channel_id=1, source_target_pairs={{0,16},{4,20},{8,24},{12,28},{16,0},{20,4},{24,8},{28,12},{1,17},{... | collective-permute-start | bytes 737288 | tf_op jit(solution)/shard_map/ppermute | solution.py:847
  45.8 14.8 %collective-permute-start.7 = (bf16[384,640]{1,0:T(8,128)(2,1)S(1)}, bf16[384,640]{1,0:T(8,128)(2,1)S(1)}, u32[]{:S(2)}, u32[]{:S(2)}) collective-permute-start(bf16[384,640]{1,0:T(8,128)(2,1)S(1)} %pad_maximum_fusion.3.refs_6_), channel_id=1, source_target_pairs={{0,8},{4,12},{8,0},{12,4},{16,24},{20,28},{24,16},{28,20},{1,9},{5... | collective-permute-start | bytes 1474568 | tf_op jit(solution)/shard_map/ppermute | solution.py:847
  71.1 17.0 %collective-permute-start.17 = (bf16[384,640]{1,0:T(8,128)(2,1)S(1)}, bf16[384,640]{1,0:T(8,128)(2,1)S(1)}, u32[]{:S(2)}, u32[]{:S(2)}) collective-permute-start(bf16[384,640]{1,0:T(8,128)(2,1)S(1)} %constant_dynamic-update-slice_fusion.3.refs_3_), channel_id=1, source_target_pairs={{0,1},{1,0},{2,3},{3,2},{4,5},{5,4},{6,7},{7,6},{8,9},{9,8},{10,11... | collective-permute-start | bytes 1474568 | tf_op jit(solution)/shard_map/ppermute | solution.py:847
  71.2 16.3 %collective-permute-start.15 = (bf16[384,640]{1,0:T(8,128)(2,1)S(1)}, bf16[384,640]{1,0:T(8,128)(2,1)S(1)}, u32[]{:S(2)}, u32[]{:S(2)}) collective-permute-start(bf16[384,640]{1,0:T(8,128)(2,1)S(1)} %constant_dynamic-update-slice_fusion.3.refs_3_), channel_id=1, source_target_pairs={{0,4},{4,0},{8,12},{12,8},{16,20},{20,16},{24,28},{28,24},{1,5},{5... | collective-permute-start | bytes 1474568 | tf_op jit(solution)/shard_map/ppermute | solution.py:847
  71.8 15.7 %collective-permute-start.16 = (bf16[64,2176]{1,0:T(8,128)(2,1)S(1)}, bf16[64,2176]{1,0:T(8,128)(2,1)S(1)}, u32[]{:S(2)}, u32[]{:S(2)}) collective-permute-start(bf16[64,2176]{1,0:T(8,128)(2,1)S(1)} %pad_maximum_fusion.9), channel_id=1, source_target_pairs={{0,16},{4,20},{8,24},{12,28},{16,0},{20,4},{24,8},{28,12},{1,17},{... | collective-permute-start | bytes 835592 | tf_op jit(solution)/shard_map/ppermute | solution.py:847
  87.5 16.5 %collective-permute-start.20 = (bf16[128,2176]{1,0:T(8,128)(2,1)S(1)}, bf16[128,2176]{1,0:T(8,128)(2,1)S(1)}, u32[]{:S(2)}, u32[]{:S(2)}) collective-permute-start(bf16[128,2176]{1,0:T(8,128)(2,1)S(1)} %constant_dynamic-update-slice_fusion.7.refs_3_), channel_id=1, source_target_pairs={{0,1},{1,0},{2,3},{3,2},{4,5},{5,4},{6,7},{7,6},{8,9},{9,8},{10,11... | collective-permute-start | bytes 1671176 | tf_op jit(solution)/shard_map/ppermute | solution.py:847
  88.1 15.8 %collective-permute-start.19 = (bf16[128,2176]{1,0:T(8,128)(2,1)S(1)}, bf16[128,2176]{1,0:T(8,128)(2,1)S(1)}, u32[]{:S(2)}, u32[]{:S(2)}) collective-permute-start(bf16[128,2176]{1,0:T(8,128)(2,1)S(1)} %constant_dynamic-update-slice_fusion.7.refs_3_), channel_id=1, source_target_pairs={{0,8},{4,12},{8,0},{12,4},{16,24},{20,28},{24,16},{28,20},{1,9},{5... | collective-permute-start | bytes 1671176 | tf_op jit(solution)/shard_map/ppermute | solution.py:847
  137.0 15.3 %collective-permute-start.28 = (bf16[128,1024]{1,0:T(8,128)(2,1)S(1)}, bf16[128,1024]{1,0:T(8,128)(2,1)S(1)}, u32[]{:S(2)}, u32[]{:S(2)}) collective-permute-start(bf16[128,1024]{1,0:T(8,128)(2,1)S(1)} %slice.227), channel_id=1, source_target_pairs={{0,4},{4,0},{8,12},{12,8},{16,20},{20,16},{24,28},{28,24},{1,5},{5... | collective-permute-start | bytes 786440 | tf_op jit(solution)/shard_map/ppermute | solution.py:847
  138.5 13.8 %collective-permute-start.27 = (bf16[128,1024]{1,0:T(8,128)(2,1)S(1)}, bf16[128,1024]{1,0:T(8,128)(2,1)S(1)}, u32[]{:S(2)}, u32[]{:S(2)}) collective-permute-start(bf16[128,1024]{1,0:T(8,128)(2,1)S(1)} %slice.226), channel_id=1, source_target_pairs={{0,4},{4,0},{8,12},{12,8},{16,20},{20,16},{24,28},{28,24},{1,5},{5... | collective-permute-start | bytes 786440 | tf_op jit(solution)/shard_map/ppermute | solution.py:847
  153.7 15.6 %collective-permute-start.31 = (bf16[128,1024]{1,0:T(8,128)(2,1)S(1)}, bf16[128,1024]{1,0:T(8,128)(2,1)S(1)}, u32[]{:S(2)}, u32[]{:S(2)}) collective-permute-start(bf16[128,1024]{1,0:T(8,128)(2,1)S(1)} %slice.229), channel_id=1, source_target_pairs={{0,4},{4,0},{8,12},{12,8},{16,20},{20,16},{24,28},{28,24},{1,5},{5... | collective-permute-start | bytes 786440 | tf_op jit(solution)/shard_map/ppermute | solution.py:847
  155.3 14.0 %collective-permute-start.32 = (bf16[128,1024]{1,0:T(8,128)(2,1)S(1)}, bf16[128,1024]{1,0:T(8,128)(2,1)S(1)}, u32[]{:S(2)}, u32[]{:S(2)}) collective-permute-start(bf16[128,1024]{1,0:T(8,128)(2,1)S(1)} %add_convert_fusion.40), channel_id=1, source_target_pairs={{0,2},{2,0},{1,3},{3,1},{4,6},{6,4},{5,7},{7,5},{8,10},{10,8},{9,1... | collective-permute-start | bytes 786440 | tf_op jit(solution)/shard_map/ppermute | solution.py:847
  156.9 14.1 %collective-permute-start.34 = (bf16[128,1408]{1,0:T(8,128)(2,1)S(1)}, bf16[128,1408]{1,0:T(8,128)(2,1)S(1)}, u32[]{:S(2)}, u32[]{:S(2)}) collective-permute-start(bf16[128,1408]{1,0:T(8,128)(2,1)S(1)} %slice.232), channel_id=1, source_target_pairs={{0,2},{2,0},{1,3},{3,1},{4,6},{6,4},{5,7},{7,5},{8,10},{10,8},{9,1... | collective-permute-start | bytes 1081352 | tf_op jit(solution)/shard_map/ppermute | solution.py:847
  173.6 18.9 %collective-permute-start.43 = (bf16[64,1536]{1,0:T(8,128)(2,1)S(1)}, bf16[64,1536]{1,0:T(8,128)(2,1)S(1)}, u32[]{:S(2)}, u32[]{:S(2)}) collective-permute-start(bf16[64,1536]{1,0:T(8,128)(2,1)S(1)} %slice.240), channel_id=1, source_target_pairs={{0,2},{2,0},{1,3},{3,1},{4,6},{6,4},{5,7},{7,5},{8,10},{10,8},{9,1... | collective-permute-start | bytes 589832 | tf_op jit(solution)/shard_map/ppermute | solution.py:847
  174.9 17.5 %collective-permute-start.42 = (bf16[2,64,1024]{2,1,0:T(8,128)(2,1)S(1)}, bf16[2,64,1024]{2,1,0:T(8,128)(2,1)S(1)}, u32[]{:S(2)}, u32[]{:S(2)}) collective-permute-start(bf16[2,64,1024]{2,1,0:T(8,128)(2,1)S(1)} %fusion.3), channel_id=1, source_target_pairs={{0,8},{4,12},{8,0},{12,4},{16,24},{20,28},{24,16},{28,20},{1,9},{5... | collective-permute-start | bytes 786440 | tf_op jit(solution)/shard_map/ppermute | solution.py:847
  176.9 15.6 %collective-permute-start.41 = (bf16[192,768]{1,0:T(8,128)(2,1)S(1)}, bf16[192,768]{1,0:T(8,128)(2,1)S(1)}, u32[]{:S(2)}, u32[]{:S(2)}) collective-permute-start(bf16[192,768]{1,0:T(8,128)(2,1)S(1)} %slice.235), channel_id=1, source_target_pairs={{0,4},{4,0},{8,12},{12,8},{16,20},{20,16},{24,28},{28,24},{1,5},{5... | collective-permute-start | bytes 884744 | tf_op jit(solution)/shard_map/ppermute | solution.py:847
  178.1 14.3 %collective-permute-start.40 = (bf16[192,768]{1,0:T(8,128)(2,1)S(1)}, bf16[192,768]{1,0:T(8,128)(2,1)S(1)}, u32[]{:S(2)}, u32[]{:S(2)}) collective-permute-start(bf16[192,768]{1,0:T(8,128)(2,1)S(1)} %slice.234), channel_id=1, source_target_pairs={{0,4},{4,0},{8,12},{12,8},{16,20},{20,16},{24,28},{28,24},{1,5},{5... | collective-permute-start | bytes 884744 | tf_op jit(solution)/shard_map/ppermute | solution.py:847
  179.1 14.3 %collective-permute-start.39 = (bf16[384,768]{1,0:T(8,128)(2,1)S(1)}, bf16[384,768]{1,0:T(8,128)(2,1)S(1)}, u32[]{:S(2)}, u32[]{:S(2)}) collective-permute-start(bf16[384,768]{1,0:T(8,128)(2,1)S(1)} %add_convert_fusion.15), channel_id=1, source_target_pairs={{0,2},{2,0},{1,3},{3,1},{4,6},{6,4},{5,7},{7,5},{8,10},{10,8},{9,1... | collective-permute-start | bytes 1769480 | tf_op jit(solution)/shard_map/ppermute | solution.py:847
  199.6 16.0 %collective-permute-start.49 = (bf16[192,768]{1,0:T(8,128)(2,1)S(1)}, bf16[192,768]{1,0:T(8,128)(2,1)S(1)}, u32[]{:S(2)}, u32[]{:S(2)}) collective-permute-start(bf16[192,768]{1,0:T(8,128)(2,1)S(1)} %slice.246), channel_id=1, source_target_pairs={{0,4},{4,0},{8,12},{12,8},{16,20},{20,16},{24,28},{28,24},{1,5},{5... | collective-permute-start | bytes 884744 | tf_op jit(solution)/shard_map/ppermute | solution.py:847
  200.5 15.2 %collective-permute-start.50 = (bf16[192,768]{1,0:T(8,128)(2,1)S(1)}, bf16[192,768]{1,0:T(8,128)(2,1)S(1)}, u32[]{:S(2)}, u32[]{:S(2)}) collective-permute-start(bf16[192,768]{1,0:T(8,128)(2,1)S(1)} %add_convert_fusion.35), channel_id=1, source_target_pairs={{0,2},{2,0},{1,3},{3,1},{4,6},{6,4},{5,7},{7,5},{8,10},{10,8},{9,1... | collective-permute-start | bytes 884744 | tf_op jit(solution)/shard_map/ppermute | solution.py:847
  203.6 17.5 %collective-permute-start.52 = (bf16[192,768]{1,0:T(8,128)(2,1)S(1)}, bf16[192,768]{1,0:T(8,128)(2,1)S(1)}, u32[]{:S(2)}, u32[]{:S(2)}) collective-permute-start(bf16[192,768]{1,0:T(8,128)(2,1)S(1)} %slice.248), channel_id=1, source_target_pairs={{0,4},{4,0},{8,12},{12,8},{16,20},{20,16},{24,28},{28,24},{1,5},{5... | collective-permute-start | bytes 884744 | tf_op jit(solution)/shard_map/ppermute | solution.py:847
  205.0 16.6 %collective-permute-start.51 = (bf16[384,768]{1,0:T(8,128)(2,1)S(1)}, bf16[384,768]{1,0:T(8,128)(2,1)S(1)}, u32[]{:S(2)}, u32[]{:S(2)}) collective-permute-start(bf16[384,768]{1,0:T(8,128)(2,1)S(1)} %add_convert_fusion.10), channel_id=1, source_target_pairs={{0,2},{2,0},{1,3},{3,1},{4,6},{6,4},{5,7},{7,5},{8,10},{10,8},{9,1... | collective-permute-start | bytes 1769480 | tf_op jit(solution)/shard_map/ppermute | solution.py:847
  241.2 22.5 %collective-permute-start.64 = (bf16[384,896]{1,0:T(8,128)(2,1)S(1)}, bf16[384,896]{1,0:T(8,128)(2,1)S(1)}, u32[]{:S(2)}, u32[]{:S(2)}) collective-permute-start(bf16[384,896]{1,0:T(8,128)(2,1)S(1)} %slice.260), channel_id=1, source_target_pairs={{0,4},{4,0},{8,12},{12,8},{16,20},{20,16},{24,28},{28,24},{1,5},{5... | collective-permute-start | bytes 2064392 | tf_op jit(solution)/shard_map/ppermute | solution.py:847
  243.1 20.6 %collective-permute-start.65 = (bf16[384,768]{1,0:T(8,128)(2,1)S(1)}, bf16[384,768]{1,0:T(8,128)(2,1)S(1)}, u32[]{:S(2)}, u32[]{:S(2)}) collective-permute-start(bf16[384,768]{1,0:T(8,128)(2,1)S(1)} %slice.261), channel_id=1, source_target_pairs={{0,2},{2,0},{1,3},{3,1},{4,6},{6,4},{5,7},{7,5},{8,10},{10,8},{9,1... | collective-permute-start | bytes 1769480 | tf_op jit(solution)/shard_map/ppermute | solution.py:847
  267.3 17.6 %collective-permute-start.71 = (bf16[4,64,1024]{2,1,0:T(8,128)(2,1)S(1)}, bf16[4,64,1024]{2,1,0:T(8,128)(2,1)S(1)}, u32[]{:S(2)}, u32[]{:S(2)}) collective-permute-start(bf16[4,64,1024]{2,1,0:T(8,128)(2,1)S(1)} %pad_maximum_fusion.1.refs_1_), channel_id=1, source_target_pairs={{0,4},{4,0},{8,12},{12,8},{16,20},{20,16},{24,28},{28,24},{1,5},{5... | collective-permute-start | bytes 1572872 | tf_op jit(solution)/shard_map/ppermute | solution.py:847
  274.6 23.7 %collective-permute-start.72 = (bf16[96,1664]{1,0:T(8,128)(2,1)S(1)}, bf16[96,1664]{1,0:T(8,128)(2,1)S(1)}, u32[]{:S(2)}, u32[]{:S(2)}) collective-permute-start(bf16[96,1664]{1,0:T(8,128)(2,1)S(1)} %pad_maximum_fusion.4), channel_id=1, source_target_pairs={{0,8},{4,12},{8,0},{12,4},{16,24},{20,28},{24,16},{28,20},{1,9},{5... | collective-permute-start | bytes 958472 | tf_op jit(solution)/shard_map/ppermute | solution.py:847
  276.7 14.5 %collective-permute-start.84 = (bf16[2,96,768]{2,1,0:T(8,128)(2,1)S(1)}, bf16[2,96,768]{2,1,0:T(8,128)(2,1)S(1)}, u32[]{:S(2)}, u32[]{:S(2)}) collective-permute-start(bf16[2,96,768]{2,1,0:T(8,128)(2,1)S(1)} %pad_maximum_fusion.8.refs_3_), channel_id=1, source_target_pairs={{0,4},{4,0},{8,12},{12,8},{16,20},{20,16},{24,28},{28,24},{1,5},{5... | collective-permute-start | bytes 884744 | tf_op jit(solution)/shard_map/ppermute | solution.py:847
  277.8 23.6 %collective-permute-start.83 = (bf16[2,96,768]{2,1,0:T(8,128)(2,1)S(1)}, bf16[2,96,768]{2,1,0:T(8,128)(2,1)S(1)}, u32[]{:S(2)}, u32[]{:S(2)}) collective-permute-start(bf16[2,96,768]{2,1,0:T(8,128)(2,1)S(1)} %pad_maximum_fusion.8.refs_3_), channel_id=1, source_target_pairs={{0,8},{4,12},{8,0},{12,4},{16,24},{20,28},{24,16},{28,20},{1,9},{5... | collective-permute-start | bytes 884744 | tf_op jit(solution)/shard_map/ppermute | solution.py:847
  284.3 13.9 %collective-permute-start.73 = (f32[1,6400]{1,0:T(1,128)S(1)}, f32[1,6400]{1,0:T(1,128)S(1)}, u32[]{:S(2)}, u32[]{:S(2)}) collective-permute-start(f32[1,6400]{1,0:T(1,128)S(1)} %add.197), channel_id=1, source_target_pairs={{0,8},{4,12},{8,0},{12,4},{16,24},{20,28},{24,16},{28,20},{1,9},{5... | collective-permute-start | bytes 76808 | tf_op jit(solution)/shard_map/ppermute | solution.py:847
  284.9 16.7 %collective-permute-start.79 = (bf16[4,96,768]{2,1,0:T(8,128)(2,1)S(1)}, bf16[4,96,768]{2,1,0:T(8,128)(2,1)S(1)}, u32[]{:S(2)}, u32[]{:S(2)}) collective-permute-start(bf16[4,96,768]{2,1,0:T(8,128)(2,1)S(1)} %pad_maximum_fusion.refs_1_), channel_id=1, source_target_pairs={{0,4},{4,0},{8,12},{12,8},{16,20},{20,16},{24,28},{28,24},{1,5},{5... | collective-permute-start | bytes 1769480 | tf_op jit(solution)/shard_map/ppermute | solution.py:847
  (91 other events, 633.3 us)
Sparse Core Ops, SparseCore 0:
  13.2 68.0 all-gather.2
  83.4 35.2 all-gather.4
